TPU v7x, 32 devices: a whole 2x2x4 slice. The times are simulated.
32 devices in a mesh: task: 4 (over y, x), batch: 8 (over z, core).
Axes of the slice: x: 2, y: 2, z: 4, core: 2. Of those that a mesh axis runs over, the one named last changes fastest.
Arguments:
- images: bfloat16 [32, 18, 24, 512], P(('task', 'batch')), may hold values from -6 to 6
- image_small: int32 [32], P(('task', 'batch')), may hold values from 0 to 1, as said below
- pool_index: int32 [32, 9, 12], P(('task', 'batch')), may hold values from 0 to 3
- row_slot: int32 [9216], replicated, may hold values from 0 to 9215, each once
- trunk_weight: float32 [9216, 512], P('batch'), may hold values from -0.09375 to 0.09375
- trunk_mean_grad: float32 [9216, 512], P('batch'), may hold values from -5.173322 to 5.173322
- trunk_mean_square: float32 [9216, 512], P('batch'), may hold values from 7.32672 to 116.1216
- trunk_statistic: float32 [2, 512, 512], replicated, as said below
- trunk_basis: float32 [2, 512, 512], replicated, as said below
- head_weight: float32 [4, 5632, 512], P('task', 'batch'), may hold values from -0.15625 to 0.15625
- head_mean_grad: float32 [4, 5632, 512], P('task', 'batch'), may hold values from -5.173322 to 5.173322
- head_mean_square: float32 [4, 5632, 512], P('task', 'batch'), may hold values from 7.32672 to 116.1216
- head_statistic: float32 [4, 3, 512, 512], P('task'), as said below
- head_basis: float32 [4, 3, 512, 512], P('task'), as said below
- trunk_gain: float32 [2, 512], replicated, may hold values from 0.5 to 1.5
- trunk_offset: float32 [2, 512], replicated, may hold values from -1.2 to 1.2
- trunk_norm_mean_grad: float32 [2, 2, 512], replicated, may hold values from -5.173322 to 5.173322
- trunk_norm_mean_square: float32 [2, 2, 512], replicated, may hold values from 7.32672 to 116.1216
- head_gain: float32 [4, 3, 512], P('task'), may hold values from 0.5 to 1.5
- head_offset: float32 [4, 3, 512], P('task'), may hold values from -1.2 to 1.2
- head_norm_mean_grad: float32 [4, 3, 2, 512], P('task'), may hold values from -5.173322 to 5.173322
- head_norm_mean_square: float32 [4, 3, 2, 512], P('task'), may hold values from 7.32672 to 116.1216
- cotangent: bfloat16 [4, 4, 8, 9, 12, 512], P('task', None, 'batch'), may hold values from -6 to 6
Outputs:
- task_features: bfloat16 [4, 4, 8, 9, 12, 512], P('task', None, 'batch')
- input_grad: float32 [32, 18, 24, 512], P(('task', 'batch'))
- trunk_weight_new: float32 [9216, 512], P('batch')
- trunk_mean_grad_new: float32 [9216, 512], P('batch')
- trunk_mean_square_new: float32 [9216, 512], P('batch')
- trunk_statistic_new: float32 [2, 512, 512], replicated
- trunk_basis_new: float32 [2, 512, 512], replicated
- head_weight_new: float32 [4, 5632, 512], P('task', 'batch')
- head_mean_grad_new: float32 [4, 5632, 512], P('task', 'batch')
- head_mean_square_new: float32 [4, 5632, 512], P('task', 'batch')
- head_statistic_new: float32 [4, 3, 512, 512], P('task')
- head_basis_new: float32 [4, 3, 512, 512], P('task')
- trunk_norm_new: float32 [2, 2, 512], replicated
- trunk_norm_mean_grad_new: float32 [2, 2, 512], replicated
- trunk_norm_mean_square_new: float32 [2, 2, 512], replicated
- head_norm_new: float32 [4, 3, 2, 512], P('task')
- head_norm_mean_grad_new: float32 [4, 3, 2, 512], P('task')
- head_norm_mean_square_new: float32 [4, 3, 2, 512], P('task')
Inputs may be any that keep to these rules, and one draw needn't show every extreme that they name: `image_small`: 1 marks a 144x192 image whose valid region is its first 9 rows and 12 columns; 0 marks a 288x384 image, valid everywhere. `pool_index`: which cell of a 2x2 window receives the value: 2 times the row offset plus the column offset. A permutation: row r of the stacked trunk kernels is held at row row_slot[r] of the slot-ordered arrays. `trunk_statistic`: each matrix is symmetric with a dominant positive diagonal. `head_statistic`: each matrix is symmetric with a dominant positive diagonal. `trunk_basis`: each matrix is orthogonal. `head_basis`: each matrix is orthogonal.
All inputs are finite; a program needn't handle non-finite values.
Results may differ from a plain program's by a relative error of at most 0.023.
Values may be sent and summed in bfloat16 or wider, within the bound.
A program may use at most 320 MiB of HBM per device.

v0:
```python
import jax
import jax.numpy as jnp
from jax import lax
from jax.sharding import PartitionSpec as P

STEP = 10


EPS = 1e-05
ADAM_EPS = 1e-08
BETA_ONE = 0.95
BETA_TWO = 0.95
STAT_DECAY = 0.95
LEARN_MATRIX = 0.02
LEARN_NORM = 0.5
DECAY_MATRIX = 0.01
HIGHEST = lax.Precision.HIGHEST


def make_validity(small_flags, height, breadth):
    shrunk = small_flags > 0
    row_limit = jnp.where(shrunk, height // 2, height)
    col_limit = jnp.where(shrunk, breadth // 2, breadth)
    row_index = lax.broadcasted_iota(jnp.int32, (1, height, breadth, 1), 1)
    col_index = lax.broadcasted_iota(jnp.int32, (1, height, breadth, 1), 2)
    inside = (row_index < row_limit[:, None, None, None]) & (
        col_index < col_limit[:, None, None, None]
    )
    return inside.astype(jnp.float32)


def conv_forward(inputs, kernel):
    height, breadth = (inputs.shape[1], inputs.shape[2])
    padded = jnp.pad(inputs, ((0, 0), (1, 1), (1, 1), (0, 0)))
    summed = None
    for position in range(9):
        window = padded[
            :, position // 3 : position // 3 + height, position % 3 : position % 3 + breadth, :
        ]
        addend = jnp.einsum(
            "nhwc,cd->nhwd", window, kernel[position], preferred_element_type=jnp.float32
        )
        summed = addend if summed is None else summed + addend
    return summed


def conv_weight_grad(inputs, upstream_low):
    height, breadth = (inputs.shape[1], inputs.shape[2])
    padded = jnp.pad(inputs, ((0, 0), (1, 1), (1, 1), (0, 0)))
    pieces = []
    for position in range(9):
        window = padded[
            :, position // 3 : position // 3 + height, position % 3 : position % 3 + breadth, :
        ]
        pieces.append(
            jnp.einsum("nhwc,nhwd->cd", window, upstream_low, preferred_element_type=jnp.float32)
        )
    return jnp.stack(pieces)


def conv_backward_input(upstream_low, kernel):
    number, height, breadth = (upstream_low.shape[0], upstream_low.shape[1], upstream_low.shape[2])
    padded = jnp.zeros((number, height + 2, breadth + 2, kernel.shape[1]), jnp.float32)
    for position in range(9):
        addend = jnp.einsum(
            "nhwd,cd->nhwc", upstream_low, kernel[position], preferred_element_type=jnp.float32
        )
        padded = padded.at[
            :, position // 3 : position // 3 + height, position % 3 : position % 3 + breadth, :
        ].add(addend)
    return padded[:, 1 : height + 1, 1 : breadth + 1, :]


def pool_mean(values):
    number, height, breadth, channels = values.shape
    return jnp.mean(values.reshape(number, height // 2, 2, breadth // 2, 2, channels), axis=(2, 4))


def pool_spread(values):
    number, height, breadth, channels = values.shape
    widened = jnp.broadcast_to(
        values[:, :, None, :, None, :], (number, height, 2, breadth, 2, channels)
    )
    return widened.reshape(number, 2 * height, 2 * breadth, channels) * 0.25


def unpool_cells(pooled, places):
    number, height, breadth, channels = pooled.shape
    choose = (places[..., None] == jnp.arange(4, dtype=jnp.int32)).astype(jnp.float32)
    placed = pooled[:, :, :, None, :] * choose[..., None]
    placed = placed.reshape(number, height, breadth, 2, 2, channels).transpose(0, 1, 3, 2, 4, 5)
    return placed.reshape(number, 2 * height, 2 * breadth, channels)


def unpool_gather(values, places):
    number, height, breadth, channels = values.shape
    grouped = values.reshape(number, height // 2, 2, breadth // 2, 2, channels).transpose(
        0, 1, 3, 2, 4, 5
    )
    grouped = grouped.reshape(number, height // 2, breadth // 2, 4, channels)
    choose = (places[..., None] == jnp.arange(4, dtype=jnp.int32)).astype(jnp.float32)
    return jnp.sum(grouped * choose[..., None], axis=3)


def silu_backward(pre_act, upstream):
    sigmoid = jax.nn.sigmoid(pre_act)
    return upstream * sigmoid * (1.0 + pre_act * (1.0 - sigmoid))


def trunk_moments(sum_values, sum_squares, sum_valid):
    return lax.psum((sum_values, sum_squares, sum_valid), ("task", "batch"))


def trunk_grad_moments(offset_sum, gain_sum):
    return lax.psum((offset_sum, gain_sum), ("task", "batch"))


def head_moments(sum_values, sum_squares, sum_valid):
    return lax.psum((sum_values, sum_squares, sum_valid), "batch")


def head_grad_moments(offset_sum, gain_sum):
    return lax.psum((offset_sum, gain_sum), "batch")


def scatter_images(rows_grad):
    return lax.psum_scatter(rows_grad, "batch", scatter_dimension=0, tiled=True)


def norm_forward(values, validity, gain_row, offset_row, totals):
    sum_values, sum_squares, sum_valid = totals(
        jnp.sum(values * validity, axis=(0, 1, 2)),
        jnp.sum(values * values * validity, axis=(0, 1, 2)),
        jnp.sum(validity),
    )
    center = sum_values / sum_valid
    inverse = lax.rsqrt(sum_squares / sum_valid - center * center + EPS)
    normal = (values - center) * inverse
    return (normal, inverse, sum_valid, normal * gain_row + offset_row)


def norm_backward(upstream, normal, inverse, sum_valid, gain_row, validity, totals):
    offset_grad, gain_grad = totals(
        jnp.sum(upstream * validity, axis=(0, 1, 2)),
        jnp.sum(upstream * normal * validity, axis=(0, 1, 2)),
    )
    lowered = (
        gain_row
        * inverse
        * (upstream - offset_grad / sum_valid - normal * gain_grad / sum_valid)
        * validity
    )
    return (lowered, gain_grad, offset_grad)


def adam_step(gradient, moment_one, moment_two):
    new_one = BETA_ONE * moment_one + (1.0 - BETA_ONE) * gradient
    new_two = BETA_TWO * moment_two + (1.0 - BETA_TWO) * gradient * gradient
    direction = (
        new_one / (1.0 - BETA_ONE**STEP) / (jnp.sqrt(new_two / (1.0 - BETA_TWO**STEP)) + ADAM_EPS)
    )
    return (new_one, new_two, direction)


def rotate_rows(rows_grad, owners, basis_set):
    turned = jnp.einsum("rc,mcd->rmd", rows_grad, basis_set, precision=HIGHEST)
    return jnp.einsum("rm,rmd->rd", owners, turned, precision=HIGHEST)


def rotate_back(rows_step, owners, basis_set):
    turned = jnp.einsum("rd,mcd->rmc", rows_step, basis_set, precision=HIGHEST)
    return jnp.einsum("rm,rmc->rc", owners, turned, precision=HIGHEST)


def owner_grams(rows_grad, owners):
    spread_rows = owners[:, :, None] * rows_grad[:, None, :]
    return jnp.einsum("rmc,rd->mcd", spread_rows, rows_grad, precision=HIGHEST)


def renew_basis(statistic, basis_set, grams):
    new_stat = STAT_DECAY * statistic + (1.0 - STAT_DECAY) * grams
    product = jnp.einsum("mcd,mde->mce", new_stat, basis_set, precision=HIGHEST)
    inner_gram = jnp.einsum("mcd,mce->mde", product, product, precision=HIGHEST)
    factor = jnp.linalg.cholesky(inner_gram)
    return (
        new_stat,
        lax.linalg.triangular_solve(factor, product, left_side=False, lower=True, transpose_a=True),
    )


def apply_rows(rows_grad, owners, weight_rows, mean_grad, mean_square, basis_set):
    rotated = rotate_rows(rows_grad, owners, basis_set)
    new_one, new_two, direction = adam_step(rotated, mean_grad, mean_square)
    stepped = rotate_back(direction, owners, basis_set)
    return (weight_rows - LEARN_MATRIX * (stepped + DECAY_MATRIX * weight_rows), new_one, new_two)


def local(
    images,
    image_small,
    pool_index,
    row_slot,
    trunk_weight,
    trunk_mean_grad,
    trunk_mean_square,
    trunk_statistic,
    trunk_basis,
    head_weight,
    head_mean_grad,
    head_mean_square,
    head_statistic,
    head_basis,
    trunk_gain,
    trunk_offset,
    trunk_norm_mean_grad,
    trunk_norm_mean_square,
    head_gain,
    head_offset,
    head_norm_mean_grad,
    head_norm_mean_square,
    cotangent,
):
    bfloat = jnp.bfloat16
    number, height, breadth, channels = images.shape
    tap_rows = 9 * channels
    slot_rows = lax.all_gather(trunk_weight.astype(bfloat), "batch", axis=0, tiled=True)
    natural = jnp.take(slot_rows, row_slot, axis=0)
    encoder = natural[:tap_rows].reshape(9, channels, channels)
    decoder = natural[tap_rows:].reshape(9, channels, channels)
    head_rows = lax.all_gather(head_weight.astype(bfloat), "batch", axis=1, tiled=True)[0]
    attend_first = head_rows[:channels]
    attend_second = head_rows[channels : 2 * channels]
    head_kernel = head_rows[2 * channels :].reshape(9, channels, channels)
    validity = make_validity(image_small, height, breadth)
    masked_in = images * validity.astype(bfloat)
    enc_pre = conv_forward(masked_in, encoder)
    enc_normal, enc_inverse, trunk_valid, enc_scaled = norm_forward(
        enc_pre, validity, trunk_gain[0], trunk_offset[0], trunk_moments
    )
    enc_act = jax.nn.silu(enc_scaled) * validity
    spread = (unpool_cells(pool_mean(enc_act), pool_index) * validity).astype(bfloat)
    dec_pre = conv_forward(spread, decoder)
    dec_normal, dec_inverse, trunk_valid, dec_scaled = norm_forward(
        dec_pre, validity, trunk_gain[1], trunk_offset[1], trunk_moments
    )
    features = (jax.nn.silu(dec_scaled) * validity).astype(bfloat)
    gathered, gathered_small = (
        lax.all_gather(features, "task", axis=0, tiled=True),
        lax.all_gather(image_small.astype(bfloat), "task", axis=0, tiled=True),
    )
    head_valid = make_validity(gathered_small, height, breadth)
    first_pre = jnp.einsum(
        "nhwc,cd->nhwd", gathered, attend_first, preferred_element_type=jnp.float32
    )
    first_normal, first_inverse, head_count, first_scaled = norm_forward(
        first_pre, head_valid, head_gain[0, 0], head_offset[0, 0], head_moments
    )
    hidden = (jax.nn.silu(first_scaled) * head_valid).astype(bfloat)
    second_pre = jnp.einsum(
        "nhwc,cd->nhwd", hidden, attend_second, preferred_element_type=jnp.float32
    )
    second_normal, second_inverse, head_count, second_scaled = norm_forward(
        second_pre, head_valid, head_gain[0, 1], head_offset[0, 1], head_moments
    )
    gate_value = jax.nn.sigmoid(second_scaled)
    gated_low = (gate_value * gathered).astype(bfloat)
    third_pre = conv_forward(gated_low, head_kernel)
    third_normal, third_inverse, head_count, third_scaled = norm_forward(
        third_pre, head_valid, head_gain[0, 2], head_offset[0, 2], head_moments
    )
    head_act = jax.nn.silu(third_scaled) * head_valid
    outputs = pool_mean(head_act)
    task_features = outputs.reshape((1, -1, number) + outputs.shape[1:]).astype(bfloat)
    upstream = pool_spread(cotangent[0].reshape(outputs.shape).astype(jnp.float32)) * head_valid
    third_grad, third_gain_grad, third_offset_grad = norm_backward(
        silu_backward(third_scaled, upstream),
        third_normal,
        third_inverse,
        head_count,
        head_gain[0, 2],
        head_valid,
        head_grad_moments,
    )
    third_low = third_grad.astype(bfloat)
    kernel_grad = conv_weight_grad(gated_low, third_low)
    gated_grad = conv_backward_input(third_low, head_kernel)
    gate_upstream = gated_grad * gathered * gate_value * (1.0 - gate_value)
    feature_grad = gated_grad * gate_value
    second_grad, second_gain_grad, second_offset_grad = norm_backward(
        gate_upstream,
        second_normal,
        second_inverse,
        head_count,
        head_gain[0, 1],
        head_valid,
        head_grad_moments,
    )
    second_low = second_grad.astype(bfloat)
    attend_second_grad = jnp.einsum(
        "nhwc,nhwd->cd", hidden, second_low, preferred_element_type=jnp.float32
    )
    hidden_grad = (
        jnp.einsum("nhwd,cd->nhwc", second_low, attend_second, preferred_element_type=jnp.float32)
        * head_valid
    )
    first_grad, first_gain_grad, first_offset_grad = norm_backward(
        silu_backward(first_scaled, hidden_grad),
        first_normal,
        first_inverse,
        head_count,
        head_gain[0, 0],
        head_valid,
        head_grad_moments,
    )
    first_low = first_grad.astype(bfloat)
    attend_first_grad = jnp.einsum(
        "nhwc,nhwd->cd", gathered, first_low, preferred_element_type=jnp.float32
    )
    feature_grad = feature_grad + jnp.einsum(
        "nhwd,cd->nhwc", first_low, attend_first, preferred_element_type=jnp.float32
    )
    head_grads = jnp.concatenate(
        [attend_first_grad, attend_second_grad, kernel_grad.reshape(tap_rows, channels)], axis=0
    )
    head_owned = lax.psum_scatter(head_grads, "batch", scatter_dimension=0, tiled=True)
    trunk_feature_grad = lax.psum_scatter(
        feature_grad.astype(jnp.bfloat16), "task", scatter_dimension=0, tiled=True
    ).astype(jnp.float32)
    dec_upstream = silu_backward(dec_scaled, trunk_feature_grad * validity)
    dec_grad, dec_gain_grad, dec_offset_grad = norm_backward(
        dec_upstream,
        dec_normal,
        dec_inverse,
        trunk_valid,
        trunk_gain[1],
        validity,
        trunk_grad_moments,
    )
    dec_low = dec_grad.astype(bfloat)
    decoder_grad = conv_weight_grad(spread, dec_low)
    spread_grad = conv_backward_input(dec_low, decoder) * validity
    enc_upstream = silu_backward(
        enc_scaled, pool_spread(unpool_gather(spread_grad, pool_index)) * validity
    )
    enc_grad, enc_gain_grad, enc_offset_grad = norm_backward(
        enc_upstream,
        enc_normal,
        enc_inverse,
        trunk_valid,
        trunk_gain[0],
        validity,
        trunk_grad_moments,
    )
    enc_low = enc_grad.astype(bfloat)
    encoder_grad = conv_weight_grad(masked_in, enc_low)
    input_grad = conv_backward_input(enc_low, encoder) * validity
    trunk_grads = jnp.concatenate(
        [encoder_grad.reshape(tap_rows, channels), decoder_grad.reshape(tap_rows, channels)], axis=0
    )
    inverse_slot = jnp.argsort(row_slot)
    ordered = jnp.take(trunk_grads, inverse_slot, axis=0)
    owned_rows = lax.psum(scatter_images(ordered).astype(jnp.bfloat16), "task").astype(jnp.float32)
    local_rows = trunk_weight.shape[0]
    slot_ids = lax.axis_index("batch") * local_rows + jnp.arange(local_rows, dtype=jnp.int32)
    trunk_owner = jnp.take(inverse_slot, slot_ids) // tap_rows
    trunk_onehot = (trunk_owner[:, None] == jnp.arange(2, dtype=jnp.int32)).astype(jnp.float32)
    trunk_weight_new, trunk_one_new, trunk_two_new = apply_rows(
        owned_rows, trunk_onehot, trunk_weight, trunk_mean_grad, trunk_mean_square, trunk_basis
    )
    head_local = head_weight.shape[1]
    head_ids = lax.axis_index("batch") * head_local + jnp.arange(head_local, dtype=jnp.int32)
    head_owner = jnp.minimum(head_ids // channels, 2)
    head_onehot = (head_owner[:, None] == jnp.arange(3, dtype=jnp.int32)).astype(jnp.float32)
    head_weight_new, head_one_new, head_two_new = apply_rows(
        head_owned,
        head_onehot,
        head_weight[0],
        head_mean_grad[0],
        head_mean_square[0],
        head_basis[0],
    )
    trunk_grams, head_grams = lax.psum(
        (owner_grams(owned_rows, trunk_onehot), owner_grams(head_owned, head_onehot)), "batch"
    )
    trunk_stat_new, trunk_basis_new = renew_basis(trunk_statistic, trunk_basis, trunk_grams)
    head_stat_new, head_basis_new = renew_basis(head_statistic[0], head_basis[0], head_grams)
    trunk_norm = jnp.stack([trunk_gain, trunk_offset], axis=1)
    trunk_norm_grad = jnp.stack(
        [jnp.stack([enc_gain_grad, enc_offset_grad]), jnp.stack([dec_gain_grad, dec_offset_grad])]
    )
    trunk_norm_one, trunk_norm_two, trunk_direction = adam_step(
        trunk_norm_grad, trunk_norm_mean_grad, trunk_norm_mean_square
    )
    head_norm = jnp.stack([head_gain, head_offset], axis=2)
    gain_stack = jnp.stack([first_gain_grad, second_gain_grad, third_gain_grad])
    offset_stack = jnp.stack([first_offset_grad, second_offset_grad, third_offset_grad])
    head_norm_grad = jnp.stack([gain_stack, offset_stack], axis=1)[None]
    head_norm_one, head_norm_two, head_direction = adam_step(
        head_norm_grad, head_norm_mean_grad, head_norm_mean_square
    )
    return (
        task_features,
        input_grad,
        trunk_weight_new,
        trunk_one_new,
        trunk_two_new,
        trunk_stat_new,
        trunk_basis_new,
        head_weight_new[None],
        head_one_new[None],
        head_two_new[None],
        head_stat_new[None],
        head_basis_new[None],
        trunk_norm - LEARN_NORM * trunk_direction,
        trunk_norm_one,
        trunk_norm_two,
        head_norm - LEARN_NORM * head_direction,
        head_norm_one,
        head_norm_two,
    )


def solution(mesh):
    placed = (
        P(("task", "batch"), None, None, None),
        P(("task", "batch")),
        P(("task", "batch"), None, None),
        P(),
        P("batch", None),
        P("batch", None),
        P("batch", None),
        P(),
        P(),
        P("task", "batch", None),
        P("task", "batch", None),
        P("task", "batch", None),
        P("task", None, None, None),
        P("task", None, None, None),
        P(),
        P(),
        P(),
        P(),
        P("task", None, None),
        P("task", None, None),
        P("task", None, None, None),
        P("task", None, None, None),
        P("task", None, "batch", None, None, None),
    )
    return jax.shard_map(
        local,
        mesh=mesh,
        in_specs=placed,
        out_specs=(
            P("task", None, "batch", None, None, None),
            P(("task", "batch"), None, None, None),
            P("batch", None),
            P("batch", None),
            P("batch", None),
            P(),
            P(),
            P("task", "batch", None),
            P("task", "batch", None),
            P("task", "batch", None),
            P("task", None, None, None),
            P("task", None, None, None),
            P(),
            P(),
            P(),
            P("task", None, None, None),
            P("task", None, None, None),
            P("task", None, None, None),
        ),
        check_vma=False,
    )
```

profile of v0, /device:TPU:0, one launch (start us, length us, event | category | flops | bytes accessed | tf_op | source)
XLA Modules:
  0.0 2110.4 jit_solution(902142087563331168)
XLA Ops:
  16.3 87.6 %all-gather.5.cloned.1.call-done = bf16[9216,512]{1,0:T(8,128)(2,1)} async-done(((bf16[1152,512]{1,0:T(8,128)(2,1)}), bf16[9216,512]{1,0:T(8,128)(2,1)}) %all-gather.5.cloned.1.call-update) | async-done | bytes 9437200 | tf_op jit(solution)/shard_map/all_gather | solution.py:226
  103.9 42.8 %gather_fusion = bf16[9216,512]{1,0:T(8,128)(2,1)} fusion(bf16[9216,512]{1,0:T(8,128)(2,1)} %all-gather.5.cloned.1.call-done, s32[9216]{0:T(1024)S(1)} %fusion.354), kind=kCustom, calls=%fused_computation | custom fusion | bytes 18911232 | tf_op jit(solution)/shard_map/jit(_take)/gather | solution.py:227
  146.7 7.4 broadcast_select_fusion.1
  159.1 39.1 %all-reduce.13 = (f32[512]{0:T(512)S(1)}, f32[]{:T(128)}, f32[512]{0:T(512)S(1)}) all-reduce(f32[512]{0:T(512)S(1)} %get-tuple-element.487, f32[]{:T(128)} %fusion.364, f32[512]{0:T(512)S(1)} %get-tuple-element.486), channel_id=1, replica_groups=mesh['task'=4,'batch'=8] {'task','batch'}, use_global_device_ids=true, to_apply=%region_5.6 | all-reduce | flops 1025 | bytes 8200 | tf_op jit(solution)/shard_map/psum | solution.py:111
  231.0 40.7 %all-reduce.12 = (f32[512]{0:T(512)S(1)}, f32[512]{0:T(512)S(1)}) all-reduce(f32[512]{0:T(512)S(1)} %get-tuple-element.485, f32[512]{0:T(512)S(1)} %get-tuple-element.484), channel_id=1, replica_groups=mesh['task'=4,'batch'=8] {'task','batch'}, use_global_device_ids=true, to_apply=%region_10.11 | all-reduce | flops 1024 | bytes 8192 | tf_op jit(solution)/shard_map/psum | solution.py:111
  276.6 11.0 all-reduce.8
  300.9 7.1 all-gather.9.cloned.1.call-done
  312.6 17.1 all-reduce.19
  337.8 14.0 all-reduce.18
  356.2 7.2 pad_slice_fusion
  383.9 8.9 multiply_reduce_fusion.7
  392.7 13.6 all-reduce.17
  407.0 6.4 multiply_reduce_fusion.5
  413.4 13.8 all-reduce.16
  443.0 17.8 scatter-add.91
  460.8 7.9 add_select_fusion
  468.7 17.8 scatter-add.94
  497.8 16.5 scatter-add.96
  520.3 16.5 scatter-add.99
  548.0 16.5 scatter-add.101
  570.5 16.5 scatter-add.104
  587.0 6.6 multiply_reduce_fusion.3
  593.6 13.6 all-reduce.15
  619.7 13.6 all-reduce.14
  664.7 10.1 pad_maximum_fusion.1
  676.0 8.9 sort.17
  691.2 38.8 %all-reduce.11 = (f32[512]{0:T(512)S(1)}, f32[512]{0:T(512)S(1)}) all-reduce(f32[512]{0:T(512)S(1)} %get-tuple-element.481, f32[512]{0:T(512)S(1)} %get-tuple-element.480), channel_id=1, replica_groups=mesh['task'=4,'batch'=8] {'task','batch'}, use_global_device_ids=true, to_apply=%region_43.44 | all-reduce | flops 1024 | bytes 8192 | tf_op jit(solution)/shard_map/psum | solution.py:115
  807.9 42.5 %all-reduce.10 = (f32[512]{0:T(512)S(1)}, f32[512]{0:T(512)S(1)}) all-reduce(f32[512]{0:T(512)S(1)} %get-tuple-element.483, f32[512]{0:T(512)S(1)} %get-tuple-element.482), channel_id=1, replica_groups=mesh['task'=4,'batch'=8] {'task','batch'}, use_global_device_ids=true, to_apply=%region_48.49 | all-reduce | flops 1024 | bytes 8192 | tf_op jit(solution)/shard_map/psum | solution.py:115
  864.4 11.3 pad_maximum_fusion
  875.6 45.5 %gather_fusion.2 = f32[9216,512]{1,0:T(8,128)} fusion(f32[9216,512]{1,0:T(8,128)} %pad_maximum_fusion, s32[9216]{0:T(1024)S(1)} %fusion.355), kind=kCustom, calls=%fused_computation.2 | custom fusion | bytes 37785600 | tf_op jit(solution)/shard_map/jit(_take)/gather | solution.py:361
  921.2 16.3 broadcast_select_fusion
  938.0 6.5 gather_fusion.1
  1032.4 8.9 fusion.22
  1041.3 8.6 fusion.2
  1051.1 10.6 fusion.20
  1061.7 63.1 %reduce-scatter.6.cloned.1.call-done = f32[1152,512]{1,0:T(8,128)} async-done(((f32[9216,512]{1,0:T(8,128)}), f32[1152,512]{1,0:T(8,128)}) %reduce-scatter.6.cloned.1.call-update) | async-done | bytes 2359312 | tf_op jit(solution)/shard_map/reduce_scatter | solution.py:127
  1128.1 10.6 fusion
  1140.2 10.0 fusion.10
  1152.3 28.9 %all-reduce.24.cloned.1.call-done = bf16[1152,512]{1,0:T(8,128)(2,1)} async-done(((bf16[1152,512]{1,0:T(8,128)(2,1)}), bf16[1152,512]{1,0:T(8,128)(2,1)}) %all-reduce.24.cloned.1.call-update) | async-done | bytes 1179664 | tf_op jit(solution)/shard_map/psum | solution.py:362
  1187.4 13.1 fusion.8
  1203.6 7.5 fusion.4
  1217.5 9.5 fusion.33
  1227.0 12.2 fusion.6
  1241.3 86.7 %all-reduce.26.cloned.1.call-done = (f32[2,512,512]{2,1,0:T(8,128)}, f32[3,512,512]{2,1,0:T(8,128)}) async-done(((f32[2,512,512]{2,1,0:T(8,128)}, f32[3,512,512]{2,1,0:T(8,128)}), (f32[2,512,512]{2,1,0:T(8,128)}, f32[3,512,512]{2,1,0:T(8,128)})) %all-reduce.26.cloned.1.call-update) | async-done | bytes 5242896 | tf_op jit(solution)/shard_map/psum | solution.py:382
  1333.5 7.2 fusion.18
  1359.8 23.5 %custom-call.68 = f32[2,128,128]{2,1,0:T(8,128)S(1)} custom-call(f32[2,128,128]{2,1,0:T(8,128)S(1)} %cholesky.542), custom_call_target="Cholesky" | custom-call | tf_op jit(solution)/shard_map/jit(cholesky)/cholesky | solution.py:184
  1385.6 9.2 fusion.439
  1404.3 36.1 %custom-call.76 = f32[3,128,128]{2,1,0:T(8,128)S(1)} custom-call(f32[3,128,128]{2,1,0:T(8,128)} %cholesky.555), custom_call_target="Cholesky" | custom-call | tf_op jit(solution)/shard_map/jit(cholesky)/cholesky | solution.py:184
  1443.2 21.1 custom-call.69
  1469.6 24.9 %custom-call.70 = f32[2,128,128]{2,1,0:T(8,128)} custom-call(f32[2,128,128]{2,1,0:T(8,128)} %cholesky.546), custom_call_target="Cholesky" | custom-call | tf_op jit(solution)/shard_map/jit(cholesky)/cholesky | solution.py:184
  1496.1 21.5 %custom-call.71 = f32[2,1,128,128]{2,3,1,0:T(8,128)} custom-call(f32[2,1,128,128]{3,2,1,0:T(8,128)} %get-tuple-element.580), custom_call_target="InvertDiagBlocksLowerTriangular" | custom-call | tf_op jit(solution)/shard_map/jit(cholesky)/cholesky | solution.py:184
  1522.9 24.9 %custom-call.72 = f32[2,128,128]{2,1,0:T(8,128)} custom-call(f32[2,128,128]{2,1,0:T(8,128)} %cholesky.551), custom_call_target="Cholesky" | custom-call | tf_op jit(solution)/shard_map/jit(cholesky)/cholesky | solution.py:184
  1549.4 21.1 custom-call.73
  1574.8 24.9 %custom-call.74 = f32[2,128,128]{2,1,0:T(8,128)} custom-call(f32[2,128,128]{2,1,0:T(8,128)} %convolution_subtract_fusion.8), custom_call_target="Cholesky" | custom-call | tf_op jit(solution)/shard_map/jit(cholesky)/cholesky | solution.py:184
  1605.2 14.1 while.29
  1619.3 80.2 %custom-call.75 = f32[2,4,128,128]{2,3,1,0:T(8,128)} custom-call(f32[2,4,128,128]{3,2,1,0:T(8,128)} %bitcast.928), custom_call_target="InvertDiagBlocksLowerTriangular" | custom-call | tf_op jit(solution)/shard_map/triangular_solve | solution.py:187
  1717.3 30.9 %custom-call.77 = f32[3,1,128,128]{2,3,1,0:T(8,128)} custom-call(f32[3,1,128,128]{3,2,1,0:T(8,128)} %select_bitcast_fusion.2), custom_call_target="InvertDiagBlocksLowerTriangular" | custom-call | tf_op jit(solution)/shard_map/jit(cholesky)/cholesky | solution.py:184
  1754.1 36.8 %custom-call.78 = f32[3,128,128]{2,1,0:T(8,128)} custom-call(f32[3,128,128]{2,1,0:T(8,128)} %cholesky.559), custom_call_target="Cholesky" | custom-call | tf_op jit(solution)/shard_map/jit(cholesky)/cholesky | solution.py:184
  1792.6 30.9 %custom-call.79 = f32[3,1,128,128]{2,3,1,0:T(8,128)} custom-call(f32[3,1,128,128]{3,2,1,0:T(8,128)} %get-tuple-element.575), custom_call_target="InvertDiagBlocksLowerTriangular" | custom-call | tf_op jit(solution)/shard_map/jit(cholesky)/cholesky | solution.py:184
  1829.6 36.6 %custom-call.80 = f32[3,128,128]{2,1,0:T(8,128)} custom-call(f32[3,128,128]{2,1,0:T(8,128)} %cholesky.564), custom_call_target="Cholesky" | custom-call | tf_op jit(solution)/shard_map/jit(cholesky)/cholesky | solution.py:184
  1867.9 31.3 %custom-call.81 = f32[3,1,128,128]{2,3,1,0:T(8,128)} custom-call(f32[3,1,128,128]{3,2,1,0:T(8,128)} %get-tuple-element.573), custom_call_target="InvertDiagBlocksLowerTriangular" | custom-call | tf_op jit(solution)/shard_map/jit(cholesky)/cholesky | solution.py:184
  1904.1 36.6 %custom-call.82 = f32[3,128,128]{2,1,0:T(8,128)} custom-call(f32[3,128,128]{2,1,0:T(8,128)} %convolution_subtract_fusion.7), custom_call_target="Cholesky" | custom-call | tf_op jit(solution)/shard_map/jit(cholesky)/cholesky | solution.py:184
  1947.2 14.9 while.30
  1962.0 119.5 %custom-call.83 = f32[3,4,128,128]{2,3,1,0:T(8,128)} custom-call(f32[3,4,128,128]{3,2,1,0:T(8,128)} %bitcast.927), custom_call_target="InvertDiagBlocksLowerTriangular" | custom-call | tf_op jit(solution)/shard_map/triangular_solve | solution.py:187
  (558 shorter events, 566.6 us)
Async XLA Ops:
  7.2 1025.2 %copy-start = (f32[1,3,512,512]{3,2,1,0:T(8,128)S(1)}, f32[1,3,512,512]{3,2,1,0:T(8,128)}, u32[]{:S(2)}) copy-start(f32[1,3,512,512]{3,2,1,0:T(8,128)} %param.90) | copy-start | bytes 9437188
  7.2 6.8 copy-start.70
  7.2 6.9 copy-start.111
  7.2 6.9 copy-start.88
  7.2 6.9 copy-start.90
  7.3 96.6 %all-gather.5.cloned.1.call-start = ((), (), s32[]{:S(2)}) async-start(), calls=%async_computation.3 | async-start | bytes 10616832 | tf_op jit(solution)/shard_map/all_gather | solution.py:226
  10.3 290.6 %all-gather.7.cloned.1.call-start = ((), (), s32[]{:S(2)}) async-start(), calls=%async_computation.4 | async-start | bytes 6488064 | tf_op jit(solution)/shard_map/all_gather | solution.py:230
  12.7 295.3 %all-gather.9.cloned.1.call-start = ((), (), s32[]{:S(2)}) async-start(), calls=%async_computation.8 | async-start | bytes 2211840 | tf_op jit(solution)/shard_map/all_gather | solution.py:248
  13.4 259.5 %copy-start.61 = (f32[18,24]{1,0:T(8,128)}, f32[18,24]{1,0:T(8,128)S(1)}, u32[]{:S(2)}) copy-start(f32[18,24]{1,0:T(8,128)S(1)} %fusion.361) | copy-start | bytes 5188
  14.1 185.3 %copy-start.86 = (f32[1,512]{1,0:T(1,128)}, f32[1,512]{1,0:T(1,128)S(1)}, u32[]{:S(2)}) copy-start(f32[1,512]{1,0:T(1,128)S(1)} %get-tuple-element.595) | copy-start | bytes 6148
  14.1 258.8 %copy-start.77 = (f32[1,512]{1,0:T(1,128)}, f32[1,512]{1,0:T(1,128)S(1)}, u32[]{:S(2)}) copy-start(f32[1,512]{1,0:T(1,128)S(1)} %get-tuple-element.594) | copy-start | bytes 6148
  14.2 185.3 %copy-start.78 = (f32[1,512]{1,0:T(1,128)}, f32[1,512]{1,0:T(1,128)S(1)}, u32[]{:S(2)}) copy-start(f32[1,512]{1,0:T(1,128)S(1)} %get-tuple-element.593) | copy-start | bytes 6148
  14.2 258.8 %copy-start.73 = (f32[1,512]{1,0:T(1,128)}, f32[1,512]{1,0:T(1,128)S(1)}, u32[]{:S(2)}) copy-start(f32[1,512]{1,0:T(1,128)S(1)} %get-tuple-element.592) | copy-start | bytes 6148
  14.3 193.7 %copy-start.44 = (f32[9,12,2,2]{3,1,2,0:T(8,128)}, f32[9,12,2,2]{3,1,2,0:T(8,128)S(1)}, u32[]{:S(2)}) copy-start(f32[9,12,2,2]{3,1,2,0:T(8,128)S(1)} %compare_convert_fusion) | copy-start | bytes 5188
  146.7 7.5 copy-start.13
  199.4 10.5 copy-start.80
  199.4 10.5 copy-start.82
  216.6 12.0 copy-start.18
  227.1 48.2 %copy-start.114 = (u32[32]{0:T(128)S(1)}, u32[32]{0:T(128)}, u32[]{:S(2)}) copy-start(u32[32]{0:T(128)} %constant.1177) | copy-start | bytes 388
  272.9 19.7 copy-start.75
  272.9 19.7 copy-start.76
  275.2 414.1 %reduce-scatter.10.cloned.1.call-start = ((), (), s32[]{:S(2)}) async-start(), calls=%async_computation.9 | async-start | bytes 2211840
  292.6 8.1 copy-start.84
  292.6 8.1 copy-start.85
  356.2 27.6 %copy-start.5 = (bf16[4,18,24,512]{3,2,1,0:T(8,128)(2,1)}, bf16[4,18,24,512]{3,2,1,0:T(8,128)(2,1)S(1)}, u32[]{:S(2)}) copy-start(bf16[4,18,24,512]{3,2,1,0:T(8,128)(2,1)S(1)} %fusion.12) | copy-start | bytes 5308420
  634.0 6.8 slice-start
  645.7 386.7 %reduce-scatter.8.cloned.1.call-start = ((), (), s32[]{:S(2)}) async-start(), calls=%async_computation.7 | async-start | bytes 12976128 | tf_op jit(solution)/shard_map/reduce_scatter | solution.py:325
  674.8 10.3 copy-start.40
  674.8 14.5 copy-start.62
  674.8 14.5 copy-start.74
  674.9 449.9 %reduce-scatter.6.cloned.1.call-start = ((), (), s32[]{:S(2)}) async-start(), calls=%async_computation.5 | async-start | bytes 21233664 | tf_op jit(solution)/shard_map/reduce_scatter | solution.py:127
  730.0 9.8 copy-start.97
  730.0 9.8 copy-start.104
  789.0 9.9 copy-start.45
  796.3 8.6 copy-start.79
  796.3 8.6 copy-start.81
  796.3 8.6 copy-start.83
  796.3 8.6 copy-start.87
  800.9 50.1 %copy-start.108 = (f32[512]{0:T(512)S(1)}, f32[512]{0:T(512)}, u32[]{:S(2)}) copy-start(f32[512]{0:T(512)} %get-tuple-element.542) | copy-start | bytes 6148
  853.4 10.5 copy-start.11
  937.5 243.8 %all-reduce.24.cloned.1.call-start = ((), (), s32[]{:S(2)}) async-start(), calls=%async_computation.6 | async-start | bytes 2359296 | tf_op jit(solution)/shard_map/psum | solution.py:362
  955.4 8.4 copy-start.100
  955.4 8.4 copy-start.102
  955.4 9.1 copy-start.94
  1014.4 13.0 copy-start.98
  1014.4 13.0 copy-start.105
  1014.4 13.0 copy-start.107
  1014.4 13.0 copy-start.110
  1014.4 13.0 copy-start.89
  1041.3 9.8 copy-start.33
  1041.3 9.8 copy-start.35
  1127.6 200.4 %all-reduce.26.cloned.1.call-start = ((), (), s32[]{:S(2)}) async-start(), calls=%async_computation.10 | async-start | bytes 10485760 | tf_op jit(solution)/shard_map/psum | solution.py:382
  1128.1 10.6 copy-start.32
  1140.2 10.1 copy-start.22
  1140.2 10.1 copy-start.34
  1140.2 10.1 copy-start.36
  1217.5 9.5 copy-start.67
  1227.0 12.3 copy-start.25
  1333.5 7.2 copy-start.47
  1333.5 7.2 copy-start.48
  1440.4 26.2 %copy-start.49 = (f32[3,128,128]{2,1,0:T(8,128)}, f32[3,128,128]{2,1,0:T(8,128)S(1)}, u32[]{:S(2)}) copy-start(f32[3,128,128]{2,1,0:T(8,128)S(1)} %custom-call.76) | copy-start | bytes 589828
  1466.6 135.2 %copy-start.46 = (pred[512,512]{1,0:T(8,128)(4,1)S(1)}, pred[512,512]{1,0:T(8,128)(4,1)}, u32[]{:S(2)}) copy-start(pred[512,512]{1,0:T(8,128)(4,1)} %iota_compare_fusion) | copy-start | bytes 786436
  1699.5 8.4 copy-start.68
  1754.1 186.6 %copy-start.72 = (pred[128,128]{1,0:T(8,128)(4,1)S(1)}, pred[128,128]{1,0:T(8,128)(4,1)}, u32[]{:S(2)}) copy-start(pred[128,128]{1,0:T(8,128)(4,1)} %iota_compare_fusion.2) | copy-start | bytes 49156
  (63 other events, 201.7 us)
Sparse Core Ops, SparseCore 0:
  10.4 93.4 all-gather.4
  106.1 58.8 all-gather.6
  275.3 32.5 all-gather.8
  645.9 29.7 reduce-scatter.9
  677.8 120.3 reduce-scatter.7
  937.6 187.0 reduce-scatter.5
  1128.4 52.8 all-reduce.23
  1211.3 116.6 all-reduce.25
where the time goes:
time: 2130 us; the launch traced here: 2110 us
  other arithmetic  798 us (37%)
  local copies, waits for them, and re-layouts  386 us (18%)
  matrix products  377 us (18%)
  waiting for transfers between devices  274 us (13%)
  blocking collectives  258 us (12%)
    another operation x30, other arithmetic, renew_basis(): factor = jnp.linalg.cholesky(inner_gram)  414 us
    another operation x7, other arithmetic, renew_basis(): lax.linalg.triangular_solve(factor, product, left_side=False, lower=True,...  210 us
    scatter-add x21, local copies, waits for them, and re-layouts, conv_backward_input(): padded = padded.at[:, position // 3:position // 3 + height, position % 3:...  171 us
    dot_general x27, matrix products, conv_backward_input(): jnp.einsum('nhwd,cd->nhwc', upstream_low, kernel[position], preferred_ele...  105 us
    all_gather x1, waiting for transfers between devices, local(): lax.all_gather(trunk_weight.astype(bfloat), 'batch', axis=0, tiled=True)  87.6 us
    psum x1, waiting for transfers between devices, local(): lax.psum((owner_grams(owned_rows, trunk_onehot), owner_grams(head_owned,...  86.7 us
    psum x2, blocking collectives, trunk_grad_moments(): return lax.psum((offset_sum, gain_sum), ('task', 'batch'))  81.4 us
    psum x2, blocking collectives, trunk_moments(): return lax.psum((sum_values, sum_squares, sum_valid), ('task', 'batch'))  79.8 us
  transfers between devices with their start and end apart: 8, of which 5 were waited for; matrix products, arithmetic and copies ran while one was open for 23% of the time, Pallas kernels for 0%

commit v1 on v0

v1 whole, which is shorter than its diff:
```python
import functools

import jax
import jax.numpy as jnp
from jax import lax
from jax.experimental import pallas as pl
from jax.experimental.pallas import tpu as pltpu
from jax.sharding import PartitionSpec as P

STEP = 10


EPS = 1e-05
ADAM_EPS = 1e-08
BETA_ONE = 0.95
BETA_TWO = 0.95
STAT_DECAY = 0.95
LEARN_MATRIX = 0.02
LEARN_NORM = 0.5
DECAY_MATRIX = 0.01
BF = jnp.bfloat16
F32 = jnp.float32
MESH = pl.DeviceIdType.MESH
MIB = 1 << 20

VMEM_SPEC = pl.BlockSpec(memory_space=pltpu.VMEM)
SMEM_SPEC = pl.BlockSpec(memory_space=pltpu.SMEM)


def run(body, outs, specs, args, scratch=(), vmem=40, flops=0):
    size = sum(o.size * o.dtype.itemsize for o in outs) + sum(a.size * a.dtype.itemsize for a in args)
    return pl.pallas_call(
        body,
        out_shape=tuple(outs),
        in_specs=[SMEM_SPEC if s == "s" else VMEM_SPEC for s in specs],
        out_specs=tuple(VMEM_SPEC for _ in outs),
        scratch_shapes=list(scratch),
        compiler_params=pltpu.CompilerParams(vmem_limit_bytes=vmem * MIB),
        cost_estimate=pl.CostEstimate(flops=flops, bytes_accessed=size, transcendentals=0),
    )(*args)


def shape(dims, kind):
    return jax.ShapeDtypeStruct(tuple(dims), kind)


def dot(a, b):
    return jnp.dot(a, b, preferred_element_type=F32)


def dot_nt(a, b):
    return lax.dot_general(a, b, (((1,), (1,)), ((), ())), preferred_element_type=F32)


def dot_tn(a, b):
    return lax.dot_general(a, b, (((0,), (0,)), ((), ())), preferred_element_type=F32)


def split(a):
    high = a.astype(BF)
    return high, (a - high.astype(F32)).astype(BF)


def dot3(kind, a, b):
    a_high, a_low = split(a)
    b_high, b_low = split(b)
    return kind(a_high, b_high) + (kind(a_high, b_low) + kind(a_low, b_high))


def places(height, breadth):
    index = lax.broadcasted_iota(jnp.int32, (height * breadth, 1), 0)
    row = lax.div(index, breadth)
    return row, index - row * breadth


def valid_rows(small, height, breadth):
    row, col = places(height, breadth)
    row_limit = jnp.where(small > 0, height // 2, height)
    col_limit = jnp.where(small > 0, breadth // 2, breadth)
    return jnp.where((row < row_limit) & (col < col_limit), 1.0, 0.0).astype(F32)


def move(values, rows):
    gap = jnp.zeros((abs(rows),) + values.shape[1:], values.dtype)
    if rows > 0:
        return jnp.concatenate([gap, values[:-rows]], axis=0)
    return jnp.concatenate([values[-rows:], gap], axis=0)


def from_left(values, col):
    return jnp.where(col > 0, pltpu.roll(values, 1, 0), 0.0)


def from_right(values, col, breadth):
    return jnp.where(col < breadth - 1, pltpu.roll(values, values.shape[0] - 1, 0), 0.0)


def gather_taps(tap, breadth, col):
    lines = [move(tap(b), breadth) + tap(3 + b) + move(tap(6 + b), -breadth) for b in range(3)]
    return lines[1] + from_left(lines[0], col) + from_right(lines[2], col, breadth)


def spread_taps(values, breadth, col):
    lines = [from_right(values, col, breadth), values, from_left(values, col)]
    return [
        move(lines[b], breadth * (a - 1)) if a != 1 else lines[b] for a in range(3) for b in range(3)
    ]


def window_sum(values, row, col, breadth):
    count = values.shape[0]
    pair = values + jnp.where(
        col % 2 == 0, pltpu.roll(values, count - 1, 0), pltpu.roll(values, 1, 0)
    )
    return pair + jnp.where(row % 2 == 0, move(pair, -breadth), move(pair, breadth))


def norm_of(values, totals, scale):
    count = totals[2:3]
    center = totals[0:1] / count
    inverse = lax.rsqrt(totals[1:2] / count - center * center + EPS)
    normal = (values - center) * inverse
    return normal, inverse, normal * scale[0:1] + scale[1:2]


def silu_back(scaled):
    sig = jax.nn.sigmoid(scaled)
    return sig * (1.0 + scaled * (1.0 - sig))


def norm_back(upstream, normal, inverse, totals, sums, scale, valid):
    count = totals[2:3]
    return (
        scale[0:1] * inverse * (upstream - sums[0:1] / count - normal * sums[1:2] / count) * valid
    )


def col_sum(values):
    return jnp.sum(values, axis=0, keepdims=True)


def put_sums(ref, rows):
    width = ref.shape[1]
    rows = list(rows) + [jnp.zeros((1, width), F32)] * (8 - len(rows))
    ref[...] = jnp.concatenate(rows, axis=0)


def each_image(geometry, body, start):
    number, height, breadth = geometry
    pixels = height * breadth

    def step(image, carry):
        return body(image, pl.ds(pl.multiple_of(image * pixels, 16), pixels), carry)

    return lax.fori_loop(0, number, step, start)


def zero_rows(count, width):
    return (jnp.zeros((1, width), F32),) * count


def trunk_conv_body(geometry, small, x, taps, pre, stats, work):
    number, height, breadth = geometry
    width = pre.shape[1]
    _, col = places(height, breadth)

    def image(i, rows, carry):
        valid = valid_rows(small[i], height, breadth)
        work[...] = dot(x[rows, :], taps[...])
        out = gather_taps(lambda p: work[:, p * width : (p + 1) * width], breadth, col)
        pre[rows, :] = out
        kept = out * valid
        return (
            carry[0] + col_sum(kept),
            carry[1] + col_sum(kept * out),
            carry[2] + jnp.broadcast_to(col_sum(valid), (1, width)),
        )

    put_sums(stats, each_image(geometry, image, zero_rows(3, width)))


def trunk_conv(geometry, small, x, taps):
    pixels = geometry[1] * geometry[2]
    width = taps.shape[1] // 9
    return run(
        functools.partial(trunk_conv_body, geometry),
        [shape((x.shape[0], width), F32), shape((8, width), F32)],
        "svv",
        (small, x, taps),
        [pltpu.VMEM((pixels, 9 * width), F32)],
        flops=2 * x.size * taps.shape[1],
    )


def enc_act_body(geometry, small, pre, totals, scale, choose, spread):
    number, height, breadth = geometry
    row, col = places(height, breadth)

    def image(i, rows, carry):
        valid = valid_rows(small[i], height, breadth)
        _, _, scaled = norm_of(pre[rows, :], totals[...], scale[...])
        act = scaled * jax.nn.sigmoid(scaled) * valid
        pooled = window_sum(act, row, col, breadth) * 0.25
        spread[rows, :] = (pooled * choose[rows, :]).astype(BF)
        return carry

    each_image(geometry, image, 0)


def enc_act(geometry, small, pre, totals, scale, choose):
    return run(
        functools.partial(enc_act_body, geometry),
        [shape(pre.shape, BF)],
        "svvvv",
        (small, pre, totals, scale, choose),
    )[0]


def dec_act_body(geometry, small, pre, totals, scale, features):
    number, height, breadth = geometry

    def image(i, rows, carry):
        valid = valid_rows(small[i], height, breadth)
        _, _, scaled = norm_of(pre[rows, :], totals[...], scale[...])
        features[rows, :] = (scaled * jax.nn.sigmoid(scaled) * valid).astype(BF)
        return carry

    each_image(geometry, image, 0)


def dec_act(geometry, small, pre, totals, scale):
    return run(
        functools.partial(dec_act_body, geometry),
        [shape(pre.shape, BF)],
        "svvv",
        (small, pre, totals, scale),
    )[0]


def trunk_upstream(rows, geometry, valid, upstream, choose, pool):
    if not pool:
        return upstream * valid
    row, col = places(geometry[1], geometry[2])
    return window_sum(upstream * choose, row, col, geometry[2]) * 0.25 * valid


def trunk_sums_body(geometry, pool, small, upstream, pre, totals, scale, choose, sums):
    number, height, breadth = geometry
    width = pre.shape[1]

    def image(i, rows, carry):
        valid = valid_rows(small[i], height, breadth)
        normal, _, scaled = norm_of(pre[rows, :], totals[...], scale[...])
        dy = silu_back(scaled) * trunk_upstream(
            rows, geometry, valid, upstream[rows, :], choose[rows, :], pool
        )
        return carry[0] + col_sum(dy), carry[1] + col_sum(dy * normal)

    put_sums(sums, each_image(geometry, image, zero_rows(2, width)))


def trunk_sums(geometry, pool, small, upstream, pre, totals, scale, choose):
    return run(
        functools.partial(trunk_sums_body, geometry, pool),
        [shape((8, pre.shape[1]), F32)],
        "svvvvv",
        (small, upstream, pre, totals, scale, choose),
    )[0]


def trunk_back_body(
    geometry, pool, small, upstream, pre, totals, sums, scale, choose, x, taps, grad, lower, nine
):
    number, height, breadth = geometry
    width = pre.shape[1]
    _, col = places(height, breadth)

    def image(i, rows, carry):
        valid = valid_rows(small[i], height, breadth)
        normal, inverse, scaled = norm_of(pre[rows, :], totals[...], scale[...])
        dy = silu_back(scaled) * trunk_upstream(
            rows, geometry, valid, upstream[rows, :], choose[rows, :], pool
        )
        dz = norm_back(dy, normal, inverse, totals[...], sums[...], scale[...], valid)
        for p, moved in enumerate(spread_taps(dz, breadth, col)):
            nine[rows, p * width : (p + 1) * width] = moved.astype(BF)
        lower[rows, :] = (dot_nt(nine[rows, :], taps[...]) * valid).astype(BF)
        return carry

    each_image(geometry, image, 0)
    grad[...] = dot_tn(x[...], nine[...])


def trunk_back(geometry, pool, small, upstream, pre, totals, sums, scale, choose, x, taps):
    return run(
        functools.partial(trunk_back_body, geometry, pool),
        [shape(taps.shape, F32), shape(x.shape, BF)],
        "svvvvvvvv",
        (small, upstream, pre, totals, sums, scale, choose, x, taps),
        [pltpu.VMEM((x.shape[0], taps.shape[1]), BF)],
        flops=4 * x.size * taps.shape[1],
    )


def put_stats(pre, out, rows, valid, carry):
    pre[rows, :] = out
    kept = out * valid
    width = out.shape[1]
    return (
        carry[0] + col_sum(kept),
        carry[1] + col_sum(kept * out),
        carry[2] + jnp.broadcast_to(col_sum(valid), (1, width)),
    )


def head_first_body(geometry, small, features, weight, pre, stats):
    number, height, breadth = geometry

    def image(i, rows, carry):
        valid = valid_rows(small[i], height, breadth)
        return put_stats(pre, dot(features[rows, :], weight[...]), rows, valid, carry)

    put_sums(stats, each_image(geometry, image, zero_rows(3, pre.shape[1])))


def head_first(geometry, small, features, weight):
    return run(
        functools.partial(head_first_body, geometry),
        [shape(features.shape, F32), shape((8, weight.shape[1]), F32)],
        "svv",
        (small, features, weight),
        flops=2 * features.size * weight.shape[1],
    )


def head_second_body(geometry, small, pre_one, totals, scale, weight, hidden, pre, stats):
    number, height, breadth = geometry

    def image(i, rows, carry):
        valid = valid_rows(small[i], height, breadth)
        _, _, scaled = norm_of(pre_one[rows, :], totals[...], scale[...])
        low = (scaled * jax.nn.sigmoid(scaled) * valid).astype(BF)
        hidden[rows, :] = low
        return put_stats(pre, dot(low, weight[...]), rows, valid, carry)

    put_sums(stats, each_image(geometry, image, zero_rows(3, pre.shape[1])))


def head_second(geometry, small, pre_one, totals, scale, weight):
    return run(
        functools.partial(head_second_body, geometry),
        [shape(pre_one.shape, BF), shape(pre_one.shape, F32), shape((8, weight.shape[1]), F32)],
        "svvvv",
        (small, pre_one, totals, scale, weight),
        flops=2 * pre_one.size * weight.shape[1],
    )


def head_third_body(
    geometry, small, pre_two, totals, scale, features, kernel, gated, pre, stats, work
):
    number, height, breadth = geometry
    width = pre.shape[1]
    half = work.shape[2]
    channels = features.shape[1]
    _, col = places(height, breadth)

    def image(i, rows, carry):
        valid = valid_rows(small[i], height, breadth)
        _, _, scaled = norm_of(pre_two[rows, :], totals[...], scale[...])
        low = (jax.nn.sigmoid(scaled) * features[rows, :].astype(F32)).astype(BF)
        gated[rows, :] = low
        parts = []
        for j in range(width // half):
            cut = slice(j * half, (j + 1) * half)
            for p in range(9):
                work[p] = dot(low, kernel[p * channels : (p + 1) * channels, cut])
            parts.append(gather_taps(lambda p: work[p], breadth, col))
        return put_stats(pre, jnp.concatenate(parts, axis=1), rows, valid, carry)

    put_sums(stats, each_image(geometry, image, zero_rows(3, width)))


def head_third(geometry, small, pre_two, totals, scale, features, kernel):
    pixels = geometry[1] * geometry[2]
    return run(
        functools.partial(head_third_body, geometry),
        [shape(pre_two.shape, BF), shape(pre_two.shape, F32), shape((8, kernel.shape[1]), F32)],
        "svvvvv",
        (small, pre_two, totals, scale, features, kernel),
        [pltpu.VMEM((9, pixels, 256), F32)],
        flops=2 * pre_two.size * kernel.shape[0],
    )


def pool_choice(height, breadth, flipped):
    pixels, windows = height * breadth, height * breadth // 4
    dims = (windows, pixels) if flipped else (pixels, windows)
    pixel = lax.broadcasted_iota(jnp.int32, dims, 1 if flipped else 0)
    window = lax.broadcasted_iota(jnp.int32, dims, 0 if flipped else 1)
    row = lax.div(pixel, breadth)
    col = pixel - row * breadth
    home = lax.div(row, 2) * (breadth // 2) + lax.div(col, 2)
    return jnp.where(home == window, 1.0, 0.0).astype(BF)


def head_out_body(geometry, small, pre, totals, scale, cotangent, pooled, sums):
    number, height, breadth = geometry
    widen = pool_choice(height, breadth, False)
    narrow = pool_choice(height, breadth, True)

    def image(i, rows, carry):
        valid = valid_rows(small[i], height, breadth)
        normal, _, scaled = norm_of(pre[rows, :], totals[...], scale[...])
        high, low = split(scaled * jax.nn.sigmoid(scaled) * valid)
        pooled[i] = ((dot(narrow, high) + dot(narrow, low)) * 0.25).astype(BF)
        dy = silu_back(scaled) * dot(widen, cotangent[i]) * 0.25 * valid
        return carry[0] + col_sum(dy), carry[1] + col_sum(dy * normal)

    put_sums(sums, each_image(geometry, image, zero_rows(2, pre.shape[1])))


def head_out(geometry, small, pre, totals, scale, cotangent):
    return run(
        functools.partial(head_out_body, geometry),
        [shape(cotangent.shape, BF), shape((8, pre.shape[1]), F32)],
        "svvvv",
        (small, pre, totals, scale, cotangent),
    )


def head_third_grad_body(
    geometry, small, pre, totals, sums, scale, cotangent, gated, kernel, grad, lower, nine
):
    number, height, breadth = geometry
    width = pre.shape[1]
    channels = gated.shape[1]
    _, col = places(height, breadth)
    widen = pool_choice(height, breadth, False)

    def image(i, rows, carry):
        valid = valid_rows(small[i], height, breadth)
        normal, inverse, scaled = norm_of(pre[rows, :], totals[...], scale[...])
        dy = silu_back(scaled) * dot(widen, cotangent[i]) * 0.25 * valid
        dz = norm_back(dy, normal, inverse, totals[...], sums[...], scale[...], valid)
        for p, moved in enumerate(spread_taps(dz, breadth, col)):
            nine[p, rows, :] = moved.astype(BF)
        total = None
        for p in range(9):
            part = dot_nt(nine[p, rows, :], kernel[p * channels : (p + 1) * channels, :])
            total = part if total is None else total + part
        lower[rows, :] = total
        return carry

    each_image(geometry, image, 0)

    def tap(p, carry):
        rows = pl.ds(pl.multiple_of(p * channels, channels), channels)
        grad[rows, :] = dot_tn(gated[...], nine[p]).astype(grad.dtype)
        return carry

    lax.fori_loop(0, 9, tap, 0)


def head_third_grad(geometry, small, pre, totals, sums, scale, cotangent, gated, kernel):
    return run(
        functools.partial(head_third_grad_body, geometry),
        [shape(kernel.shape, BF), shape(gated.shape, F32)],
        "svvvvvvv",
        (small, pre, totals, sums, scale, cotangent, gated, kernel),
        [pltpu.VMEM((9,) + pre.shape, BF)],
        vmem=56,
        flops=4 * pre.size * kernel.shape[0],
    )


def head_gate_body(geometry, small, lower, pre, totals, scale, features, sums):
    number, height, breadth = geometry

    def image(i, rows, carry):
        valid = valid_rows(small[i], height, breadth)
        normal, _, scaled = norm_of(pre[rows, :], totals[...], scale[...])
        gate = jax.nn.sigmoid(scaled)
        dy = lower[rows, :] * features[rows, :].astype(F32) * gate * (1.0 - gate) * valid
        return carry[0] + col_sum(dy), carry[1] + col_sum(dy * normal)

    put_sums(sums, each_image(geometry, image, zero_rows(2, pre.shape[1])))


def head_gate(geometry, small, lower, pre, totals, scale, features):
    return run(
        functools.partial(head_gate_body, geometry),
        [shape((8, pre.shape[1]), F32)],
        "svvvvv",
        (small, lower, pre, totals, scale, features),
    )[0]


def head_second_grad_body(
    geometry, small, lower, pre, totals, sums, scale, features, weight, hidden,
    pre_one, totals_one, scale_one, grad, upstream, sums_one, low,
):
    number, height, breadth = geometry

    def image(i, rows, carry):
        valid = valid_rows(small[i], height, breadth)
        normal, inverse, scaled = norm_of(pre[rows, :], totals[...], scale[...])
        gate = jax.nn.sigmoid(scaled)
        dy = lower[rows, :] * features[rows, :].astype(F32) * gate * (1.0 - gate) * valid
        dz = norm_back(dy, normal, inverse, totals[...], sums[...], scale[...], valid).astype(BF)
        low[rows, :] = dz
        normal, _, scaled = norm_of(pre_one[rows, :], totals_one[...], scale_one[...])
        dy = silu_back(scaled) * dot_nt(dz, weight[...]) * valid
        upstream[rows, :] = dy
        return carry[0] + col_sum(dy), carry[1] + col_sum(dy * normal)

    put_sums(sums_one, each_image(geometry, image, zero_rows(2, pre.shape[1])))
    grad[...] = dot_tn(hidden[...], low[...]).astype(grad.dtype)


def head_second_grad(
    geometry, small, lower, pre, totals, sums, scale, features, weight, hidden,
    pre_one, totals_one, scale_one,
):
    return run(
        functools.partial(head_second_grad_body, geometry),
        [shape(weight.shape, BF), shape(pre.shape, F32), shape((8, pre.shape[1]), F32)],
        "svvvvvvvvvvv",
        (small, lower, pre, totals, sums, scale, features, weight, hidden, pre_one, totals_one, scale_one),
        [pltpu.VMEM(pre.shape, BF)],
        flops=4 * pre.size * weight.shape[0],
    )


def head_first_grad_body(
    geometry, small, upstream, pre, totals, sums, scale, features, weight,
    lower, pre_two, totals_two, scale_two, grad, out, low,
):
    number, height, breadth = geometry

    def image(i, rows, carry):
        valid = valid_rows(small[i], height, breadth)
        normal, inverse, _ = norm_of(pre[rows, :], totals[...], scale[...])
        dz = norm_back(
            upstream[rows, :], normal, inverse, totals[...], sums[...], scale[...], valid
        ).astype(BF)
        low[rows, :] = dz
        _, _, scaled = norm_of(pre_two[rows, :], totals_two[...], scale_two[...])
        total = lower[rows, :] * jax.nn.sigmoid(scaled) + dot_nt(dz, weight[...])
        out[rows, :] = (total * valid).astype(BF)
        return carry

    each_image(geometry, image, 0)
    grad[...] = dot_tn(features[...], low[...]).astype(grad.dtype)


def head_first_grad(
    geometry, small, upstream, pre, totals, sums, scale, features, weight,
    lower, pre_two, totals_two, scale_two,
):
    return run(
        functools.partial(head_first_grad_body, geometry),
        [shape(weight.shape, BF), shape(pre.shape, BF)],
        "svvvvvvvvvvv",
        (small, upstream, pre, totals, sums, scale, features, weight, lower, pre_two, totals_two, scale_two),
        [pltpu.VMEM(pre.shape, BF)],
        flops=4 * pre.size * weight.shape[0],
    )


def to_taps_body(index, slots, enc, dec, wide, tap):
    count = slots.shape[0]
    channels = enc.shape[0]
    width = slots.shape[1]
    step = 1024

    def widen(i, carry):
        rows = pl.ds(pl.multiple_of(i * step, step), step)
        wide[rows, :] = slots[rows, :].astype(F32)
        return carry

    lax.fori_loop(0, count // step, widen, 0)
    group = 32
    for p in range(18):

        def fetch(i, carry):
            base = i * group
            for u in range(group):
                tap[pl.ds(base + u, 1), :] = wide[pl.ds(index[p * channels + base + u], 1), :]
            return carry

        lax.fori_loop(0, channels // group, fetch, 0)
        out = enc if p < 9 else dec
        q = p % 9
        out[:, q * width : (q + 1) * width] = tap[...].astype(BF)


def to_taps(index, slots, channels):
    width = slots.shape[1]
    return run(
        to_taps_body,
        [shape((channels, 9 * width), BF)] * 2,
        "sv",
        (index, slots),
        [pltpu.VMEM(slots.shape, F32), pltpu.VMEM((channels, width), F32)],
    )


def to_slots_body(index, enc, dec, slots, wide):
    count = slots.shape[0]
    channels = enc.shape[0]
    width = slots.shape[1]
    step = 1024
    group = 32
    for p in range(18):
        source = enc if p < 9 else dec
        q = p % 9

        def place(i, carry):
            base = pl.multiple_of(i * group, group)
            values = source[pl.ds(base, group), q * width : (q + 1) * width]
            for u in range(group):
                wide[pl.ds(index[p * channels + base + u], 1), :] = values[u : u + 1, :]
            return carry

        lax.fori_loop(0, channels // group, place, 0)

    def narrow(i, carry):
        rows = pl.ds(pl.multiple_of(i * step, step), step)
        slots[rows, :] = wide[rows, :].astype(BF)
        return carry

    lax.fori_loop(0, count // step, narrow, 0)


def to_slots(index, enc, dec):
    width = enc.shape[1] // 9
    dims = (index.shape[0], width)
    return run(
        to_slots_body, [shape(dims, BF)], "svv", (index, enc, dec), [pltpu.VMEM(dims, F32)]
    )[0]


def adam(gradient, moment_one, moment_two):
    new_one = BETA_ONE * moment_one + (1.0 - BETA_ONE) * gradient
    new_two = BETA_TWO * moment_two + (1.0 - BETA_TWO) * gradient * gradient
    direction = (
        new_one / (1.0 - BETA_ONE**STEP) / (jnp.sqrt(new_two / (1.0 - BETA_TWO**STEP)) + ADAM_EPS)
    )
    return new_one, new_two, direction


def soap_body(
    cuts, grad, owners, weight, one, two, basis, weight_new, one_new, two_new, low
):
    count = basis.shape[0]
    total = grad.shape[0]
    for m in range(count):
        low[m] = basis[m].astype(BF)

    def chunk(i, carry):
        rows = pl.ds(pl.multiple_of(i * (total // cuts), 8), total // cuts)
        values = grad[rows, :].astype(F32)
        rotated = None
        for m in range(count):
            part = dot((values * owners[rows, m : m + 1]).astype(BF), low[m])
            rotated = part if rotated is None else rotated + part
        new_one, new_two, direction = adam(rotated, one[rows, :], two[rows, :])
        one_new[rows, :] = new_one
        two_new[rows, :] = new_two
        stepped = None
        for m in range(count):
            part = dot_nt((direction * owners[rows, m : m + 1]).astype(BF), low[m])
            stepped = part if stepped is None else stepped + part
        old = weight[rows, :]
        weight_new[rows, :] = old - LEARN_MATRIX * (stepped + DECAY_MATRIX * old)
        return carry

    lax.fori_loop(0, cuts, chunk, 0)


def soap(grad, owners, weight, one, two, basis):
    total = grad.shape[0]
    cuts = 4 if total % 64 == 0 else 1
    return run(
        functools.partial(soap_body, cuts),
        [shape(weight.shape, F32)] * 3,
        "vvvvvv",
        (grad, owners, weight, one, two, basis),
        [pltpu.VMEM(basis.shape, BF)],
        flops=4 * weight.size * weight.shape[1] * basis.shape[0],
    )


def grams_body(grad, part, owners, grams):
    for m in range(grams.shape[0]):
        held = (grad[...].astype(F32) * owners[:, m : m + 1]).astype(BF)
        grams[m] = dot_tn(held, part[...])


def owner_grams(grad, part, owners):
    dims = (owners.shape[1], grad.shape[1], part.shape[1])
    return run(
        grams_body,
        [shape(dims, F32)],
        "vvv",
        (grad, part, owners),
        flops=2 * grad.size * part.shape[1] * owners.shape[1],
    )[0]


def factor_rows(values, identity, turn):
    width = values.shape[1]
    sub = lax.broadcasted_iota(jnp.int32, (8, width), 0)
    rolled = pltpu.roll(values, turn, 1)
    columns = [jnp.broadcast_to(rolled[:, j : j + 1], (8, width)) for j in range(8)]
    scale = jnp.zeros((8, width), F32)
    for j in range(8):
        root = lax.rsqrt(columns[j][j : j + 1, :])
        scale = jnp.where(sub == j, root, scale)
        lower = jnp.where(sub > j, columns[j] * root, 0.0)
        values = values - lower * (values[j : j + 1, :] * root)
        identity = identity - lower * (identity[j : j + 1, :] * root)
        for i in range(j + 1, 8):
            columns[i] = columns[i] - lower * (columns[i][j : j + 1, :] * root)
    return values * scale, identity * scale


def renew_body(stat, basis, gram, stat_new, basis_new, product, *work):
    count, size = stat.shape[0], stat.shape[1]
    panel = 128
    matrices = range(count)
    tables, inverses = work[:count], work[count:]
    row = lax.broadcasted_iota(jnp.int32, (panel, panel), 0)
    col = lax.broadcasted_iota(jnp.int32, (panel, panel), 1)
    unit = jnp.where(row == col, 1.0, 0.0).astype(F32)
    for m in matrices:
        stat_new[m] = STAT_DECAY * stat[m] + (1.0 - STAT_DECAY) * gram[m]
        product[m] = dot3(dot, stat_new[m], basis[m])
    for k in range(size // panel):
        here = slice(k * panel, (k + 1) * panel)
        for m in matrices:
            tables[m][:, :panel] = dot3(dot_tn, product[m, :, here], product[m, :, here])
            tables[m][:, panel:] = unit

        def group(q, carry):
            rows = pl.ds(pl.multiple_of(q * 8, 8), 8)
            turn = lax.rem(panel - q * 8, panel)
            done = [
                factor_rows(tables[m][rows, :panel], tables[m][rows, panel:], turn)
                for m in matrices
            ]
            for m in matrices:
                upper, inverse = done[m]
                inverses[m][rows, :] = inverse
                both = jnp.concatenate([upper, inverse], axis=1)
                tables[m][...] = tables[m][...] - dot3(dot_tn, upper, both)
            return carry

        lax.fori_loop(0, panel // 8, group, 0)
        for m in matrices:
            basis_new[m, :, here] = dot3(dot_nt, product[m, :, here], inverses[m][...])
            if k < size // panel - 1:
                rest = slice((k + 1) * panel, size)
                turned = basis_new[m, :, here]
                product[m, :, rest] = product[m, :, rest] - dot3(
                    dot, turned, dot3(dot_tn, turned, product[m, :, rest])
                )


def renew_basis(stat, basis, gram):
    count = stat.shape[0]
    return run(
        renew_body,
        [shape(stat.shape, F32)] * 2,
        "vvv",
        (stat, basis, gram),
        [pltpu.VMEM(stat.shape, F32)]
        + [pltpu.VMEM((128, 256), F32)] * count
        + [pltpu.VMEM((128, 128), F32)] * count,
        flops=12 * stat.size * stat.shape[1],
    )


def greet(axis, size):
    me = lax.axis_index(axis)
    barrier = pltpu.get_barrier_semaphore()
    for step in range(1, size):
        pl.semaphore_signal(
            barrier, inc=1, device_id={axis: lax.rem(me + step, size)}, device_id_type=MESH
        )
    pl.semaphore_wait(barrier, size - 1)
    return me


def remote(source, target, sends, receives, peer, axis):
    return pltpu.make_async_remote_copy(
        src_ref=source,
        dst_ref=target,
        send_sem=sends,
        recv_sem=receives,
        device_id={axis: peer},
        device_id_type=MESH,
    )


def exchange(body, outs, args, scratch, identity, vmem=32):
    size = sum(o.size * o.dtype.itemsize for o in outs) + sum(a.size * a.dtype.itemsize for a in args)
    return pl.pallas_call(
        body,
        out_shape=tuple(outs),
        in_specs=[VMEM_SPEC] * len(args),
        out_specs=tuple(VMEM_SPEC for _ in outs),
        scratch_shapes=list(scratch),
        compiler_params=pltpu.CompilerParams(
            vmem_limit_bytes=vmem * MIB, collective_id=identity, has_side_effects=True
        ),
        cost_estimate=pl.CostEstimate(flops=0, bytes_accessed=size, transcendentals=0),
    )(*args)


def total_body(axis, size, x, out, slots, sends, receives):
    me = greet(axis, size)
    copies = []
    for step in range(1, size):
        peer = lax.rem(me + step, size)
        copy = remote(x, slots.at[me], sends.at[step], receives.at[me], peer, axis)
        copy.start()
        copies.append(copy)
    slots[me] = x[...]
    for step in range(1, size):
        peer = lax.rem(me + size - step, size)
        remote(x, slots.at[peer], sends.at[step], receives.at[peer], peer, axis).wait_recv()
    total = slots[0]
    for peer in range(1, size):
        total = total + slots[peer]
    out[...] = total
    for copy in copies:
        copy.wait_send()


def total_over(axis, size, x, identity):
    return exchange(
        functools.partial(total_body, axis, size),
        [shape(x.shape, F32)],
        (x,),
        [
            pltpu.VMEM((size,) + x.shape, F32),
            pltpu.SemaphoreType.DMA((size,)),
            pltpu.SemaphoreType.DMA((size,)),
        ],
        identity,
    )[0]


def block_of(ref, place, size, dim):
    length = ref.shape[dim] // size
    start = place * length
    if dim == 0:
        return ref.at[pl.ds(pl.multiple_of(start, 8), length), :]
    return ref.at[:, pl.ds(pl.multiple_of(start, 128), length)]


def gather_body(axis, size, dims, *refs):
    count = len(dims)
    sources, targets = refs[:count], refs[count : 2 * count]
    sends, receives, own = refs[2 * count :]
    me = greet(axis, size)
    copies = []
    for k in range(count):
        mine = block_of(targets[k], me, size, dims[k])
        for step in range(1, size):
            peer = lax.rem(me + step, size)
            copy = remote(sources[k], mine, sends.at[k, step], receives.at[k, me], peer, axis)
            copy.start()
            copies.append(copy)
    locals_ = []
    for k in range(count):
        mine = block_of(targets[k], me, size, dims[k])
        copy = pltpu.make_async_copy(sources[k], mine, own.at[k])
        copy.start()
        locals_.append(copy)
    for copy in locals_:
        copy.wait()
    for k in range(count):
        for step in range(1, size):
            peer = lax.rem(me + size - step, size)
            theirs = block_of(targets[k], peer, size, dims[k])
            remote(
                sources[k], theirs, sends.at[k, step], receives.at[k, peer], peer, axis
            ).wait_recv()
    for copy in copies:
        copy.wait_send()


def gather_over(axis, size, arrays, dims, identity):
    outs = []
    for x, dim in zip(arrays, dims):
        full = list(x.shape)
        full[dim] *= size
        outs.append(shape(full, x.dtype))
    count = len(arrays)
    return exchange(
        functools.partial(gather_body, axis, size, tuple(dims)),
        outs,
        arrays,
        [
            pltpu.SemaphoreType.DMA((count, size)),
            pltpu.SemaphoreType.DMA((count, size)),
            pltpu.SemaphoreType.DMA((count,)),
        ],
        identity,
    )


def scatter_body(axis, size, dim, x, out, slots, sends, receives):
    me = greet(axis, size)
    copies = []
    for step in range(1, size):
        peer = lax.rem(me + step, size)
        copy = remote(
            block_of(x, peer, size, dim), slots.at[me], sends.at[step], receives.at[me], peer, axis
        )
        copy.start()
        copies.append(copy)
    out[...] = block_of(x, me, size, dim)[...].astype(F32)
    for step in range(1, size):
        peer = lax.rem(me + size - step, size)
        remote(
            block_of(x, peer, size, dim), slots.at[peer], sends.at[step], receives.at[peer], peer, axis
        ).wait_recv()
        out[...] = out[...] + slots[peer].astype(F32)
    for copy in copies:
        copy.wait_send()


def scatter_over(axis, size, x, dim, identity):
    part = list(x.shape)
    part[dim] //= size
    return exchange(
        functools.partial(scatter_body, axis, size, dim),
        [shape(part, F32)],
        (x,),
        [
            pltpu.VMEM((size,) + tuple(part), x.dtype),
            pltpu.SemaphoreType.DMA((size,)),
            pltpu.SemaphoreType.DMA((size,)),
        ],
        identity,
    )[0]


def local(
    tasks,
    batches,
    images,
    image_small,
    pool_index,
    row_slot,
    trunk_weight,
    trunk_mean_grad,
    trunk_mean_square,
    trunk_statistic,
    trunk_basis,
    head_weight,
    head_mean_grad,
    head_mean_square,
    head_statistic,
    head_basis,
    trunk_gain,
    trunk_offset,
    trunk_norm_mean_grad,
    trunk_norm_mean_square,
    head_gain,
    head_offset,
    head_norm_mean_grad,
    head_norm_mean_square,
    cotangent,
):
    number, height, breadth, channels = images.shape
    pixels = height * breadth
    tap_rows = 9 * channels
    shown = tasks * number
    geometry = (shown, height, breadth)
    task = lax.axis_index("task")
    batch = lax.axis_index("batch")
    width = channels // tasks

    def quarter(values):
        return lax.dynamic_slice_in_dim(values, task * width, width, values.ndim - 1)

    slots = lax.all_gather(quarter(trunk_weight).astype(BF), "batch", axis=0, tiled=True)
    head_rows = lax.all_gather(head_weight.astype(BF), "batch", axis=1, tiled=True)[0]
    kinds = jnp.concatenate([image_small, pool_index.reshape(-1)])
    kinds = lax.all_gather(kinds, "task", axis=0, tiled=True).reshape(tasks, -1)
    small = kinds[:, :number].reshape(-1)
    cells = kinds[:, number:].reshape(shown, height // 2, 1, breadth // 2, 1)
    cell = 2 * jnp.arange(2, dtype=jnp.int32)[:, None, None] + jnp.arange(2, dtype=jnp.int32)
    choose = (cells == cell).reshape(shown, height, breadth)
    row_limit = jnp.where(small > 0, height // 2, height)[:, None, None]
    col_limit = jnp.where(small > 0, breadth // 2, breadth)[:, None, None]
    inside = (jnp.arange(height, dtype=jnp.int32)[None, :, None] < row_limit) & (
        jnp.arange(breadth, dtype=jnp.int32)[None, None, :] < col_limit
    )
    choose = (choose & inside).astype(F32).reshape(shown * pixels, 1)
    inverse_slot = jnp.argsort(row_slot)
    own_valid = (
        (jnp.arange(height, dtype=jnp.int32)[None, :, None] < jnp.where(image_small > 0, height // 2, height)[:, None, None])
        & (jnp.arange(breadth, dtype=jnp.int32)[None, None, :] < jnp.where(image_small > 0, breadth // 2, breadth)[:, None, None])
    )[..., None]
    masked = (images * own_valid.astype(BF)).reshape(number * pixels, channels)
    x = gather_over("task", tasks, (masked,), (0,), 1)[0]
    enc_taps, dec_taps = to_taps(row_slot, slots, channels)

    scales = quarter(jnp.stack([trunk_gain, trunk_offset], axis=1))
    enc_pre, stats = trunk_conv(geometry, small, x, enc_taps)
    enc_totals = total_over("batch", batches, stats, 2)
    spread = enc_act(geometry, small, enc_pre, enc_totals, scales[0], choose)
    spread = gather_over("task", tasks, (spread,), (1,), 3)[0]
    dec_pre, stats = trunk_conv(geometry, small, spread, dec_taps)
    dec_totals = total_over("batch", batches, stats, 2)
    features = dec_act(geometry, small, dec_pre, dec_totals, scales[1])
    features = gather_over("task", tasks, (features,), (1,), 3)[0]

    first = head_rows[:channels]
    second = head_rows[channels : 2 * channels]
    kernel = head_rows[2 * channels :]
    head_scales = jnp.stack([head_gain[0], head_offset[0]], axis=1)
    cot = cotangent.reshape(shown, pixels // 4, channels)
    pre_one, stats = head_first(geometry, small, features, first)
    totals_one = total_over("batch", batches, stats, 4)
    hidden, pre_two, stats = head_second(
        geometry, small, pre_one, totals_one, head_scales[0], second
    )
    totals_two = total_over("batch", batches, stats, 4)
    gated, pre_three, stats = head_third(
        geometry, small, pre_two, totals_two, head_scales[1], features, kernel
    )
    totals_three = total_over("batch", batches, stats, 4)
    pooled, sums = head_out(geometry, small, pre_three, totals_three, head_scales[2], cot)
    task_features = pooled.reshape(cotangent.shape)

    sums_three = total_over("batch", batches, sums, 4)
    kernel_grad, lower = head_third_grad(
        geometry, small, pre_three, totals_three, sums_three, head_scales[2], cot, gated, kernel
    )
    sums = head_gate(geometry, small, lower, pre_two, totals_two, head_scales[1], features)
    sums_two = total_over("batch", batches, sums, 4)
    second_grad, upstream, sums = head_second_grad(
        geometry, small, lower, pre_two, totals_two, sums_two, head_scales[1], features, second,
        hidden, pre_one, totals_one, head_scales[0],
    )
    sums_one = total_over("batch", batches, sums, 4)
    first_grad, feature_grad = head_first_grad(
        geometry, small, upstream, pre_one, totals_one, sums_one, head_scales[0], features, first,
        lower, pre_two, totals_two, head_scales[1],
    )
    head_grads = jnp.concatenate([first_grad, second_grad, kernel_grad], axis=0)
    head_owned = lax.psum_scatter(head_grads, "batch", scatter_dimension=0, tiled=True)

    upstream = scatter_over("task", tasks, feature_grad, 1, 5)
    sums = trunk_sums(geometry, False, small, upstream, dec_pre, dec_totals, scales[1], choose)
    dec_sums = total_over("batch", batches, sums, 2)
    dec_grad, lower = trunk_back(
        geometry, False, small, upstream, dec_pre, dec_totals, dec_sums, scales[1], choose, spread,
        dec_taps,
    )
    upstream = scatter_over("task", tasks, lower, 1, 5)
    sums = trunk_sums(geometry, True, small, upstream, enc_pre, enc_totals, scales[0], choose)
    enc_sums = total_over("batch", batches, sums, 2)
    enc_grad, lower = trunk_back(
        geometry, True, small, upstream, enc_pre, enc_totals, enc_sums, scales[0], choose, x,
        enc_taps,
    )
    trunk_part = lax.psum_scatter(
        to_slots(row_slot, enc_grad, dec_grad), "batch", scatter_dimension=0, tiled=True
    )
    input_grad = scatter_over("task", tasks, lower, 0, 6).reshape(images.shape)

    head_local = head_weight.shape[1]
    head_ids = batch * head_local + jnp.arange(head_local, dtype=jnp.int32)
    head_owner = jnp.minimum(head_ids // channels, 2)
    head_onehot = (head_owner[:, None] == jnp.arange(3, dtype=jnp.int32)).astype(F32)
    head_grams = lax.psum(owner_grams(head_owned, head_owned, head_onehot).astype(BF), "batch")
    head_weight_new, head_one_new, head_two_new = soap(
        head_owned, head_onehot, head_weight[0], head_mean_grad[0], head_mean_square[0],
        head_basis[0],
    )
    head_stat_new, head_basis_new = renew_basis(head_statistic[0], head_basis[0], head_grams.astype(F32))

    norm_part = jnp.concatenate([enc_sums[:2], dec_sums[:2], jnp.zeros((4, width), F32)], axis=0)
    trunk_owned, norm_sums = gather_over("task", tasks, (trunk_part, norm_part), (1, 1), 7)
    local_rows = trunk_weight.shape[0]
    slot_ids = batch * local_rows + jnp.arange(local_rows, dtype=jnp.int32)
    trunk_owner = jnp.take(inverse_slot, slot_ids) // tap_rows
    trunk_onehot = (trunk_owner[:, None] == jnp.arange(2, dtype=jnp.int32)).astype(F32)
    trunk_grams = lax.psum(owner_grams(trunk_owned, trunk_part, trunk_onehot), "batch").astype(BF)
    trunk_grams = gather_over(
        "task", tasks, (trunk_grams.reshape(2 * channels, width),), (1,), 8
    )[0].reshape(2, channels, channels)
    trunk_weight_new, trunk_one_new, trunk_two_new = soap(
        trunk_owned, trunk_onehot, trunk_weight, trunk_mean_grad, trunk_mean_square, trunk_basis
    )
    trunk_stat_new, trunk_basis_new = renew_basis(trunk_statistic, trunk_basis, trunk_grams.astype(F32))

    trunk_norm = jnp.stack([trunk_gain, trunk_offset], axis=1)
    trunk_norm_grad = norm_sums[:4].reshape(2, 2, channels)[:, ::-1]
    trunk_norm_one, trunk_norm_two, trunk_direction = adam(
        trunk_norm_grad, trunk_norm_mean_grad, trunk_norm_mean_square
    )
    head_norm = jnp.stack([head_gain, head_offset], axis=2)
    head_norm_grad = jnp.stack([sums_one[:2], sums_two[:2], sums_three[:2]])[None, :, ::-1]
    head_norm_one, head_norm_two, head_direction = adam(
        head_norm_grad, head_norm_mean_grad, head_norm_mean_square
    )
    return (
        task_features,
        input_grad,
        trunk_weight_new,
        trunk_one_new,
        trunk_two_new,
        trunk_stat_new,
        trunk_basis_new,
        head_weight_new[None],
        head_one_new[None],
        head_two_new[None],
        head_stat_new[None],
        head_basis_new[None],
        trunk_norm - LEARN_NORM * trunk_direction,
        trunk_norm_one,
        trunk_norm_two,
        head_norm - LEARN_NORM * head_direction,
        head_norm_one,
        head_norm_two,
    )


def solution(mesh):
    placed = (
        P(("task", "batch"), None, None, None),
        P(("task", "batch")),
        P(("task", "batch"), None, None),
        P(),
        P("batch", None),
        P("batch", None),
        P("batch", None),
        P(),
        P(),
        P("task", "batch", None),
        P("task", "batch", None),
        P("task", "batch", None),
        P("task", None, None, None),
        P("task", None, None, None),
        P(),
        P(),
        P(),
        P(),
        P("task", None, None),
        P("task", None, None),
        P("task", None, None, None),
        P("task", None, None, None),
        P("task", None, "batch", None, None, None),
    )
    return jax.shard_map(
        functools.partial(local, mesh.shape["task"], mesh.shape["batch"]),
        mesh=mesh,
        in_specs=placed,
        out_specs=(
            P("task", None, "batch", None, None, None),
            P(("task", "batch"), None, None, None),
            P("batch", None),
            P("batch", None),
            P("batch", None),
            P(),
            P(),
            P("task", "batch", None),
            P("task", "batch", None),
            P("task", "batch", None),
            P("task", None, None, None),
            P("task", None, None, None),
            P(),
            P(),
            P(),
            P("task", None, None, None),
            P("task", None, None, None),
            P("task", None, None, None),
        ),
        check_vma=False,
    )
```

time: 2130 us -> 612 us (0.29)
  other arithmetic: 798 us -> 26 us
  Pallas kernels: 0 us -> 463 us
  matrix products: 377 us -> 0 us
  local copies, waits for them, and re-layouts: 386 us -> 43.6 us
  waiting for transfers between devices: 274 us -> 0.13 us
  blocking collectives: 258 us -> 53.5 us
    another operation x43 -> x2, other arithmetic: 626 us -> 0.09 us  [the longest x1 0.08 us: local(): scales = quarter(jnp.stack([trunk_gain, trunk_offset], axis=1))]
    pallas_call x0 -> x42, Pallas kernels: none -> 463 us  [the longest x24 235 us: run(): pl.pallas_call(body, out_shape=tuple(outs), in_specs=[SMEM_SPEC if s == '...]
    dot_general x101 -> x0, matrix products: 321 us -> none  [the longest x27 105 us: conv_backward_input(): jnp.einsum('nhwd,cd->nhwc', upstream_low, kernel[position], preferred_ele...]
    psum x10 -> x1, blocking collectives: 247 us -> 44.6 us  [local(): lax.psum(owner_grams(trunk_owned, trunk_part, trunk_onehot), 'batch')]
    scatter-add x21 -> x0, local copies, waits for them, and re-layouts: 171 us -> none  [conv_backward_input(): padded = padded.at[:, position // 3:position // 3 + height, position % 3:...]
    psum x2 -> x1, waiting for transfers between devices: 116 us -> 0.01 us  [local(): lax.psum(owner_grams(head_owned, head_owned, head_onehot).astype(BF), 'ba...]
    all_gather x3 -> x2, waiting for transfers between devices: 94.7 us -> 0.04 us  [the longest x1 0.02 us: local(): lax.all_gather(head_weight.astype(BF), 'batch', axis=1, tiled=True)[0]]
    gather x2 -> x0, local copies, waits for them, and re-layouts: 88.3 us -> none  [the longest x1 45.5 us: local(): ordered = jnp.take(trunk_grads, inverse_slot, axis=0)]
  transfers between devices with their start and end apart: 8 -> 5, of which waited for: 5 -> 0; matrix products, arithmetic and copies ran while one was open for 23% -> 6% of each run, Pallas kernels for 0% -> 35%
where the time goes in v1:
time: 612 us; the launch traced here: 603 us
  Pallas kernels  463 us (76%)
  blocking collectives  53.5 us (9%)
  local copies, waits for them, and re-layouts  43.6 us (7%)
  other arithmetic  26 us (4%)
  between operations  16.6 us (3%)
    pallas_call x24, Pallas kernels, run(): pl.pallas_call(body, out_shape=tuple(outs), in_specs=[SMEM_SPEC if s == '...  235 us
    pallas_call x18, Pallas kernels, exchange(): pl.pallas_call(body, out_shape=tuple(outs), in_specs=[VMEM_SPEC] * len(ar...  228 us
    psum x1, blocking collectives, local(): lax.psum(owner_grams(trunk_owned, trunk_part, trunk_onehot), 'batch')  44.6 us
    unnamed x149, local copies, waits for them, and re-layouts  24.1 us
  transfers between devices with their start and end apart: 5, of which 0 were waited for; matrix products, arithmetic and copies ran while one was open for 6% of the time, Pallas kernels for 35%

profile of v1, /device:TPU:0, one launch (start us, length us, event | category | flops | bytes accessed | tf_op | source)
XLA Modules:
  0.0 602.9 jit_solution(9275808298466931163)
XLA Ops:
  7.3 1.9 dynamic-slice_convert_fusion
  9.2 2.3 convert_element_type.47
  13.8 8.8 %all-reduce = s32[436]{0:T(512)S(1)} all-reduce(s32[436]{0:T(512)S(1)} %add_dynamic-update-slice_fusion), channel_id=1, replica_groups=mesh['task'=4,'batch'=8] {'task'}, use_global_device_ids=true, to_apply=%add | all-reduce | flops 436 | bytes 3488
  23.0 20.4 %shard_map.358.x = bf16[1728,512]{1,0:T(8,128)(2,1)S(1)} custom-call(bf16[432,512]{1,0:T(8,128)(2,1)S(1)} %bitcast.61), custom_call_target="tpu_custom_call" | custom-call | bytes 2211840 | tf_op jit(solution)/shard_map/pallas_call | solution.py:809
  46.7 1.7 copy-done.21
  48.4 10.3 %shard_map.359 = (bf16[512,1152]{1,0:T(8,128)(2,1)S(1)}, bf16[512,1152]{1,0:T(8,128)(2,1)S(1)}) custom-call(s32[9216]{0:T(1024)S(1)} %copy-done.45, bf16[9216,128]{1,0:T(8,128)(2,1)S(1)} %copy-done.21), custom_call_target="tpu_custom_call" | custom-call | bytes 4755456 | tf_op jit(solution)/shard_map/pallas_call | solution.py:32
  58.7 3.8 shard_map.360
  62.6 6.2 %shard_map.361.totals = f32[8,128]{1,0:T(8,128)S(1)} custom-call(f32[8,128]{1,0:T(8,128)S(1)} %get-tuple-element.60.x), custom_call_target="tpu_custom_call" | custom-call | bytes 8192 | tf_op jit(solution)/shard_map/pallas_call | solution.py:809
  68.8 2.0 shard_map.362.refs_0_
  71.8 23.1 %shard_map.363.x = bf16[1728,512]{1,0:T(8,128)(2,1)S(1)} custom-call(bf16[1728,128]{1,0:T(8,128)(2,1)S(1)} %shard_map.362.refs_0_), custom_call_target="tpu_custom_call" | custom-call | bytes 2211840 | tf_op jit(solution)/shard_map/pallas_call | solution.py:809
  94.9 3.8 shard_map.364
  98.7 6.9 %shard_map.365.totals = f32[8,128]{1,0:T(8,128)S(1)} custom-call(f32[8,128]{1,0:T(8,128)S(1)} %get-tuple-element.63.x), custom_call_target="tpu_custom_call" | custom-call | bytes 8192 | tf_op jit(solution)/shard_map/pallas_call | solution.py:809
  105.6 1.1 shard_map.366.refs_0_
  107.7 22.9 %shard_map.367.features = bf16[1728,512]{1,0:T(8,128)(2,1)S(1)} custom-call(bf16[1728,128]{1,0:T(8,128)(2,1)S(1)} %shard_map.366.refs_0_), custom_call_target="tpu_custom_call" | custom-call | bytes 2211840 | tf_op jit(solution)/shard_map/pallas_call | solution.py:809
  130.6 1.9 slice_bitcast_fusion.1
  132.5 2.3 shard_map.368
  134.9 6.9 %shard_map.369.totals.totals_one = f32[8,512]{1,0:T(8,128)S(1)} custom-call(f32[8,512]{1,0:T(8,128)S(1)} %get-tuple-element.65.x), custom_call_target="tpu_custom_call" | custom-call | bytes 32768 | tf_op jit(solution)/shard_map/pallas_call | solution.py:809
  141.8 2.8 shard_map.370
  144.6 1.2 copy-done.28
  145.8 6.8 %shard_map.371.totals.totals_two = f32[8,512]{1,0:T(8,128)S(1)} custom-call(f32[8,512]{1,0:T(8,128)S(1)} %get-tuple-element.67.x), custom_call_target="tpu_custom_call" | custom-call | bytes 32768 | tf_op jit(solution)/shard_map/pallas_call | solution.py:809
  152.7 2.4 slice_bitcast_fusion.kernel
  155.1 12.2 %shard_map.372 = (bf16[1728,512]{1,0:T(8,128)(2,1)S(1)}, f32[1728,512]{1,0:T(8,128)S(1)}, f32[8,512]{1,0:T(8,128)S(1)}) custom-call(s32[4]{0:T(128)S(1)} %slice_reduce_fusion.small, f32[1728,512]{1,0:T(8,128)S(1)} %get-tuple-element.66.pre_two.pre, f32[8,512]{1,0:T(8,128)S(1)} %shard_map.371.totals.totals_two, ...), custom_call_target="tpu_custom_call" | custom-call | flops 8153726976 | bytes 15372304 | tf_op jit(solution)/shard_map/pallas_call | solution.py:32
  167.4 1.2 copy-done.59
  168.6 6.8 %shard_map.373.totals = f32[8,512]{1,0:T(8,128)S(1)} custom-call(f32[8,512]{1,0:T(8,128)S(1)} %get-tuple-element.69.x), custom_call_target="tpu_custom_call" | custom-call | bytes 32768 | tf_op jit(solution)/shard_map/pallas_call | solution.py:809
  175.5 4.4 shard_map.374
  180.7 6.8 %shard_map.375.sums = f32[8,512]{1,0:T(8,128)S(1)} custom-call(f32[8,512]{1,0:T(8,128)S(1)} %get-tuple-element.71.x), custom_call_target="tpu_custom_call" | custom-call | bytes 32768 | tf_op jit(solution)/shard_map/pallas_call | solution.py:809
  188.1 29.5 %shard_map.376 = (bf16[4608,512]{1,0:T(8,128)(2,1)}, f32[1728,512]{1,0:T(8,128)}) custom-call(s32[4]{0:T(128)} %copy-done.47, f32[1728,512]{1,0:T(8,128)} %copy-done.13, f32[8,512]{1,0:T(8,128)} %copy-done.46, f32[8,512]{1,0:T(8,128)} %copy-done.49, f32[2,512]{1,0:T(2,128)} %copy-done.50, bf16[4,108,512]{2,1,0:T(8,128)(2,1)} %copy.58.cotangent, ...), custom_call_target="tpu_custom_call" | custom-call | flops 16307453952 | bytes 18763792 | tf_op jit(solution)/shard_map/pallas_call | solution.py:32
  217.7 2.0 copy-done.3
  219.7 1.5 copy-done.7
  221.1 4.3 shard_map.377.x
  225.4 6.9 %shard_map.378.sums = f32[8,512]{1,0:T(8,128)S(1)} custom-call(f32[8,512]{1,0:T(8,128)S(1)} %shard_map.377.x), custom_call_target="tpu_custom_call" | custom-call | bytes 32768 | tf_op jit(solution)/shard_map/pallas_call | solution.py:809
  232.4 9.0 %shard_map.379 = (bf16[512,512]{1,0:T(8,128)(2,1)S(1)}, f32[1728,512]{1,0:T(8,128)S(1)}, f32[8,512]{1,0:T(8,128)S(1)}) custom-call(s32[4]{0:T(128)S(1)} %copy-done.48, f32[1728,512]{1,0:T(8,128)S(1)} %copy-done.4, f32[1728,512]{1,0:T(8,128)} %copy-done.2, f32[8,512]{1,0:T(8,128)S(1)} %shard_map.371.totals.totals_two, f32[8,512]{1,0:T(8,128)S(1)} %shard_map.378.sums, ...), custom_call_target="tpu_custom_call" | custom-call | flops 1811939328 | bytes 18817040 | tf_op jit(solution)/shard_map/pallas_call | solution.py:32
  241.3 6.9 %shard_map.380.sums = f32[8,512]{1,0:T(8,128)S(1)} custom-call(f32[8,512]{1,0:T(8,128)S(1)} %get-tuple-element.76.x), custom_call_target="tpu_custom_call" | custom-call | bytes 32768 | tf_op jit(solution)/shard_map/pallas_call | solution.py:809
  248.2 7.1 %shard_map.381 = (bf16[512,512]{1,0:T(8,128)(2,1)S(1)}, bf16[1728,512]{1,0:T(8,128)(2,1)S(1)}) custom-call(s32[4]{0:T(128)S(1)} %copy-done.48, f32[1728,512]{1,0:T(8,128)S(1)} %get-tuple-element.75.upstream, f32[1728,512]{1,0:T(8,128)S(1)} %copy-done.1, f32[8,512]{1,0:T(8,128)S(1)} %shard_map.369.totals.totals_one, f32[8,512]{1,0:T(8,128)S(1)} %shard_map.380.sums, ...), custom_call_target="tpu_custom_call" | custom-call | flops 1811939328 | bytes 18800656 | tf_op jit(solution)/shard_map/pallas_call | solution.py:32
  256.2 22.8 %shard_map.382.upstream = f32[1728,128]{1,0:T(8,128)S(1)} custom-call(bf16[1728,512]{1,0:T(8,128)(2,1)S(1)} %get-tuple-element.77.x), custom_call_target="tpu_custom_call" | custom-call | bytes 2654208 | tf_op jit(solution)/shard_map/pallas_call | solution.py:809
  279.0 1.6 shard_map.383.x
  280.6 6.0 shard_map.384.sums
  286.6 6.9 %shard_map.385 = (f32[512,1152]{1,0:T(8,128)S(1)}, bf16[1728,512]{1,0:T(8,128)(2,1)S(1)}) custom-call(s32[4]{0:T(128)S(1)} %copy-done.48, f32[1728,128]{1,0:T(8,128)S(1)} %shard_map.382.upstream, f32[1728,128]{1,0:T(8,128)S(1)} %copy-done.17, f32[8,128]{1,0:T(8,128)S(1)} %shard_map.365.totals, f32[8,128]{1,0:T(8,128)S(1)} %shard_map.384.sums, ...), custom_call_target="tpu_custom_call" | custom-call | flops 4076863488 | bytes 8863504 | tf_op jit(solution)/shard_map/pallas_call | solution.py:32
  293.5 22.8 %shard_map.386.upstream = f32[1728,128]{1,0:T(8,128)S(1)} custom-call(bf16[1728,512]{1,0:T(8,128)(2,1)S(1)} %get-tuple-element.78.x), custom_call_target="tpu_custom_call" | custom-call | bytes 2654208 | tf_op jit(solution)/shard_map/pallas_call | solution.py:809
  316.3 2.4 shard_map.387.x
  318.7 5.8 shard_map.388.sums
  324.6 8.1 %shard_map.389 = (f32[512,1152]{1,0:T(8,128)S(1)}, bf16[1728,512]{1,0:T(8,128)(2,1)S(1)}) custom-call(s32[4]{0:T(128)S(1)} %copy-done.48, f32[1728,128]{1,0:T(8,128)S(1)} %shard_map.386.upstream, f32[1728,128]{1,0:T(8,128)S(1)} %copy-done.15, f32[8,128]{1,0:T(8,128)S(1)} %shard_map.361.totals, f32[8,128]{1,0:T(8,128)S(1)} %shard_map.388.sums, ...), custom_call_target="tpu_custom_call" | custom-call | flops 4076863488 | bytes 8863504 | tf_op jit(solution)/shard_map/pallas_call | solution.py:32
  332.7 1.2 copy-done.34
  333.9 11.3 %shard_map.391 = bf16[9216,128]{1,0:T(8,128)(2,1)} custom-call(s32[9216]{0:T(1024)S(1)} %copy-done.45, f32[512,1152]{1,0:T(8,128)S(1)} %get-tuple-element.80.enc, f32[512,1152]{1,0:T(8,128)S(1)} %get-tuple-element.81.dec), custom_call_target="tpu_custom_call" | custom-call | bytes 7114752 | tf_op jit(solution)/shard_map/pallas_call | solution.py:32
  346.3 8.5 %pad_maximum_fusion = bf16[5632,512]{1,0:T(8,128)(2,1)} fusion(bf16[4608,512]{1,0:T(8,128)(2,1)} %get-tuple-element.91, bf16[512,512]{1,0:T(8,128)(2,1)S(1)} %get-tuple-element.90, bf16[512,512]{1,0:T(8,128)(2,1)S(1)} %copy-done.42), kind=kLoop, calls=%fused_computation.1 | loop fusion | flops 17301504 | bytes 11534336 | tf_op jit(solution)/shard_map/concatenate | solution.py:1058
  354.8 8.8 %sort.17 = (s32[9216]{0:T(1024)}, s32[9216]{0:T(1024)S(1)}) sort(s32[9216]{0:T(1024)S(1)} %copy-done.45, s32[9216]{0:T(1024)S(1)} %iota.66), dimensions={0}, to_apply=%region_1.2 | sort | flops 129024 | bytes 147456 | tf_op jit(solution)/shard_map/jit(argsort)/sort | solution.py:1006
  363.8 6.5 %gather_fusion = s32[1152]{0:T(1024)S(1)} fusion(s32[9216]{0:T(1024)S(1)} %get-tuple-element.83, s32[2048]{0:T(1024)S(1)} %pad_clamp_fusion), kind=kCustom, calls=%fused_computation | custom fusion | bytes 13824 | tf_op jit(solution)/shard_map/jit(_take)/gather | solution.py:1095
  371.9 22.6 %shard_map.390 = f32[432,512]{1,0:T(8,128)S(1)} custom-call(bf16[1728,512]{1,0:T(8,128)(2,1)S(1)} %copy-done.35), custom_call_target="tpu_custom_call" | custom-call | bytes 2654208 | tf_op jit(solution)/shard_map/pallas_call | solution.py:809
  397.1 16.5 %shard_map.392 = (bf16[1152,512]{1,0:T(8,128)(2,1)S(1)}, f32[8,512]{1,0:T(8,128)S(1)}) custom-call(bf16[1152,128]{1,0:T(8,128)(2,1)S(1)} %copy-done.38, f32[8,128]{1,0:T(8,128)S(1)} %maximum_maximum_fusion.refs_1_), custom_call_target="tpu_custom_call" | custom-call | bytes 1495040 | tf_op jit(solution)/shard_map/pallas_call | solution.py:809
  414.5 1.4 shard_map.394
  416.5 1.4 rev.6
  418.0 44.6 %all-reduce.5 = bf16[2,512,128]{2,1,0:T(8,128)(2,1)} all-reduce(f32[2,512,128]{2,1,0:T(8,128)S(1)} %shard_map.394), channel_id=1, replica_groups=mesh['task'=4,'batch'=8] {'batch'}, use_global_device_ids=true, to_apply=%region_2.3 | all-reduce | flops 131072 | bytes 786432 | tf_op jit(solution)/shard_map/psum | solution.py:1097
  462.6 1.1 copy-done.8
  463.7 1.6 shard_map.398
  465.3 1.3 convert_element_type.53
  467.4 10.8 %shard_map.395 = bf16[1024,512]{1,0:T(8,128)(2,1)S(1)} custom-call(bf16[1024,128]{1,0:T(8,128)(2,1)S(1)} %bitcast.64), custom_call_target="tpu_custom_call" | custom-call | bytes 1310720 | tf_op jit(solution)/shard_map/pallas_call | solution.py:809
  478.5 1.7 copy-done.22
  480.2 1.7 copy-done.23
  481.9 8.0 %shard_map.393 = (f32[1152,512]{1,0:T(8,128)}, f32[1152,512]{1,0:T(8,128)}, f32[1152,512]{1,0:T(8,128)}) custom-call(bf16[1152,512]{1,0:T(8,128)(2,1)S(1)} %get-tuple-element.82.grad, f32[1152,2]{1,0:T(8,128)S(1)} %fusion.owners, f32[1152,512]{1,0:T(8,128)S(1)} %copy-done.20, f32[1152,512]{1,0:T(8,128)S(1)} %copy-done.22, f32[1152,512]{1,0:T(8,128)S(1)} %copy-done.23, ...), custom_call_target="tpu_custom_call" | custom-call | flops 2415919104 | bytes 17441792 | tf_op jit(solution)/shard_map/pallas_call | solution.py:32
  489.9 42.9 %shard_map.396 = (f32[2,512,512]{2,1,0:T(8,128)}, f32[2,512,512]{2,1,0:T(8,128)}) custom-call(f32[2,512,512]{2,1,0:T(8,128)S(1)} %copy-done.54, f32[2,512,512]{2,1,0:T(8,128)S(1)} %copy-done.24, f32[2,512,512]{2,1,0:T(8,128)S(1)} %convert.1.gram), custom_call_target="tpu_custom_call" | custom-call | flops 3221225472 | bytes 10485760 | tf_op jit(solution)/shard_map/pallas_call | solution.py:32
  532.9 6.8 %shard_map.397 = (f32[704,512]{1,0:T(8,128)}, f32[704,512]{1,0:T(8,128)}, f32[704,512]{1,0:T(8,128)}) custom-call(bf16[704,512]{1,0:T(8,128)(2,1)S(1)} %copy-done.9, f32[704,3]{1,0:T(8,128)S(1)} %fusion.1.owners, f32[704,512]{1,0:T(8,128)S(1)} %bitcast.56, f32[704,512]{1,0:T(8,128)S(1)} %bitcast.62, f32[704,512]{1,0:T(8,128)S(1)} %bitcast.63, ...), custom_call_target="tpu_custom_call" | custom-call | flops 2214592512 | bytes 12525824 | tf_op jit(solution)/shard_map/pallas_call | solution.py:32
  539.7 2.0 convert_element_type.54.gram
  542.1 1.9 copy-done.53
  544.0 51.3 %shard_map.399 = (f32[3,512,512]{2,1,0:T(8,128)}, f32[3,512,512]{2,1,0:T(8,128)}) custom-call(f32[3,512,512]{2,1,0:T(8,128)S(1)} %bitcast.65, f32[3,512,512]{2,1,0:T(8,128)S(1)} %bitcast.60, f32[3,512,512]{2,1,0:T(8,128)S(1)} %convert_element_type.54.gram), custom_call_target="tpu_custom_call" | custom-call | flops 4831838208 | bytes 15728640 | tf_op jit(solution)/shard_map/pallas_call | solution.py:32
  (211 shorter events, 17.8 us)
Async XLA Ops:
  7.2 5.2 copy-start.72
  7.2 4.4 copy-start.69
  7.2 15.6 %copy-start.61 = (bf16[1,18,24,512]{3,2,1,0:T(8,128)(2,1)S(1)}, bf16[1,18,24,512]{3,2,1,0:T(8,128)(2,1)}, u32[]{:S(2)}) copy-start(bf16[1,18,24,512]{3,2,1,0:T(8,128)(2,1)} %param.23) | copy-start | bytes 1327108
  7.2 39.5 %all-gather.3.cloned.1.call-start = ((), (), s32[]{:S(2)}) async-start(), calls=%async_computation.2 | async-start | bytes 2654208 | tf_op jit(solution)/shard_map/all_gather | solution.py:992
  9.2 121.5 %all-gather.5.cloned.1.call-start = ((), (), s32[]{:S(2)}) async-start(), calls=%async_computation.3 | async-start | bytes 6488064 | tf_op jit(solution)/shard_map/all_gather | solution.py:993
  11.5 31.9 %copy-start.70 = (f32[2,512]{1,0:T(2,128)S(1)}, f32[2,512]{1,0:T(2,128)}, u32[]{:S(2)}) copy-start(f32[2,512]{1,0:T(2,128)} %param.37) | copy-start | bytes 12292
  11.5 31.9 %copy-start.71 = (f32[2,512]{1,0:T(2,128)S(1)}, f32[2,512]{1,0:T(2,128)}, u32[]{:S(2)}) copy-start(f32[2,512]{1,0:T(2,128)} %param.38) | copy-start | bytes 12292
  11.5 384.6 %reduce-scatter.3.cloned.1.call-start = ((), (), s32[]{:S(2)}) async-start(), calls=%async_computation.4 | async-start | bytes 2654208 | tf_op jit(solution)/shard_map/reduce_scatter | solution.py:1075
  22.9 22.6 %copy-start.62 = (bf16[1,4,1,9,12,512]{5,1,4,3,2,0:T(4,128)(2,1)S(1)}, bf16[1,4,1,9,12,512]{5,1,4,3,2,0:T(4,128)(2,1)}, u32[]{:S(2)}) copy-start(bf16[1,4,1,9,12,512]{5,1,4,3,2,0:T(4,128)(2,1)} %param.45) | copy-start | bytes 1327108
  23.0 23.6 %copy-start.63 = (f32[1,3,512]{2,0,1:T(1,128)S(1)}, f32[1,3,512]{2,0,1:T(1,128)}, u32[]{:S(2)}) copy-start(f32[1,3,512]{2,0,1:T(1,128)} %param.42) | copy-start | bytes 18436
  23.0 23.5 %copy-start.64 = (f32[1,3,512]{2,0,1:T(1,128)S(1)}, f32[1,3,512]{2,0,1:T(1,128)}, u32[]{:S(2)}) copy-start(f32[1,3,512]{2,0,1:T(1,128)} %param.41) | copy-start | bytes 18436
  43.4 15.3 %copy-start.30 = (bf16[1728,512]{1,0:T(8,128)(2,1)}, bf16[1728,512]{1,0:T(8,128)(2,1)S(1)}, u32[]{:S(2)}) copy-start(bf16[1728,512]{1,0:T(8,128)(2,1)S(1)} %shard_map.358.x) | copy-start | bytes 5308420
  43.4 3.3 copy-start.45
  44.9 130.6 %copy-start.47 = (s32[4]{0:T(128)}, s32[4]{0:T(128)S(1)}, u32[]{:S(2)}) copy-start(s32[4]{0:T(128)S(1)} %slice_reduce_fusion.small) | copy-start | bytes 52
  46.5 128.9 %copy-start.50 = (f32[2,512]{1,0:T(2,128)}, f32[2,512]{1,0:T(2,128)S(1)}, u32[]{:S(2)}) copy-start(f32[2,512]{1,0:T(2,128)S(1)} %get-tuple-element.124.scale) | copy-start | bytes 12292
  46.7 1.7 copy-start.21
  58.7 3.9 copy-start.55
  58.7 36.2 %copy-start.57 = (bf16[512,1152]{1,0:T(8,128)(2,1)}, bf16[512,1152]{1,0:T(8,128)(2,1)S(1)}, u32[]{:S(2)}) copy-start(bf16[512,1152]{1,0:T(8,128)(2,1)S(1)} %get-tuple-element.61.taps) | copy-start | bytes 3538948
  94.9 3.8 copy-start.32
  130.6 4.3 copy-start.5
  132.5 9.3 %copy-start.25 = (bf16[512,512]{1,0:T(8,128)(2,1)}, bf16[512,512]{1,0:T(8,128)(2,1)S(1)}, u32[]{:S(2)}) copy-start(bf16[512,512]{1,0:T(8,128)(2,1)S(1)} %get-tuple-element.123.weight) | copy-start | bytes 1572868
  132.5 12.1 %copy-start.11 = (bf16[512,512]{1,0:T(8,128)(2,1)}, bf16[512,512]{1,0:T(8,128)(2,1)S(1)}, u32[]{:S(2)}) copy-start(bf16[512,512]{1,0:T(8,128)(2,1)S(1)} %get-tuple-element.122.weight) | copy-start | bytes 1572868
  132.5 20.1 %copy-start.60 = (bf16[1,5632,512]{2,1,0:T(8,128)(2,1)S(1)}, bf16[1,5632,512]{2,1,0:T(8,128)(2,1)}, u32[]{:S(2)}) copy-start(bf16[1,5632,512]{2,1,0:T(8,128)(2,1)} %all-gather.5.cloned.1.call-done) | copy-start | bytes 17301508
  134.9 20.2 %copy-start = (f32[1728,512]{1,0:T(8,128)}, f32[1728,512]{1,0:T(8,128)S(1)}, u32[]{:S(2)}) copy-start(f32[1728,512]{1,0:T(8,128)S(1)} %get-tuple-element.64.pre_one.pre) | copy-start | bytes 10616836
  145.8 71.9 %copy-start.2 = (f32[1728,512]{1,0:T(8,128)}, f32[1728,512]{1,0:T(8,128)S(1)}, u32[]{:S(2)}) copy-start(f32[1728,512]{1,0:T(8,128)S(1)} %get-tuple-element.66.pre_two.pre) | copy-start | bytes 10616836
  152.7 2.4 copy-start.6
  155.1 20.3 %copy-start.27 = (bf16[4,108,512]{2,1,0:T(8,128)(2,1)S(1)}, bf16[4,108,512]{2,1,0:T(8,128)(2,1)}, u32[]{:S(2)}) copy-start(bf16[4,108,512]{2,1,0:T(8,128)(2,1)} %copy.58.cotangent) | copy-start | bytes 1327108
  168.6 19.6 %copy-start.13 = (f32[1728,512]{1,0:T(8,128)}, f32[1728,512]{1,0:T(8,128)S(1)}, u32[]{:S(2)}) copy-start(f32[1728,512]{1,0:T(8,128)S(1)} %get-tuple-element.68.pre) | copy-start | bytes 10616836
  175.4 12.7 %copy-start.46 = (f32[8,512]{1,0:T(8,128)}, f32[8,512]{1,0:T(8,128)S(1)}, u32[]{:S(2)}) copy-start(f32[8,512]{1,0:T(8,128)S(1)} %shard_map.373.totals) | copy-start | bytes 49156
  188.1 29.5 %copy-start.48 = (s32[4]{0:T(128)S(1)}, s32[4]{0:T(128)}, u32[]{:S(2)}) copy-start(s32[4]{0:T(128)} %copy-done.47) | copy-start | bytes 52
  217.7 2.0 copy-start.3
  221.1 11.2 %copy-start.4 = (f32[1728,512]{1,0:T(8,128)S(1)}, f32[1728,512]{1,0:T(8,128)}, u32[]{:S(2)}) copy-start(f32[1728,512]{1,0:T(8,128)} %get-tuple-element.73.lower) | copy-start | bytes 10616836
  221.1 11.2 %copy-start.12 = (bf16[512,512]{1,0:T(8,128)(2,1)S(1)}, bf16[512,512]{1,0:T(8,128)(2,1)}, u32[]{:S(2)}) copy-start(bf16[512,512]{1,0:T(8,128)(2,1)} %copy-done.11) | copy-start | bytes 1572868
  221.1 11.2 %copy-start.29 = (bf16[1728,512]{1,0:T(8,128)(2,1)S(1)}, bf16[1728,512]{1,0:T(8,128)(2,1)}, u32[]{:S(2)}) copy-start(bf16[1728,512]{1,0:T(8,128)(2,1)} %copy-done.28) | copy-start | bytes 5308420
  232.4 15.9 %copy-start.1 = (f32[1728,512]{1,0:T(8,128)S(1)}, f32[1728,512]{1,0:T(8,128)}, u32[]{:S(2)}) copy-start(f32[1728,512]{1,0:T(8,128)} %copy-done) | copy-start | bytes 10616836
  232.4 15.9 %copy-start.26 = (bf16[512,512]{1,0:T(8,128)(2,1)S(1)}, bf16[512,512]{1,0:T(8,128)(2,1)}, u32[]{:S(2)}) copy-start(bf16[512,512]{1,0:T(8,128)(2,1)} %copy-done.25) | copy-start | bytes 1572868
  256.1 22.8 %copy-start.17 = (f32[1728,128]{1,0:T(8,128)S(1)}, f32[1728,128]{1,0:T(8,128)}, u32[]{:S(2)}) copy-start(f32[1728,128]{1,0:T(8,128)} %copy-done.16) | copy-start | bytes 2654212
  256.1 30.5 %copy-start.33 = (bf16[1728,512]{1,0:T(8,128)(2,1)S(1)}, bf16[1728,512]{1,0:T(8,128)(2,1)}, u32[]{:S(2)}) copy-start(bf16[1728,512]{1,0:T(8,128)(2,1)} %copy-done.32) | copy-start | bytes 5308420
  256.2 30.5 %copy-start.58 = (bf16[512,1152]{1,0:T(8,128)(2,1)S(1)}, bf16[512,1152]{1,0:T(8,128)(2,1)}, u32[]{:S(2)}) copy-start(bf16[512,1152]{1,0:T(8,128)(2,1)} %copy-done.57) | copy-start | bytes 3538948
  286.6 84.1 %copy-start.51 = (f32[8,128]{1,0:T(8,128)}, f32[8,128]{1,0:T(8,128)S(1)}, u32[]{:S(2)}) copy-start(f32[8,128]{1,0:T(8,128)S(1)} %shard_map.384.sums) | copy-start | bytes 12292
  293.5 22.8 %copy-start.15 = (f32[1728,128]{1,0:T(8,128)S(1)}, f32[1728,128]{1,0:T(8,128)}, u32[]{:S(2)}) copy-start(f32[1728,128]{1,0:T(8,128)} %copy-done.14) | copy-start | bytes 2654212
  293.5 31.0 %copy-start.31 = (bf16[1728,512]{1,0:T(8,128)(2,1)S(1)}, bf16[1728,512]{1,0:T(8,128)(2,1)}, u32[]{:S(2)}) copy-start(bf16[1728,512]{1,0:T(8,128)(2,1)} %copy-done.30) | copy-start | bytes 5308420
  293.5 31.0 %copy-start.56 = (bf16[512,1152]{1,0:T(8,128)(2,1)S(1)}, bf16[512,1152]{1,0:T(8,128)(2,1)}, u32[]{:S(2)}) copy-start(bf16[512,1152]{1,0:T(8,128)(2,1)} %copy-done.55) | copy-start | bytes 3538948
  324.6 46.1 %copy-start.52 = (f32[8,128]{1,0:T(8,128)}, f32[8,128]{1,0:T(8,128)S(1)}, u32[]{:S(2)}) copy-start(f32[8,128]{1,0:T(8,128)S(1)} %shard_map.388.sums) | copy-start | bytes 12292
  345.2 117.4 %reduce-scatter.5.cloned.1.call-start = ((), (), s32[]{:S(2)}) async-start(), calls=%async_computation.5 | async-start | bytes 6488064 | tf_op jit(solution)/shard_map/reduce_scatter | solution.py:1059
  354.8 184.9 %all-reduce.4.cloned.1.call-start = ((), (), s32[]{:S(2)}) async-start(), calls=%async_computation.6 | async-start | bytes 3145728 | tf_op jit(solution)/shard_map/psum | solution.py:1084
  363.8 7.0 %copy-start.44 = (bf16[4,108,512]{2,1,0:T(8,128)(2,1)S(1)}, bf16[4,108,512]{2,1,0:T(8,128)(2,1)}, u32[]{:S(2)}) copy-start(bf16[4,108,512]{2,1,0:T(8,128)(2,1)} %copy-done.43) | copy-start | bytes 1327108
  370.3 25.2 %copy-start.65 = (f32[1,3,2,512]{3,2,1,0:T(2,128)S(1)}, f32[1,3,2,512]{3,2,1,0:T(2,128)}, u32[]{:S(2)}) copy-start(f32[1,3,2,512]{3,2,1,0:T(2,128)} %param.43) | copy-start | bytes 36868
  370.3 25.2 %copy-start.66 = (f32[1,3,2,512]{3,2,1,0:T(2,128)S(1)}, f32[1,3,2,512]{3,2,1,0:T(2,128)}, u32[]{:S(2)}) copy-start(f32[1,3,2,512]{3,2,1,0:T(2,128)} %param.44) | copy-start | bytes 36868
  370.7 24.6 %slice-start = ((f32[8,128]{1,0:T(8,128)}), f32[2,128]{1,0:T(2,128)S(1)}, s32[]{:S(2)}) async-start(f32[8,128]{1,0:T(8,128)} %copy-done.51), calls=%async_computation.7 | async-start | bytes 2048 | tf_op jit(solution)/shard_map/slice | solution.py:1091
  370.8 24.6 %slice-start.1 = ((f32[8,128]{1,0:T(8,128)}), f32[2,128]{1,0:T(2,128)S(1)}, s32[]{:S(2)}) async-start(f32[8,128]{1,0:T(8,128)} %copy-done.52), calls=%async_computation.8 | async-start | bytes 2048 | tf_op jit(solution)/shard_map/slice | solution.py:1091
  465.3 2.1 copy-start.40
  466.7 11.8 %copy-start.20 = (f32[1152,512]{1,0:T(8,128)S(1)}, f32[1152,512]{1,0:T(8,128)}, u32[]{:S(2)}) copy-start(f32[1152,512]{1,0:T(8,128)} %weight.1) | copy-start | bytes 7077892
  466.7 11.8 %copy-start.24 = (f32[2,512,512]{2,1,0:T(8,128)S(1)}, f32[2,512,512]{2,1,0:T(8,128)}, u32[]{:S(2)}) copy-start(f32[2,512,512]{2,1,0:T(8,128)} %basis.3) | copy-start | bytes 6291460
  478.5 1.7 copy-start.22
  480.2 1.7 copy-start.23
  481.9 8.0 %copy-start.54 = (f32[2,512,512]{2,1,0:T(8,128)S(1)}, f32[2,512,512]{2,1,0:T(8,128)}, u32[]{:S(2)}) copy-start(f32[2,512,512]{2,1,0:T(8,128)} %stat.1) | copy-start | bytes 6291460
  489.9 43.0 %copy-start.9 = (bf16[704,512]{1,0:T(8,128)(2,1)S(1)}, bf16[704,512]{1,0:T(8,128)(2,1)}, u32[]{:S(2)}) copy-start(bf16[704,512]{1,0:T(8,128)(2,1)} %reduce-scatter.5.cloned.1.call-done.grad.part) | copy-start | bytes 2162692
  489.9 43.0 %copy-start.10 = (f32[1,704,512]{2,1,0:T(8,128)S(1)}, f32[1,704,512]{2,1,0:T(8,128)}, u32[]{:S(2)}) copy-start(f32[1,704,512]{2,1,0:T(8,128)} %param.32) | copy-start | bytes 4325380
  489.9 43.0 %copy-start.18 = (f32[1,3,512,512]{3,2,1,0:T(8,128)S(1)}, f32[1,3,512,512]{3,2,1,0:T(8,128)}, u32[]{:S(2)}) copy-start(f32[1,3,512,512]{3,2,1,0:T(8,128)} %param.36) | copy-start | bytes 9437188
  489.9 43.0 %copy-start.36 = (f32[1,704,512]{2,1,0:T(8,128)S(1)}, f32[1,704,512]{2,1,0:T(8,128)}, u32[]{:S(2)}) copy-start(f32[1,704,512]{2,1,0:T(8,128)} %param.33) | copy-start | bytes 4325380
  489.9 43.0 %copy-start.37 = (f32[1,704,512]{2,1,0:T(8,128)S(1)}, f32[1,704,512]{2,1,0:T(8,128)}, u32[]{:S(2)}) copy-start(f32[1,704,512]{2,1,0:T(8,128)} %param.34) | copy-start | bytes 4325380
  539.7 2.4 copy-start.19
  542.1 1.9 copy-start.53
  (16 other events, 17.6 us)
Sparse Core Ops, SparseCore 0:
  10.3 34.3 all-gather.2
  46.9 60.7 all-gather.4
  345.4 36.2 reduce-scatter.2
  383.8 71.3 reduce-scatter.4
  466.8 59.4 all-reduce.3

commit v2 on v1

v2 whole, which is shorter than its diff:
```python
import functools

import jax
import jax.numpy as jnp
from jax import lax
from jax.experimental import pallas as pl
from jax.experimental.pallas import tpu as pltpu
from jax.sharding import PartitionSpec as P

STEP = 10


EPS = 1e-05
ADAM_EPS = 1e-08
BETA_ONE = 0.95
BETA_TWO = 0.95
STAT_DECAY = 0.95
LEARN_MATRIX = 0.02
LEARN_NORM = 0.5
DECAY_MATRIX = 0.01
BF = jnp.bfloat16
F32 = jnp.float32
MESH = pl.DeviceIdType.MESH
MIB = 1 << 20

VMEM_SPEC = pl.BlockSpec(memory_space=pltpu.VMEM)
SMEM_SPEC = pl.BlockSpec(memory_space=pltpu.SMEM)


def run(body, outs, specs, args, scratch=(), vmem=40, flops=0):
    size = sum(o.size * o.dtype.itemsize for o in outs) + sum(a.size * a.dtype.itemsize for a in args)
    return pl.pallas_call(
        body,
        out_shape=tuple(outs),
        in_specs=[SMEM_SPEC if s == "s" else VMEM_SPEC for s in specs],
        out_specs=tuple(VMEM_SPEC for _ in outs),
        scratch_shapes=list(scratch),
        compiler_params=pltpu.CompilerParams(vmem_limit_bytes=vmem * MIB),
        cost_estimate=pl.CostEstimate(flops=flops, bytes_accessed=size, transcendentals=0),
    )(*args)


def shape(dims, kind):
    return jax.ShapeDtypeStruct(tuple(dims), kind)


def dot(a, b):
    return jnp.dot(a, b, preferred_element_type=F32)


def dot_nt(a, b):
    return lax.dot_general(a, b, (((1,), (1,)), ((), ())), preferred_element_type=F32)


def dot_tn(a, b):
    return lax.dot_general(a, b, (((0,), (0,)), ((), ())), preferred_element_type=F32)


def split(a):
    high = a.astype(BF)
    return high, (a - high.astype(F32)).astype(BF)


def dot3(kind, a, b):
    a_high, a_low = split(a)
    b_high, b_low = split(b)
    return kind(a_high, b_high) + (kind(a_high, b_low) + kind(a_low, b_high))


def places(height, breadth):
    index = lax.broadcasted_iota(jnp.int32, (height * breadth, 1), 0)
    row = lax.div(index, breadth)
    return row, index - row * breadth


def valid_rows(small, height, breadth):
    row, col = places(height, breadth)
    row_limit = jnp.where(small > 0, height // 2, height)
    col_limit = jnp.where(small > 0, breadth // 2, breadth)
    return jnp.where((row < row_limit) & (col < col_limit), 1.0, 0.0).astype(F32)


def move(values, rows):
    gap = jnp.zeros((abs(rows),) + values.shape[1:], values.dtype)
    if rows > 0:
        return jnp.concatenate([gap, values[:-rows]], axis=0)
    return jnp.concatenate([values[-rows:], gap], axis=0)


def from_left(values, col):
    return jnp.where(col > 0, pltpu.roll(values, 1, 0), 0.0)


def from_right(values, col, breadth):
    return jnp.where(col < breadth - 1, pltpu.roll(values, values.shape[0] - 1, 0), 0.0)


def gather_taps(tap, breadth, col):
    lines = [move(tap(b), breadth) + tap(3 + b) + move(tap(6 + b), -breadth) for b in range(3)]
    return lines[1] + from_left(lines[0], col) + from_right(lines[2], col, breadth)


def spread_taps(values, breadth, col):
    lines = [from_right(values, col, breadth), values, from_left(values, col)]
    return [
        move(lines[b], breadth * (a - 1)) if a != 1 else lines[b] for a in range(3) for b in range(3)
    ]


def window_sum(values, row, col, breadth):
    count = values.shape[0]
    pair = values + jnp.where(
        col % 2 == 0, pltpu.roll(values, count - 1, 0), pltpu.roll(values, 1, 0)
    )
    return pair + jnp.where(row % 2 == 0, move(pair, -breadth), move(pair, breadth))


def silu_back(scaled):
    sig = jax.nn.sigmoid(scaled)
    return sig * (1.0 + scaled * (1.0 - sig))


def col_sum(values):
    return jnp.sum(values, axis=0, keepdims=True)


def put_sums(ref, rows):
    width = ref.shape[1]
    rows = list(rows) + [jnp.zeros((1, width), F32)] * (8 - len(rows))
    ref[...] = jnp.concatenate(rows, axis=0)


def each_image(geometry, body, start):
    number, height, breadth = geometry
    pixels = height * breadth

    def step(image, carry):
        return body(image, pl.ds(pl.multiple_of(image * pixels, 16), pixels), carry)

    return lax.fori_loop(0, number, step, start)


def zero_rows(count, width):
    return (jnp.zeros((1, width), F32),) * count


def greet(axes):
    barrier = pltpu.get_barrier_semaphore()
    for axis, size in axes:
        me = lax.axis_index(axis)
        for step in range(1, size):
            pl.semaphore_signal(
                barrier, inc=1, device_id={axis: lax.rem(me + step, size)}, device_id_type=MESH
            )
    pl.semaphore_wait(barrier, sum(size - 1 for _, size in axes))


def remote(source, target, sends, receives, peer, axis):
    return pltpu.make_async_remote_copy(
        src_ref=source,
        dst_ref=target,
        send_sem=sends,
        recv_sem=receives,
        device_id={axis: peer},
        device_id_type=MESH,
    )


def pack(rows):
    parts = [row[:, i : i + 128] for row in rows for i in range(0, row.shape[1], 128)]
    parts += [jnp.zeros((1, 128), F32)] * (8 - len(parts))
    return jnp.concatenate(parts, axis=0)


def unpack(tile, count, width):
    per = width // 128
    return [
        jnp.concatenate([tile[k * per + i : k * per + i + 1, :] for i in range(per)], axis=1)
        for k in range(count)
    ]


def total_rows(k, axis, size, rows, mine, slots, sends, receives):
    me = lax.axis_index(axis)
    tile = pack(rows)
    mine[k] = tile
    slots[k, me] = tile
    for step in range(1, size):
        peer = lax.rem(me + step, size)
        remote(mine.at[k], slots.at[k, me], sends.at[k, step], receives.at[k, me], peer, axis).start()
    for step in range(1, size):
        peer = lax.rem(me + size - step, size)
        remote(
            mine.at[k], slots.at[k, peer], sends.at[k, step], receives.at[k, peer], peer, axis
        ).wait_recv()
    total = slots[k, 0]
    for peer in range(1, size):
        total = total + slots[k, peer]
    for step in range(1, size):
        peer = lax.rem(me + step, size)
        remote(
            mine.at[k], slots.at[k, me], sends.at[k, step], receives.at[k, me], peer, axis
        ).wait_send()
    return unpack(total, len(rows), rows[0].shape[1])


def total_scratch(count, size):
    return [
        pltpu.VMEM((count, 8, 128), F32),
        pltpu.VMEM((count, size, 8, 128), F32),
        pltpu.SemaphoreType.DMA((count, size)),
        pltpu.SemaphoreType.DMA((count, size)),
    ]


def columns_of(place, width):
    return pl.ds(pl.multiple_of(place * width, 128), width)


def exchange_kernel(body, outs, specs, args, scratch, identity, vmem, flops=0):
    size = sum(o.size * o.dtype.itemsize for o in outs) + sum(a.size * a.dtype.itemsize for a in args)
    return pl.pallas_call(
        body,
        out_shape=tuple(outs),
        in_specs=[SMEM_SPEC if s == "s" else VMEM_SPEC for s in specs],
        out_specs=tuple(VMEM_SPEC for _ in outs),
        scratch_shapes=list(scratch),
        compiler_params=pltpu.CompilerParams(
            vmem_limit_bytes=vmem * MIB, collective_id=identity, has_side_effects=True
        ),
        cost_estimate=pl.CostEstimate(flops=flops, bytes_accessed=size, transcendentals=0),
    )(*args)


def norm_with(values, totals, scale):
    total, squares, count = totals
    center = total / count
    inverse = lax.rsqrt(squares / count - center * center + EPS)
    normal = (values - center) * inverse
    return normal, inverse, normal * scale[0] + scale[1]


def norm_back_with(upstream, normal, inverse, count, sums, scale, valid):
    return scale[0] * inverse * (upstream - sums[0] / count - normal * (sums[1] / count)) * valid


def silu(values):
    return values * jax.nn.sigmoid(values)


def window_count(height, breadth):
    return -(-(height * breadth // 4) // 16) * 16


def pool_choice(height, breadth, windows, flipped):
    pixels = height * breadth
    dims = (windows, pixels) if flipped else (pixels, windows)
    pixel = lax.broadcasted_iota(jnp.int32, dims, 1 if flipped else 0)
    window = lax.broadcasted_iota(jnp.int32, dims, 0 if flipped else 1)
    row = lax.div(pixel, breadth)
    col = pixel - row * breadth
    home = lax.div(row, 2) * (breadth // 2) + lax.div(col, 2)
    return jnp.where(home == window, 1.0, 0.0).astype(F32)


def rows_of(ref, first, count):
    return [ref[first + k : first + k + 1, :] for k in range(count)]


def window_rows(i, windows):
    return pl.ds(pl.multiple_of(i * windows, 16), windows)


def trunk_forward_body(
    geometry, tasks, batches,
    small, x, enc_taps, dec_taps, scales, choose,
    enc_pre, enc_totals, spread, dec_pre, dec_totals, features,
    work, pooled, pooled_all, part, pool_sends, pool_receives, sends, receives,
    mine, slots, total_sends, total_receives,
):
    number, height, breadth = geometry
    width = enc_pre.shape[1]
    windows = window_count(height, breadth)
    task = lax.axis_index("task")
    _, col = places(height, breadth)
    widen = pool_choice(height, breadth, windows, False).astype(BF)
    narrow = pool_choice(height, breadth, windows, True).astype(BF)

    def conv(x, taps, pre):
        def image(i, rows, carry):
            valid = valid_rows(small[i], height, breadth)
            work[...] = dot(x[rows, :], taps[...])
            out = gather_taps(lambda p: work[:, p * width : (p + 1) * width], breadth, col)
            pre[rows, :] = out
            kept = out * valid
            return (
                carry[0] + col_sum(kept),
                carry[1] + col_sum(kept * out),
                carry[2] + jnp.broadcast_to(col_sum(valid), (1, width)),
            )

        return each_image(geometry, image, zero_rows(3, width))

    def total(k, rows):
        return total_rows(
            k, "batch", batches, list(rows), mine, slots, total_sends, total_receives
        )

    sums = conv(x, enc_taps, enc_pre)
    greet((("task", tasks), ("batch", batches)))
    totals = total(0, sums)
    put_sums(enc_totals, totals)
    scale = rows_of(scales, 0, 2)

    def peer_of(step, incoming):
        return lax.rem(task + (tasks - step if incoming else step), tasks)

    def pool_copy(i, step, incoming=False):
        rows = window_rows(i, windows)
        peer = peer_of(step, incoming)
        target = pooled_all.at[rows, columns_of(peer if incoming else task, width)]
        return remote(
            pooled.at[rows, :], target, pool_sends.at[i, step], pool_receives.at[i, step], peer, "task"
        )

    def pool(i, rows, carry):
        valid = valid_rows(small[i], height, breadth)
        _, _, scaled = norm_with(enc_pre[rows, :], totals, scale)
        high, low = split(silu(scaled) * valid)
        mean = ((dot(narrow, high) + dot(narrow, low)) * 0.25).astype(BF)
        here = window_rows(i, windows)
        pooled[here, :] = mean
        pooled_all[here, columns_of(task, width)] = mean
        for step in range(1, tasks):
            pool_copy(i, step).start()
        return carry

    each_image(geometry, pool, 0)

    def unpool(i, rows, carry):
        for step in range(1, tasks):
            pool_copy(i, step, True).wait_recv()
        wide = dot(widen, pooled_all[window_rows(i, windows), :])
        spread[rows, :] = (wide * choose[rows, :]).astype(BF)
        return carry

    each_image(geometry, unpool, 0)
    sums = conv(spread, dec_taps, dec_pre)
    totals = total(1, sums)
    put_sums(dec_totals, totals)
    scale = rows_of(scales, 2, 2)

    def feature_copy(i, rows, step, incoming=False):
        peer = peer_of(step, incoming)
        target = features.at[rows, columns_of(peer if incoming else task, width)]
        return remote(
            part.at[rows, :], target, sends.at[i, step], receives.at[i, step], peer, "task"
        )

    def finish(i, rows, carry):
        valid = valid_rows(small[i], height, breadth)
        _, _, scaled = norm_with(dec_pre[rows, :], totals, scale)
        low = (silu(scaled) * valid).astype(BF)
        part[rows, :] = low
        features[rows, columns_of(task, width)] = low
        for step in range(1, tasks):
            feature_copy(i, rows, step).start()
        return carry

    each_image(geometry, finish, 0)

    def settle(i, rows, carry):
        for step in range(1, tasks):
            feature_copy(i, rows, step, True).wait_recv()
            feature_copy(i, rows, step).wait_send()
            pool_copy(i, step).wait_send()
        return carry

    each_image(geometry, settle, 0)


def trunk_forward(geometry, tasks, batches, small, x, enc_taps, dec_taps, scales, choose):
    number, height, breadth = geometry
    pixels = height * breadth
    channels = x.shape[1]
    width = channels // tasks
    windows = window_count(height, breadth)
    return exchange_kernel(
        functools.partial(trunk_forward_body, geometry, tasks, batches),
        [
            shape((x.shape[0], width), F32),
            shape((8, width), F32),
            shape(x.shape, BF),
            shape((x.shape[0], width), F32),
            shape((8, width), F32),
            shape(x.shape, BF),
        ],
        "svvvvv",
        (small, x, enc_taps, dec_taps, scales, choose),
        [
            pltpu.VMEM((pixels, 9 * width), F32),
            pltpu.VMEM((number * windows, width), BF),
            pltpu.VMEM((number * windows, channels), BF),
            pltpu.VMEM((x.shape[0], width), BF),
        ]
        + [pltpu.SemaphoreType.DMA((number, tasks))] * 4
        + total_scratch(2, batches),
        1,
        32,
        flops=4 * x.size * enc_taps.shape[1],
    )


def head_body(
    geometry, tasks, batches,
    small, features, rows_in, cotangent, scales, counts,
    task_out, grads, upstream, norm_sums,
    pre_one, pre_two, pre_three, hidden, gated, nine, work, lower, out, arrived, sends, receives,
    mine, slots, total_sends, total_receives,
):
    number, height, breadth = geometry
    channels = features.shape[1]
    width = channels // tasks
    windows = task_out.shape[1]
    task = lax.axis_index("task")
    half = work.shape[2]
    _, col = places(height, breadth)
    widen = pool_choice(height, breadth, windows, False).astype(BF)
    narrow = pool_choice(height, breadth, windows, True).astype(BF)
    count = jnp.broadcast_to(counts[2:3, 0:1], (1, channels))
    first = rows_in.at[pl.ds(0, channels), :]
    second = rows_in.at[pl.ds(channels, channels), :]

    def kernel_rows(p):
        return pl.ds((2 + p) * channels, channels)

    def total(k, rows):
        return total_rows(
            k, "batch", batches, list(rows), mine, slots, total_sends, total_receives
        )

    def put_stats(pre, rows, value, valid, carry):
        pre[rows, :] = value
        kept = value * valid
        return carry[0] + col_sum(kept), carry[1] + col_sum(kept * value)

    nothing = zero_rows(2, channels)
    scale_one, scale_two, scale_three = (rows_of(scales, 2 * k, 2) for k in range(3))

    def first_step(i, rows, carry):
        valid = valid_rows(small[i], height, breadth)
        return put_stats(pre_one, rows, dot(features[rows, :], first[...]), valid, carry)

    sums = each_image(geometry, first_step, nothing)
    greet((("task", tasks), ("batch", batches)))
    totals_one = total(0, sums) + [count]

    def second_step(i, rows, carry):
        valid = valid_rows(small[i], height, breadth)
        _, _, scaled = norm_with(pre_one[rows, :], totals_one, scale_one)
        low = (silu(scaled) * valid).astype(BF)
        hidden[rows, :] = low
        return put_stats(pre_two, rows, dot(low, second[...]), valid, carry)

    sums = each_image(geometry, second_step, nothing)
    totals_two = total(1, sums) + [count]

    def third_step(i, rows, carry):
        valid = valid_rows(small[i], height, breadth)
        _, _, scaled = norm_with(pre_two[rows, :], totals_two, scale_two)
        low = (jax.nn.sigmoid(scaled) * features[rows, :].astype(F32)).astype(BF)
        gated[rows, :] = low
        parts = []
        for j in range(channels // half):
            cut = slice(j * half, (j + 1) * half)
            for p in range(9):
                work[p] = dot(low, rows_in[kernel_rows(p), cut])
            parts.append(gather_taps(lambda p: work[p], breadth, col))
        return put_stats(pre_three, rows, jnp.concatenate(parts, axis=1), valid, carry)

    sums = each_image(geometry, third_step, nothing)
    totals_three = total(2, sums) + [count]

    def out_step(i, rows, carry):
        valid = valid_rows(small[i], height, breadth)
        normal, _, scaled = norm_with(pre_three[rows, :], totals_three, scale_three)
        high, low = split(silu(scaled) * valid)
        mean = (dot(narrow, high) + dot(narrow, low)) * 0.25
        task_out[i] = mean.astype(BF)
        dy = silu_back(scaled) * dot(widen, cotangent[i]) * 0.25 * valid
        lower[rows, :] = dy
        return carry[0] + col_sum(dy), carry[1] + col_sum(dy * normal)

    sums = each_image(geometry, out_step, nothing)
    sums_three = total(3, sums)

    def third_back(i, rows, carry):
        valid = valid_rows(small[i], height, breadth)
        normal, inverse, _ = norm_with(pre_three[rows, :], totals_three, scale_three)
        dz = norm_back_with(lower[rows, :], normal, inverse, count, sums_three, scale_three, valid)
        for p, moved in enumerate(spread_taps(dz, breadth, col)):
            nine[p, rows, :] = moved.astype(BF)
        flow = None
        for p in range(9):
            piece = dot_nt(nine[p, rows, :], rows_in[kernel_rows(p), :])
            flow = piece if flow is None else flow + piece
        lower[rows, :] = flow
        normal, _, scaled = norm_with(pre_two[rows, :], totals_two, scale_two)
        gate = jax.nn.sigmoid(scaled)
        dy = flow * features[rows, :].astype(F32) * gate * (1.0 - gate) * valid
        pre_three[rows, :] = dy
        return carry[0] + col_sum(dy), carry[1] + col_sum(dy * normal)

    sums = each_image(geometry, third_back, nothing)
    sums_two = total(4, sums)

    def second_back(i, rows, carry):
        valid = valid_rows(small[i], height, breadth)
        normal, inverse, scaled = norm_with(pre_two[rows, :], totals_two, scale_two)
        dz = norm_back_with(
            pre_three[rows, :], normal, inverse, count, sums_two, scale_two, valid
        ).astype(BF)
        out[rows, :] = dz
        lower[rows, :] = lower[rows, :] * jax.nn.sigmoid(scaled)
        normal, _, scaled = norm_with(pre_one[rows, :], totals_one, scale_one)
        dy = silu_back(scaled) * dot_nt(dz, second[...]) * valid
        pre_three[rows, :] = dy
        return carry[0] + col_sum(dy), carry[1] + col_sum(dy * normal)

    sums = each_image(geometry, second_back, nothing)
    sums_one = total(5, sums)
    grads[pl.ds(channels, channels), :] = dot_tn(hidden[...], out[...]).astype(BF)

    def flow_copy(i, rows, step, incoming=False):
        peer = lax.rem(task + (tasks - step if incoming else step), tasks)
        return remote(
            out.at[rows, columns_of(peer, width)], arrived.at[step - 1, rows, :],
            sends.at[i, step], receives.at[i, step], peer, "task",
        )

    def first_back(i, rows, carry):
        valid = valid_rows(small[i], height, breadth)
        normal, inverse, _ = norm_with(pre_one[rows, :], totals_one, scale_one)
        dz = norm_back_with(
            pre_three[rows, :], normal, inverse, count, sums_one, scale_one, valid
        ).astype(BF)
        hidden[rows, :] = dz
        flow = (lower[rows, :] + dot_nt(dz, first[...])) * valid
        out[rows, :] = flow.astype(BF)
        for step in range(1, tasks):
            flow_copy(i, rows, step).start()
        return carry

    each_image(geometry, first_back, 0)
    grads[pl.ds(0, channels), :] = dot_tn(features[...], hidden[...]).astype(BF)

    def tap(p, carry):
        rows = pl.ds(pl.multiple_of((2 + p) * channels, channels), channels)
        grads[rows, :] = dot_tn(gated[...], nine[p]).astype(BF)
        return carry

    lax.fori_loop(0, 9, tap, 0)
    put_sums(norm_sums, sums_one + sums_two + sums_three)

    def settle(i, rows, carry):
        for step in range(1, tasks):
            flow_copy(i, rows, step, True).wait_recv()
        flow = out[rows, columns_of(task, width)].astype(F32)
        for step in range(1, tasks):
            flow = flow + arrived[step - 1, rows, :].astype(F32)
        upstream[rows, :] = flow
        for step in range(1, tasks):
            flow_copy(i, rows, step).wait_send()
        return carry

    each_image(geometry, settle, 0)


def head(geometry, tasks, batches, small, features, rows_in, cotangent, scales, counts):
    number, height, breadth = geometry
    pixels = height * breadth
    total, channels = features.shape
    width = channels // tasks
    return exchange_kernel(
        functools.partial(head_body, geometry, tasks, batches),
        [
            shape((number, pixels // 4, channels), BF),
            shape(rows_in.shape, BF),
            shape((total, width), F32),
            shape((8, channels), F32),
        ],
        "svvvvv",
        (small, features, rows_in, cotangent, scales, counts),
        [
            pltpu.VMEM(features.shape, F32),
            pltpu.VMEM(features.shape, F32),
            pltpu.VMEM(features.shape, F32),
            pltpu.VMEM(features.shape, BF),
            pltpu.VMEM(features.shape, BF),
            pltpu.VMEM((9,) + features.shape, BF),
            pltpu.VMEM((9, pixels, min(channels, 256)), F32),
            pltpu.VMEM(features.shape, F32),
            pltpu.VMEM(features.shape, BF),
            pltpu.VMEM((tasks - 1, total, width), BF),
        ]
        + [pltpu.SemaphoreType.DMA((number, tasks))] * 2
        + total_scratch(6, batches),
        2,
        60,
        flops=6 * total * channels * rows_in.shape[0],
    )


def trunk_backward_body(
    geometry, tasks, batches,
    small, upstream, enc_pre, enc_totals, dec_pre, dec_totals, scales, choose, choose_row,
    x, spread, enc_taps, dec_taps,
    enc_grad, dec_grad, flow_out, norm_sums,
    nine, change, packed, arrived, pooled, sends, receives,
    mine, slots, total_sends, total_receives,
):
    number, height, breadth = geometry
    channels = x.shape[1]
    width = enc_pre.shape[1]
    windows = window_count(height, breadth)
    task = lax.axis_index("task")
    _, col = places(height, breadth)
    widen = pool_choice(height, breadth, windows, False).astype(BF)
    narrow = pool_choice(height, breadth, windows, True)
    nothing = zero_rows(2, width)

    def total(k, rows):
        return total_rows(
            k, "batch", batches, list(rows), mine, slots, total_sends, total_receives
        )

    def change_of(pre, totals, scale, flow):
        def image(i, rows, carry):
            valid = valid_rows(small[i], height, breadth)
            normal, _, scaled = norm_with(pre[rows, :], totals, scale)
            dy = silu_back(scaled) * flow(i, rows) * valid
            change[rows, :] = dy
            return carry[0] + col_sum(dy), carry[1] + col_sum(dy * normal)

        return each_image(geometry, image, nothing)

    def back(pre, totals, scale, sums, taps, put):
        def image(i, rows, carry):
            valid = valid_rows(small[i], height, breadth)
            normal, inverse, _ = norm_with(pre[rows, :], totals, scale)
            dz = norm_back_with(change[rows, :], normal, inverse, totals[2], sums, scale, valid)
            for p, moved in enumerate(spread_taps(dz, breadth, col)):
                nine[rows, p * width : (p + 1) * width] = moved.astype(BF)
            put(i, rows, dot_nt(nine[rows, :], taps[...]) * valid)
            return carry

        each_image(geometry, image, 0)

    totals = rows_of(dec_totals, 0, 3)
    scale = rows_of(scales, 2, 2)
    sums = change_of(dec_pre, totals, scale, lambda i, rows: upstream[rows, :])
    greet((("task", tasks), ("batch", batches)))
    dec_sums = total(0, sums)

    def copy_of(i, step, incoming=False):
        rows = window_rows(i, windows)
        peer = lax.rem(task + (tasks - step if incoming else step), tasks)
        return remote(
            packed.at[rows, columns_of(peer, width)], arrived.at[step - 1, rows, :],
            sends.at[i, step], receives.at[i, step], peer, "task",
        )

    def put_packed(i, rows, flow):
        chosen = (narrow * choose_row[i]).astype(BF)
        packed[window_rows(i, windows), :] = dot(chosen, flow.astype(BF)).astype(BF)
        for step in range(1, tasks):
            copy_of(i, step).start()

    back(dec_pre, totals, scale, dec_sums, dec_taps, put_packed)
    dec_grad[...] = dot_tn(spread[...], nine[...])

    def collect(i, carry):
        for step in range(1, tasks):
            copy_of(i, step, True).wait_recv()
        rows = window_rows(i, windows)
        flow = packed[rows, columns_of(task, width)].astype(F32)
        for step in range(1, tasks):
            flow = flow + arrived[step - 1, rows, :].astype(F32)
        pooled[rows, :] = flow
        for step in range(1, tasks):
            copy_of(i, step).wait_send()
        return carry

    lax.fori_loop(0, number, collect, 0)

    def widened(i, rows):
        high, low = split(pooled[window_rows(i, windows), :])
        return (dot(widen, high) + dot(widen, low)) * 0.25

    totals = rows_of(enc_totals, 0, 3)
    scale = rows_of(scales, 0, 2)
    sums = change_of(enc_pre, totals, scale, widened)
    enc_sums = total(1, sums)

    def put_flow(i, rows, flow):
        flow_out[rows, :] = flow.astype(BF)

    back(enc_pre, totals, scale, enc_sums, enc_taps, put_flow)
    enc_grad[...] = dot_tn(x[...], nine[...])
    put_sums(norm_sums, enc_sums + dec_sums)


def trunk_backward(
    geometry, tasks, batches, small, upstream, enc_pre, enc_totals, dec_pre, dec_totals, scales,
    choose, choose_row, x, spread, enc_taps, dec_taps,
):
    number, height, breadth = geometry
    total, channels = x.shape
    width = channels // tasks
    windows = window_count(height, breadth)
    return exchange_kernel(
        functools.partial(trunk_backward_body, geometry, tasks, batches),
        [
            shape(enc_taps.shape, F32),
            shape(dec_taps.shape, F32),
            shape(x.shape, BF),
            shape((8, width), F32),
        ],
        "svvvvvvvvvvvv",
        (small, upstream, enc_pre, enc_totals, dec_pre, dec_totals, scales, choose, choose_row, x,
         spread, enc_taps, dec_taps),
        [
            pltpu.VMEM((total, 9 * width), BF),
            pltpu.VMEM((total, width), F32),
            pltpu.VMEM((number * windows, channels), BF),
            pltpu.VMEM((tasks - 1, number * windows, width), BF),
            pltpu.VMEM((number * windows, width), F32),
        ]
        + [pltpu.SemaphoreType.DMA((number, tasks))] * 2
        + total_scratch(2, batches),
        3,
        40,
        flops=8 * x.size * enc_taps.shape[1],
    )


def exchange(body, outs, args, scratch, identity, vmem=32):
    size = sum(o.size * o.dtype.itemsize for o in outs) + sum(a.size * a.dtype.itemsize for a in args)
    return pl.pallas_call(
        body,
        out_shape=tuple(outs),
        in_specs=[VMEM_SPEC] * len(args),
        out_specs=tuple(VMEM_SPEC for _ in outs),
        scratch_shapes=list(scratch),
        compiler_params=pltpu.CompilerParams(
            vmem_limit_bytes=vmem * MIB, collective_id=identity, has_side_effects=True
        ),
        cost_estimate=pl.CostEstimate(flops=0, bytes_accessed=size, transcendentals=0),
    )(*args)


def block_of(ref, place, size, dim):
    length = ref.shape[dim] // size
    start = place * length
    if dim == 0:
        return ref.at[pl.ds(pl.multiple_of(start, 8), length), :]
    return ref.at[:, pl.ds(pl.multiple_of(start, 128), length)]


def gather_body(axis, size, dims, *refs):
    count = len(dims)
    sources, targets = refs[:count], refs[count : 2 * count]
    sends, receives, own = refs[2 * count :]
    greet(((axis, size),))
    me = lax.axis_index(axis)
    copies = []
    for k in range(count):
        mine = block_of(targets[k], me, size, dims[k])
        for step in range(1, size):
            peer = lax.rem(me + step, size)
            copy = remote(sources[k], mine, sends.at[k, step], receives.at[k, me], peer, axis)
            copy.start()
            copies.append(copy)
    locals_ = []
    for k in range(count):
        mine = block_of(targets[k], me, size, dims[k])
        copy = pltpu.make_async_copy(sources[k], mine, own.at[k])
        copy.start()
        locals_.append(copy)
    for copy in locals_:
        copy.wait()
    for k in range(count):
        for step in range(1, size):
            peer = lax.rem(me + size - step, size)
            theirs = block_of(targets[k], peer, size, dims[k])
            remote(
                sources[k], theirs, sends.at[k, step], receives.at[k, peer], peer, axis
            ).wait_recv()
    for copy in copies:
        copy.wait_send()


def gather_over(axis, size, arrays, dims, identity):
    outs = []
    for x, dim in zip(arrays, dims):
        full = list(x.shape)
        full[dim] *= size
        outs.append(shape(full, x.dtype))
    count = len(arrays)
    return exchange(
        functools.partial(gather_body, axis, size, tuple(dims)),
        outs,
        arrays,
        [
            pltpu.SemaphoreType.DMA((count, size)),
            pltpu.SemaphoreType.DMA((count, size)),
            pltpu.SemaphoreType.DMA((count,)),
        ],
        identity,
    )


def to_taps_body(index, slots, enc, dec, wide, tap):
    count = slots.shape[0]
    channels = enc.shape[0]
    width = slots.shape[1]
    step = 1024

    def widen(i, carry):
        rows = pl.ds(pl.multiple_of(i * step, step), step)
        wide[rows, :] = slots[rows, :].astype(F32)
        return carry

    lax.fori_loop(0, count // step, widen, 0)
    group = 32
    for p in range(18):

        def fetch(i, carry):
            base = i * group
            for u in range(group):
                tap[pl.ds(base + u, 1), :] = wide[pl.ds(index[p * channels + base + u], 1), :]
            return carry

        lax.fori_loop(0, channels // group, fetch, 0)
        out = enc if p < 9 else dec
        q = p % 9
        out[:, q * width : (q + 1) * width] = tap[...].astype(BF)


def to_taps(index, slots, channels):
    width = slots.shape[1]
    return run(
        to_taps_body,
        [shape((channels, 9 * width), BF)] * 2,
        "sv",
        (index, slots),
        [pltpu.VMEM(slots.shape, F32), pltpu.VMEM((channels, width), F32)],
    )


def to_slots_body(index, enc, dec, slots, wide):
    count = slots.shape[0]
    channels = enc.shape[0]
    width = slots.shape[1]
    step = 1024
    group = 32
    for p in range(18):
        source = enc if p < 9 else dec
        q = p % 9

        def place(i, carry):
            base = pl.multiple_of(i * group, group)
            values = source[pl.ds(base, group), q * width : (q + 1) * width]
            for u in range(group):
                wide[pl.ds(index[p * channels + base + u], 1), :] = values[u : u + 1, :]
            return carry

        lax.fori_loop(0, channels // group, place, 0)

    def narrow(i, carry):
        rows = pl.ds(pl.multiple_of(i * step, step), step)
        slots[rows, :] = wide[rows, :].astype(BF)
        return carry

    lax.fori_loop(0, count // step, narrow, 0)


def to_slots(index, enc, dec):
    width = enc.shape[1] // 9
    dims = (index.shape[0], width)
    return run(
        to_slots_body, [shape(dims, BF)], "svv", (index, enc, dec), [pltpu.VMEM(dims, F32)]
    )[0]


def adam(gradient, moment_one, moment_two):
    new_one = BETA_ONE * moment_one + (1.0 - BETA_ONE) * gradient
    new_two = BETA_TWO * moment_two + (1.0 - BETA_TWO) * gradient * gradient
    direction = (
        new_one / (1.0 - BETA_ONE**STEP) / (jnp.sqrt(new_two / (1.0 - BETA_TWO**STEP)) + ADAM_EPS)
    )
    return new_one, new_two, direction


def soap_body(
    cuts, grad, owners, weight, one, two, basis, weight_new, one_new, two_new, low
):
    count = basis.shape[0]
    total = grad.shape[0]
    for m in range(count):
        low[m] = basis[m].astype(BF)

    def chunk(i, carry):
        rows = pl.ds(pl.multiple_of(i * (total // cuts), 8), total // cuts)
        values = grad[rows, :].astype(F32)
        rotated = None
        for m in range(count):
            part = dot((values * owners[rows, m : m + 1]).astype(BF), low[m])
            rotated = part if rotated is None else rotated + part
        new_one, new_two, direction = adam(rotated, one[rows, :], two[rows, :])
        one_new[rows, :] = new_one
        two_new[rows, :] = new_two
        stepped = None
        for m in range(count):
            part = dot_nt((direction * owners[rows, m : m + 1]).astype(BF), low[m])
            stepped = part if stepped is None else stepped + part
        old = weight[rows, :]
        weight_new[rows, :] = old - LEARN_MATRIX * (stepped + DECAY_MATRIX * old)
        return carry

    lax.fori_loop(0, cuts, chunk, 0)


def soap(grad, owners, weight, one, two, basis):
    total = grad.shape[0]
    cuts = 4 if total % 64 == 0 else 1
    return run(
        functools.partial(soap_body, cuts),
        [shape(weight.shape, F32)] * 3,
        "vvvvvv",
        (grad, owners, weight, one, two, basis),
        [pltpu.VMEM(basis.shape, BF)],
        flops=4 * weight.size * weight.shape[1] * basis.shape[0],
    )


def grams_body(grad, part, owners, grams):
    for m in range(grams.shape[0]):
        held = (grad[...].astype(F32) * owners[:, m : m + 1]).astype(BF)
        grams[m] = dot_tn(held, part[...])


def owner_grams(grad, part, owners):
    dims = (owners.shape[1], grad.shape[1], part.shape[1])
    return run(
        grams_body,
        [shape(dims, F32)],
        "vvv",
        (grad, part, owners),
        flops=2 * grad.size * part.shape[1] * owners.shape[1],
    )[0]


def factor_rows(values, identity, turn):
    width = values.shape[1]
    sub = lax.broadcasted_iota(jnp.int32, (8, width), 0)
    rolled = pltpu.roll(values, turn, 1)
    columns = [jnp.broadcast_to(rolled[:, j : j + 1], (8, width)) for j in range(8)]
    scale = jnp.zeros((8, width), F32)
    for j in range(8):
        root = lax.rsqrt(columns[j][j : j + 1, :])
        scale = jnp.where(sub == j, root, scale)
        lower = jnp.where(sub > j, columns[j] * root, 0.0)
        values = values - lower * (values[j : j + 1, :] * root)
        identity = identity - lower * (identity[j : j + 1, :] * root)
        for i in range(j + 1, 8):
            columns[i] = columns[i] - lower * (columns[i][j : j + 1, :] * root)
    return values * scale, identity * scale


def renew_body(counts, *refs):
    groups = len(counts)
    stats, bases, grams = (refs[k * groups : (k + 1) * groups] for k in range(3))
    stats_new, bases_new = (refs[k * groups : (k + 1) * groups] for k in (3, 4))
    count = sum(counts)
    product = refs[5 * groups]
    tables = refs[5 * groups + 1 : 5 * groups + 1 + count]
    inverses = refs[5 * groups + 1 + count :]
    homes = [(g, m) for g in range(groups) for m in range(counts[g])]
    size = stats[0].shape[1]
    panel = 128
    matrices = range(count)
    row = lax.broadcasted_iota(jnp.int32, (panel, panel), 0)
    col = lax.broadcasted_iota(jnp.int32, (panel, panel), 1)
    unit = jnp.where(row == col, 1.0, 0.0).astype(F32)
    for n, (g, m) in enumerate(homes):
        new = STAT_DECAY * stats[g][m] + (1.0 - STAT_DECAY) * grams[g][m].astype(F32)
        stats_new[g][m] = new
        product[n] = dot3(dot, new, bases[g][m])
    for k in range(size // panel):
        here = slice(k * panel, (k + 1) * panel)
        for n in matrices:
            tables[n][:, :panel] = dot3(dot_tn, product[n, :, here], product[n, :, here])
            tables[n][:, panel:] = unit

        def group(q, carry):
            rows = pl.ds(pl.multiple_of(q * 8, 8), 8)
            turn = lax.rem(panel - q * 8, panel)
            done = [
                factor_rows(tables[n][rows, :panel], tables[n][rows, panel:], turn)
                for n in matrices
            ]
            for n in matrices:
                upper, inverse = done[n]
                inverses[n][rows, :] = inverse
                both = jnp.concatenate([upper, inverse], axis=1)
                tables[n][...] = tables[n][...] - dot3(dot_tn, upper, both)
            return carry

        lax.fori_loop(0, panel // 8, group, 0)
        for n, (g, m) in enumerate(homes):
            turned = dot3(dot_nt, product[n, :, here], inverses[n][...])
            bases_new[g][m, :, here] = turned
            if k < size // panel - 1:
                rest = slice((k + 1) * panel, size)
                product[n, :, rest] = product[n, :, rest] - dot3(
                    dot, turned, dot3(dot_tn, turned, product[n, :, rest])
                )


def renew_bases(stats, bases, grams):
    counts = tuple(s.shape[0] for s in stats)
    count = sum(counts)
    size = stats[0].shape[1]
    return run(
        functools.partial(renew_body, counts),
        [shape(s.shape, F32) for s in stats] * 2,
        "v" * (3 * len(stats)),
        (*stats, *bases, *grams),
        [pltpu.VMEM((count, size, size), F32)]
        + [pltpu.VMEM((128, 256), F32)] * count
        + [pltpu.VMEM((128, 128), F32)] * count,
        flops=60 * MIB * MIB // 1024,
    )


def local(
    tasks,
    batches,
    images,
    image_small,
    pool_index,
    row_slot,
    trunk_weight,
    trunk_mean_grad,
    trunk_mean_square,
    trunk_statistic,
    trunk_basis,
    head_weight,
    head_mean_grad,
    head_mean_square,
    head_statistic,
    head_basis,
    trunk_gain,
    trunk_offset,
    trunk_norm_mean_grad,
    trunk_norm_mean_square,
    head_gain,
    head_offset,
    head_norm_mean_grad,
    head_norm_mean_square,
    cotangent,
):
    number, height, breadth, channels = images.shape
    pixels = height * breadth
    tap_rows = 9 * channels
    shown = tasks * number
    geometry = (shown, height, breadth)
    task = lax.axis_index("task")
    batch = lax.axis_index("batch")
    width = channels // tasks

    def quarter(values):
        return lax.dynamic_slice_in_dim(values, task * width, width, values.ndim - 1)

    def inside(flags):
        row_limit = jnp.where(flags > 0, height // 2, height)[:, None, None]
        col_limit = jnp.where(flags > 0, breadth // 2, breadth)[:, None, None]
        return (jnp.arange(height, dtype=jnp.int32)[None, :, None] < row_limit) & (
            jnp.arange(breadth, dtype=jnp.int32)[None, None, :] < col_limit
        )

    slots = lax.all_gather(quarter(trunk_weight).astype(BF), "batch", axis=0, tiled=True)
    head_rows = lax.all_gather(head_weight.astype(BF), "batch", axis=1, tiled=True)[0]
    kinds = jnp.concatenate([image_small, pool_index.reshape(-1)])
    kinds = lax.all_gather(kinds, "task", axis=0, tiled=True).reshape(tasks, -1)
    small = kinds[:, :number].reshape(-1)
    cells = kinds[:, number:].reshape(shown, height // 2, 1, breadth // 2, 1)
    cell = 2 * jnp.arange(2, dtype=jnp.int32)[:, None, None] + jnp.arange(2, dtype=jnp.int32)
    choose = (cells == cell).reshape(shown, height, breadth) & inside(small)
    choose = choose.astype(F32)
    choose_row = choose.reshape(shown, 1, pixels)
    choose = choose.reshape(shown * pixels, 1)
    masked = (images * inside(image_small)[..., None].astype(BF)).reshape(number * pixels, channels)
    x = gather_over("task", tasks, (masked,), (0,), 4)[0]
    enc_taps, dec_taps = to_taps(row_slot, slots, channels)

    scales = quarter(jnp.stack([trunk_gain, trunk_offset], axis=1)).reshape(4, width)
    enc_pre, enc_totals, spread, dec_pre, dec_totals, features = trunk_forward(
        geometry, tasks, batches, small, x, enc_taps, dec_taps, scales, choose
    )
    head_scales = jnp.stack([head_gain[0], head_offset[0]], axis=1).reshape(6, channels)
    pooled, head_grads, upstream, head_sums = head(
        geometry, tasks, batches, small, features, head_rows,
        cotangent.reshape(shown, pixels // 4, channels), head_scales, enc_totals,
    )
    task_features = pooled.reshape(cotangent.shape)
    head_owned = lax.psum_scatter(head_grads, "batch", scatter_dimension=0, tiled=True)
    enc_grad, dec_grad, flow, trunk_sums = trunk_backward(
        geometry, tasks, batches, small, upstream, enc_pre, enc_totals, dec_pre, dec_totals,
        scales, choose, choose_row, x, spread, enc_taps, dec_taps,
    )
    trunk_part = lax.psum_scatter(
        to_slots(row_slot, enc_grad, dec_grad), "batch", scatter_dimension=0, tiled=True
    )
    input_grad = lax.psum_scatter(flow, "task", scatter_dimension=0, tiled=True)
    input_grad = input_grad.astype(F32).reshape(images.shape)

    head_local = head_weight.shape[1]
    head_ids = batch * head_local + jnp.arange(head_local, dtype=jnp.int32)
    head_owner = jnp.minimum(head_ids // channels, 2)
    head_onehot = (head_owner[:, None] == jnp.arange(3, dtype=jnp.int32)).astype(F32)
    head_grams = lax.psum(owner_grams(head_owned, head_owned, head_onehot).astype(BF), "batch")
    head_weight_new, head_one_new, head_two_new = soap(
        head_owned, head_onehot, head_weight[0], head_mean_grad[0], head_mean_square[0],
        head_basis[0],
    )

    trunk_owned, norm_sums = gather_over("task", tasks, (trunk_part, trunk_sums), (1, 1), 5)
    local_rows = trunk_weight.shape[0]
    slot_ids = batch * local_rows + jnp.arange(local_rows, dtype=jnp.int32)
    trunk_owner = jnp.take(jnp.argsort(row_slot), slot_ids) // tap_rows
    trunk_onehot = (trunk_owner[:, None] == jnp.arange(2, dtype=jnp.int32)).astype(F32)
    trunk_grams = lax.psum(owner_grams(trunk_owned, trunk_part, trunk_onehot), "batch").astype(BF)
    trunk_grams = gather_over(
        "task", tasks, (trunk_grams.reshape(2 * channels, width),), (1,), 6
    )[0].reshape(2, channels, channels)
    trunk_weight_new, trunk_one_new, trunk_two_new = soap(
        trunk_owned, trunk_onehot, trunk_weight, trunk_mean_grad, trunk_mean_square, trunk_basis
    )
    trunk_stat_new, head_stat_new, trunk_basis_new, head_basis_new = renew_bases(
        (trunk_statistic, head_statistic[0]),
        (trunk_basis, head_basis[0]),
        (trunk_grams, head_grams),
    )

    trunk_norm = jnp.stack([trunk_gain, trunk_offset], axis=1)
    trunk_norm_grad = norm_sums[:4].reshape(2, 2, channels)[:, ::-1]
    trunk_norm_one, trunk_norm_two, trunk_direction = adam(
        trunk_norm_grad, trunk_norm_mean_grad, trunk_norm_mean_square
    )
    head_norm = jnp.stack([head_gain, head_offset], axis=2)
    head_norm_grad = head_sums[:6].reshape(1, 3, 2, channels)[:, :, ::-1]
    head_norm_one, head_norm_two, head_direction = adam(
        head_norm_grad, head_norm_mean_grad, head_norm_mean_square
    )
    return (
        task_features,
        input_grad,
        trunk_weight_new,
        trunk_one_new,
        trunk_two_new,
        trunk_stat_new,
        trunk_basis_new,
        head_weight_new[None],
        head_one_new[None],
        head_two_new[None],
        head_stat_new[None],
        head_basis_new[None],
        trunk_norm - LEARN_NORM * trunk_direction,
        trunk_norm_one,
        trunk_norm_two,
        head_norm - LEARN_NORM * head_direction,
        head_norm_one,
        head_norm_two,
    )


def solution(mesh):
    placed = (
        P(("task", "batch"), None, None, None),
        P(("task", "batch")),
        P(("task", "batch"), None, None),
        P(),
        P("batch", None),
        P("batch", None),
        P("batch", None),
        P(),
        P(),
        P("task", "batch", None),
        P("task", "batch", None),
        P("task", "batch", None),
        P("task", None, None, None),
        P("task", None, None, None),
        P(),
        P(),
        P(),
        P(),
        P("task", None, None),
        P("task", None, None),
        P("task", None, None, None),
        P("task", None, None, None),
        P("task", None, "batch", None, None, None),
    )
    return jax.shard_map(
        functools.partial(local, mesh.shape["task"], mesh.shape["batch"]),
        mesh=mesh,
        in_specs=placed,
        out_specs=(
            P("task", None, "batch", None, None, None),
            P(("task", "batch"), None, None, None),
            P("batch", None),
            P("batch", None),
            P("batch", None),
            P(),
            P(),
            P("task", "batch", None),
            P("task", "batch", None),
            P("task", "batch", None),
            P("task", None, None, None),
            P("task", None, None, None),
            P(),
            P(),
            P(),
            P("task", None, None, None),
            P("task", None, None, None),
            P("task", None, None, None),
        ),
        check_vma=False,
    )
```

time: 612 us -> 552 us (0.902)
  Pallas kernels: 463 us -> 319 us
  waiting for transfers between devices: 0.13 us -> 86.1 us
  local copies, waits for them, and re-layouts: 43.6 us -> 54.4 us
  other arithmetic: 26 us -> 16.6 us
    pallas_call x18 -> x3, Pallas kernels: 228 us -> 45.8 us  [exchange(): pl.pallas_call(body, out_shape=tuple(outs), in_specs=[VMEM_SPEC] * len(ar...]
    pallas_call x0 -> x3, Pallas kernels: none -> 162 us  [exchange_kernel(): pl.pallas_call(body, out_shape=tuple(outs), in_specs=[SMEM_SPEC if s == '...]
    pallas_call x24 -> x7, Pallas kernels: 235 us -> 112 us  [run(): pl.pallas_call(body, out_shape=tuple(outs), in_specs=[SMEM_SPEC if s == '...]
    reduce_scatter x1, waiting for transfers between devices: 0.01 us -> 48.8 us  [local(): lax.psum_scatter(head_grads, 'batch', scatter_dimension=0, tiled=True)]
    reduce_scatter x1, waiting for transfers between devices: 0.01 us -> 36.6 us  [local(): lax.psum_scatter(to_slots(row_slot, enc_grad, dec_grad), 'batch', scatter...]
    unnamed x149 -> x115, local copies, waits for them, and re-layouts: 24.1 us -> 41 us
    concatenate x2 -> x0, other arithmetic: 8.56 us -> none  [the longest x1 8.49 us: local(): head_grads = jnp.concatenate([first_grad, second_grad, kernel_grad], axis=0)]
  transfers between devices with their start and end apart: 5 -> 6, of which waited for: 0 -> 2; matrix products, arithmetic and copies ran while one was open for 6% -> 5% of each run, Pallas kernels for 35% -> 25%
where the time goes in v2:
time: 552 us; the launch traced here: 541 us
  Pallas kernels  319 us (58%)
  waiting for transfers between devices  86.1 us (16%)
  local copies, waits for them, and re-layouts  54.4 us (10%)
  blocking collectives  47.8 us (9%)
  other arithmetic  16.6 us (3%)
  between operations  16.6 us (3%)
    pallas_call x3, Pallas kernels, exchange_kernel(): pl.pallas_call(body, out_shape=tuple(outs), in_specs=[SMEM_SPEC if s == '...  162 us
    pallas_call x7, Pallas kernels, run(): pl.pallas_call(body, out_shape=tuple(outs), in_specs=[SMEM_SPEC if s == '...  112 us
    reduce_scatter x1, waiting for transfers between devices, local(): lax.psum_scatter(head_grads, 'batch', scatter_dimension=0, tiled=True)  48.8 us
    pallas_call x3, Pallas kernels, exchange(): pl.pallas_call(body, out_shape=tuple(outs), in_specs=[VMEM_SPEC] * len(ar...  45.8 us
    unnamed x115, local copies, waits for them, and re-layouts  41 us
    psum x1, blocking collectives, local(): lax.psum(owner_grams(trunk_owned, trunk_part, trunk_onehot), 'batch')  39 us
    reduce_scatter x1, waiting for transfers between devices, local(): lax.psum_scatter(to_slots(row_slot, enc_grad, dec_grad), 'batch', scatter...  36.6 us
  transfers between devices with their start and end apart: 6, of which 2 were waited for; matrix products, arithmetic and copies ran while one was open for 5% of the time, Pallas kernels for 25%

profile of v2, /device:TPU:0, one launch (start us, length us, event | category | flops | bytes accessed | tf_op | source)
XLA Modules:
  0.0 541.2 jit_solution(17520072012819904216)
XLA Ops:
  7.3 1.8 dynamic-slice_convert_fusion
  9.2 2.4 convert_element_type.49
  12.4 0.6 dynamic-slice
  13.8 8.8 %all-reduce = s32[436]{0:T(512)S(1)} all-reduce(s32[436]{0:T(512)S(1)} %add_dynamic-update-slice_fusion), channel_id=1, replica_groups=mesh['task'=4,'batch'=8] {'task'}, use_global_device_ids=true, to_apply=%add | all-reduce | flops 436 | bytes 3488
  23.2 0.4 and.119
  24.3 20.4 %shard_map.358.x = bf16[1728,512]{1,0:T(8,128)(2,1)S(1)} custom-call(bf16[432,512]{1,0:T(8,128)(2,1)S(1)} %bitcast.33), custom_call_target="tpu_custom_call" | custom-call | bytes 2211840 | tf_op jit(solution)/shard_map/pallas_call | solution.py:749
  45.5 0.4 copy.79
  45.9 0.8 copy.81.cotangent
  46.8 0.6 reshape.404.scales
  47.8 1.7 copy-done.7
  49.5 10.3 %shard_map.359 = (bf16[512,1152]{1,0:T(8,128)(2,1)S(1)}, bf16[512,1152]{1,0:T(8,128)(2,1)S(1)}) custom-call(s32[9216]{0:T(1024)S(1)} %copy-done.21, bf16[9216,128]{1,0:T(8,128)(2,1)S(1)} %copy-done.7), custom_call_target="tpu_custom_call" | custom-call | bytes 4755456 | tf_op jit(solution)/shard_map/pallas_call | solution.py:32
  59.8 49.3 %shard_map.360 = (f32[1728,128]{1,0:T(8,128)S(1)}, f32[8,128]{1,0:T(8,128)S(1)}, bf16[1728,512]{1,0:T(8,128)(2,1)S(1)}, f32[1728,128]{1,0:T(8,128)S(1)}, f32[8,1...) custom-call(s32[4]{0:T(128)S(1)} %slice_reduce_fusion.small, bf16[1728,512]{1,0:T(8,128)(2,1)S(1)} %shard_map.358.x, ...), custom_call_target="tpu_custom_call" | custom-call | flops 4076863488 | bytes 9454352 | tf_op jit(solution)/shard_map/pallas_call | solution.py:222
  109.1 1.0 copy-done.27
  110.1 1.0 copy-done.29
  111.1 1.2 copy-done.31
  112.3 1.2 copy-done.33
  113.5 0.9 copy-done.34
  114.4 0.9 copy-done.36
  115.3 0.6 copy-done.39
  115.9 85.5 %shard_map.361 = (bf16[4,108,512]{2,1,0:T(8,128)(2,1)}, bf16[5632,512]{1,0:T(8,128)(2,1)}, f32[1728,128]{1,0:T(8,128)}, f32[8,512]{1,0:T(8,128)}) custom-call(s32[4]{0:T(128)} %copy-done.22, bf16[1728,512]{1,0:T(8,128)(2,1)} %copy-done.33, bf16[5632,512]{1,0:T(8,128)(2,1)} %bitcast.54, bf16[4,108,512]{2,1,0:T(8,128)(2,1)} %copy.81.cotangent, ...), custom_call_target="tpu_custom_call" | custom-call | flops 29896998912 | bytes 15106064 | tf_op jit(solution)/shard_map/pallas_call | solution.py:222
  201.5 1.5 copy-done.14
  202.9 1.3 copy-done.28
  204.2 1.3 copy-done.30
  205.5 1.5 copy-done.32
  207.0 1.2 copy-done.35
  208.1 1.2 copy-done.37
  209.3 1.2 copy-done.38
  210.5 0.7 copy-done.40
  211.1 27.0 %shard_map.362 = (f32[512,1152]{1,0:T(8,128)S(1)}, f32[512,1152]{1,0:T(8,128)}, bf16[1728,512]{1,0:T(8,128)(2,1)S(1)}, f32[8,128]{1,0:T(8,128)S(1)}) custom-call(s32[4]{0:T(128)S(1)} %copy-done.23, f32[1728,128]{1,0:T(8,128)S(1)} %copy-done.38, f32[1728,128]{1,0:T(8,128)S(1)} %copy-done.35, f32[8,128]{1,0:T(8,128)S(1)} %copy-done.40, ...), custom_call_target="tpu_custom_call" | custom-call | flops 8153726976 | bytes 15068688 | tf_op jit(solution)/shard_map/pallas_call | solution.py:222
  238.1 1.2 copy-done.12
  239.4 1.7 copy-done.6
  241.1 11.3 %shard_map.363 = bf16[9216,128]{1,0:T(8,128)(2,1)} custom-call(s32[9216]{0:T(1024)S(1)} %copy-done.21, f32[512,1152]{1,0:T(8,128)S(1)} %get-tuple-element.58.enc, f32[512,1152]{1,0:T(8,128)S(1)} %copy-done.6), custom_call_target="tpu_custom_call" | custom-call | bytes 7114752 | tf_op jit(solution)/shard_map/pallas_call | solution.py:32
  252.5 0.5 reduce-scatter.8.cloned.1.call-update
  253.3 8.8 %sort.17 = (s32[9216]{0:T(1024)}, s32[9216]{0:T(1024)S(1)}) sort(s32[9216]{0:T(1024)S(1)} %copy-done.21, s32[9216]{0:T(1024)S(1)} %iota.68), dimensions={0}, to_apply=%region_2.3 | sort | flops 129024 | bytes 147456 | tf_op jit(solution)/shard_map/jit(argsort)/sort | solution.py:1142
  262.2 6.5 %gather_fusion = s32[1152]{0:T(1024)S(1)} fusion(s32[9216]{0:T(1024)S(1)} %get-tuple-element.62, s32[2048]{0:T(1024)S(1)} %pad_clamp_fusion), kind=kCustom, calls=%fused_computation | custom fusion | bytes 13824 | tf_op jit(solution)/shard_map/jit(_take)/gather | solution.py:1142
  269.1 1.1 copy.82
  270.4 0.7 maximum_subtract_fusion
  271.0 2.0 convert.1
  273.1 36.6 %reduce-scatter.6.cloned.1.call-done.refs_0_.part = bf16[1152,128]{1,0:T(8,128)(2,1)} async-done(((bf16[9216,128]{1,0:T(8,128)(2,1)}), bf16[1152,128]{1,0:T(8,128)(2,1)}) %reduce-scatter.6.cloned.1.call-update) | async-done | bytes 294928 | tf_op jit(solution)/shard_map/reduce_scatter | solution.py:1123
  309.7 1.0 copy-done.17
  310.7 14.1 %shard_map.364 = (bf16[1152,512]{1,0:T(8,128)(2,1)S(1)}, f32[8,512]{1,0:T(8,128)S(1)}) custom-call(bf16[1152,128]{1,0:T(8,128)(2,1)S(1)} %copy-done.17, f32[8,128]{1,0:T(8,128)S(1)} %get-tuple-element.60.refs_1_), custom_call_target="tpu_custom_call" | custom-call | bytes 1495040 | tf_op jit(solution)/shard_map/pallas_call | solution.py:749
  324.8 1.0 copy-done.18
  325.7 1.4 shard_map.366
  327.1 48.8 %reduce-scatter.8.cloned.1.call-done.grad.part = bf16[704,512]{1,0:T(8,128)(2,1)} async-done(((bf16[5632,512]{1,0:T(8,128)(2,1)}), bf16[704,512]{1,0:T(8,128)(2,1)}) %reduce-scatter.8.cloned.1.call-update) | async-done | bytes 720912 | tf_op jit(solution)/shard_map/reduce_scatter | solution.py:1118
  375.9 1.1 copy-done
  377.0 1.6 shard_map.368
  378.6 1.3 convert_element_type.54
  380.0 39.0 %all-reduce.5 = bf16[2,512,128]{2,1,0:T(8,128)(2,1)S(1)} all-reduce(f32[2,512,128]{2,1,0:T(8,128)S(1)} %shard_map.366), channel_id=1, replica_groups=mesh['task'=4,'batch'=8] {'batch'}, use_global_device_ids=true, to_apply=%region_3.4 | all-reduce | flops 131072 | bytes 786432 | tf_op jit(solution)/shard_map/psum | solution.py:1144
  419.0 11.3 %shard_map.367 = bf16[1024,512]{1,0:T(8,128)(2,1)S(1)} custom-call(bf16[1024,128]{1,0:T(8,128)(2,1)S(1)} %bitcast.36), custom_call_target="tpu_custom_call" | custom-call | bytes 1310720 | tf_op jit(solution)/shard_map/pallas_call | solution.py:749
  430.2 1.0 copy-done.19
  431.3 0.6 copy.89
  431.9 0.6 copy.90
  432.5 0.6 copy.91
  433.1 1.7 copy-done.5
  434.8 1.7 copy-done.8
  436.5 1.7 copy-done.9
  438.2 1.6 copy-done.10
  439.8 8.0 %shard_map.365 = (f32[1152,512]{1,0:T(8,128)}, f32[1152,512]{1,0:T(8,128)}, f32[1152,512]{1,0:T(8,128)}) custom-call(bf16[1152,512]{1,0:T(8,128)(2,1)S(1)} %get-tuple-element.61.grad, f32[1152,2]{1,0:T(8,128)S(1)} %fusion.owners, f32[1152,512]{1,0:T(8,128)S(1)} %copy-done.5, f32[1152,512]{1,0:T(8,128)S(1)} %copy-done.8, f32[1152,512]{1,0:T(8,128)S(1)} %copy-done.9, ...), custom_call_target="tpu_custom_call" | custom-call | flops 2415919104 | bytes 17441792 | tf_op jit(solution)/shard_map/pallas_call | solution.py:32
  447.8 6.8 %shard_map.370 = (f32[704,512]{1,0:T(8,128)}, f32[704,512]{1,0:T(8,128)}, f32[704,512]{1,0:T(8,128)}) custom-call(bf16[704,512]{1,0:T(8,128)(2,1)S(1)} %copy-done.1, f32[704,3]{1,0:T(8,128)S(1)} %fusion.1.owners, f32[704,512]{1,0:T(8,128)S(1)} %bitcast.30, f32[704,512]{1,0:T(8,128)S(1)} %bitcast.34, f32[704,512]{1,0:T(8,128)S(1)} %bitcast.35, ...), custom_call_target="tpu_custom_call" | custom-call | flops 2214592512 | bytes 12525824 | tf_op jit(solution)/shard_map/pallas_call | solution.py:32
  454.6 1.9 copy-done.4
  456.5 1.6 copy-done.11
  458.1 1.9 copy-done.24
  460.0 1.4 copy-done.26
  461.4 72.5 %shard_map.369 = (f32[2,512,512]{2,1,0:T(8,128)}, f32[3,512,512]{2,1,0:T(8,128)}, f32[2,512,512]{2,1,0:T(8,128)}, f32[3,512,512]{2,1,0:T(8,128)}) custom-call(f32[2,512,512]{2,1,0:T(8,128)S(1)} %copy-done.25, f32[3,512,512]{2,1,0:T(8,128)S(1)} %bitcast.40, f32[2,512,512]{2,1,0:T(8,128)S(1)} %copy-done.11, f32[3,512,512]{2,1,0:T(8,128)S(1)} %bitcast.32, ...), custom_call_target="tpu_custom_call" | custom-call | flops 64424509440 | bytes 23592960 | tf_op jit(solution)/shard_map/pallas_call | solution.py:32
  (143 shorter events, 3.9 us)
Async XLA Ops:
  7.2 5.2 copy-start.54
  7.2 4.4 copy-start.53
  7.2 40.6 %all-gather.3.cloned.1.call-start = ((), (), s32[]{:S(2)}) async-start(), calls=%async_computation.3 | async-start | bytes 2654208 | tf_op jit(solution)/shard_map/all_gather | solution.py:1093
  9.1 15.0 %copy-start.42 = (bf16[1,18,24,512]{3,2,1,0:T(8,128)(2,1)S(1)}, bf16[1,18,24,512]{3,2,1,0:T(8,128)(2,1)}, u32[]{:S(2)}) copy-start(bf16[1,18,24,512]{3,2,1,0:T(8,128)(2,1)} %param.23) | copy-start | bytes 1327108
  9.1 106.2 %all-gather.5.cloned.1.call-start = ((), (), s32[]{:S(2)}) async-start(), calls=%async_computation.4 | async-start | bytes 6488064 | tf_op jit(solution)/shard_map/all_gather | solution.py:1094
  11.5 33.2 %copy-start.46 = (f32[2,512]{1,0:T(2,128)S(1)}, f32[2,512]{1,0:T(2,128)}, u32[]{:S(2)}) copy-start(f32[2,512]{1,0:T(2,128)} %param.37) | copy-start | bytes 12292
  11.5 33.2 %copy-start.47 = (f32[2,512]{1,0:T(2,128)S(1)}, f32[2,512]{1,0:T(2,128)}, u32[]{:S(2)}) copy-start(f32[2,512]{1,0:T(2,128)} %param.38) | copy-start | bytes 12292
  11.6 259.5 %reduce-scatter.4.cloned.1.call-start = ((), (), s32[]{:S(2)}) async-start(), calls=%async_computation.5 | async-start | bytes 2211840 | tf_op jit(solution)/shard_map/reduce_scatter | solution.py:1126
  22.9 36.9 %copy-start.22 = (s32[4]{0:T(128)}, s32[4]{0:T(128)S(1)}, u32[]{:S(2)}) copy-start(s32[4]{0:T(128)S(1)} %slice_reduce_fusion.small) | copy-start | bytes 52
  24.2 21.7 %copy-start.43 = (bf16[1,4,1,9,12,512]{5,1,4,3,2,0:T(4,128)(2,1)S(1)}, bf16[1,4,1,9,12,512]{5,1,4,3,2,0:T(4,128)(2,1)}, u32[]{:S(2)}) copy-start(bf16[1,4,1,9,12,512]{5,1,4,3,2,0:T(4,128)(2,1)} %param.45) | copy-start | bytes 1327108
  24.3 22.5 %copy-start.44 = (f32[1,3,512]{2,0,1:T(1,128)S(1)}, f32[1,3,512]{2,0,1:T(1,128)}, u32[]{:S(2)}) copy-start(f32[1,3,512]{2,0,1:T(1,128)} %param.42) | copy-start | bytes 18436
  24.3 22.5 %copy-start.45 = (f32[1,3,512]{2,0,1:T(1,128)S(1)}, f32[1,3,512]{2,0,1:T(1,128)}, u32[]{:S(2)}) copy-start(f32[1,3,512]{2,0,1:T(1,128)} %param.41) | copy-start | bytes 18436
  44.7 15.1 %copy-start.13 = (bf16[1728,512]{1,0:T(8,128)(2,1)}, bf16[1728,512]{1,0:T(8,128)(2,1)S(1)}, u32[]{:S(2)}) copy-start(bf16[1728,512]{1,0:T(8,128)(2,1)S(1)} %shard_map.358.x) | copy-start | bytes 5308420
  45.0 2.8 copy-start.21
  47.8 1.7 copy-start.7
  109.1 1.0 copy-start.27
  110.1 1.0 copy-start.29
  111.1 1.2 copy-start.31
  112.3 1.2 copy-start.33
  113.5 0.9 copy-start.34
  114.4 0.9 copy-start.36
  115.3 0.6 copy-start.39
  115.9 85.5 %copy-start.23 = (s32[4]{0:T(128)S(1)}, s32[4]{0:T(128)}, u32[]{:S(2)}) copy-start(s32[4]{0:T(128)} %copy-done.22) | copy-start | bytes 52
  201.5 1.5 copy-start.14
  202.9 1.3 copy-start.28
  204.2 1.3 copy-start.30
  205.5 1.5 copy-start.32
  207.0 1.2 copy-start.35
  208.1 1.2 copy-start.37
  209.3 1.2 copy-start.38
  210.5 0.7 copy-start.40
  238.1 1.2 copy-start.12
  239.4 70.4 %reduce-scatter.6.cloned.1.call-start = ((), (), s32[]{:S(2)}) async-start(), calls=%async_computation.6 | async-start | bytes 2654208 | tf_op jit(solution)/shard_map/reduce_scatter | solution.py:1123
  239.4 1.7 copy-start.6
  252.4 123.5 %reduce-scatter.8.cloned.1.call-start = ((), (), s32[]{:S(2)}) async-start(), calls=%async_computation.7 | async-start | bytes 6488064 | tf_op jit(solution)/shard_map/reduce_scatter | solution.py:1118
  253.0 201.6 %all-reduce.4.cloned.1.call-start = ((), (), s32[]{:S(2)}) async-start(), calls=%async_computation.8 | async-start | bytes 3145728 | tf_op jit(solution)/shard_map/psum | solution.py:1133
  262.1 7.0 %copy-start.41 = (bf16[4,108,512]{2,1,0:T(8,128)(2,1)S(1)}, bf16[4,108,512]{2,1,0:T(8,128)(2,1)}, u32[]{:S(2)}) copy-start(bf16[4,108,512]{2,1,0:T(8,128)(2,1)} %get-tuple-element.51) | copy-start | bytes 1327108
  262.1 8.1 %copy-start.48 = (f32[8,512]{1,0:T(8,128)S(1)}, f32[8,512]{1,0:T(8,128)}, u32[]{:S(2)}) copy-start(f32[8,512]{1,0:T(8,128)} %get-tuple-element.75) | copy-start | bytes 49156
  262.1 8.2 %copy-start.49 = (f32[1,3,2,512]{3,2,1,0:T(2,128)S(1)}, f32[1,3,2,512]{3,2,1,0:T(2,128)}, u32[]{:S(2)}) copy-start(f32[1,3,2,512]{3,2,1,0:T(2,128)} %param.43) | copy-start | bytes 36868
  262.1 8.2 %copy-start.50 = (f32[1,3,2,512]{3,2,1,0:T(2,128)S(1)}, f32[1,3,2,512]{3,2,1,0:T(2,128)}, u32[]{:S(2)}) copy-start(f32[1,3,2,512]{3,2,1,0:T(2,128)} %param.44) | copy-start | bytes 36868
  309.7 1.0 copy-start.17
  324.8 1.0 copy-start.18
  375.9 1.1 copy-start
  379.9 51.3 %copy-start.51 = (f32[2,2,512]{2,1,0:T(2,128)S(1)}, f32[2,2,512]{2,1,0:T(2,128)}, u32[]{:S(2)}) copy-start(f32[2,2,512]{2,1,0:T(2,128)} %param.39) | copy-start | bytes 24580
  379.9 51.3 %copy-start.52 = (f32[2,2,512]{2,1,0:T(2,128)S(1)}, f32[2,2,512]{2,1,0:T(2,128)}, u32[]{:S(2)}) copy-start(f32[2,2,512]{2,1,0:T(2,128)} %param.40) | copy-start | bytes 24580
  430.2 1.0 copy-start.19
  433.1 1.7 copy-start.5
  434.8 1.7 copy-start.8
  436.5 1.7 copy-start.9
  438.2 1.6 copy-start.10
  439.8 8.0 %copy-start.1 = (bf16[704,512]{1,0:T(8,128)(2,1)S(1)}, bf16[704,512]{1,0:T(8,128)(2,1)}, u32[]{:S(2)}) copy-start(bf16[704,512]{1,0:T(8,128)(2,1)} %reduce-scatter.8.cloned.1.call-done.grad.part) | copy-start | bytes 2162692
  439.8 8.0 %copy-start.2 = (f32[1,704,512]{2,1,0:T(8,128)S(1)}, f32[1,704,512]{2,1,0:T(8,128)}, u32[]{:S(2)}) copy-start(f32[1,704,512]{2,1,0:T(8,128)} %param.32) | copy-start | bytes 4325380
  439.8 8.0 %copy-start.3 = (f32[1,3,512,512]{3,2,1,0:T(8,128)S(1)}, f32[1,3,512,512]{3,2,1,0:T(8,128)}, u32[]{:S(2)}) copy-start(f32[1,3,512,512]{3,2,1,0:T(8,128)} %param.36) | copy-start | bytes 9437188
  439.8 8.0 %copy-start.15 = (f32[1,704,512]{2,1,0:T(8,128)S(1)}, f32[1,704,512]{2,1,0:T(8,128)}, u32[]{:S(2)}) copy-start(f32[1,704,512]{2,1,0:T(8,128)} %param.33) | copy-start | bytes 4325380
  439.8 8.0 %copy-start.16 = (f32[1,704,512]{2,1,0:T(8,128)S(1)}, f32[1,704,512]{2,1,0:T(8,128)}, u32[]{:S(2)}) copy-start(f32[1,704,512]{2,1,0:T(8,128)} %param.34) | copy-start | bytes 4325380
  447.8 6.8 %copy-start.20 = (bf16[1024,512]{1,0:T(8,128)(2,1)S(1)}, bf16[1024,512]{1,0:T(8,128)(2,1)}, u32[]{:S(2)}) copy-start(bf16[1024,512]{1,0:T(8,128)(2,1)} %copy-done.19) | copy-start | bytes 3145732
  447.8 6.8 %copy-start.25 = (f32[2,512,512]{2,1,0:T(8,128)S(1)}, f32[2,512,512]{2,1,0:T(8,128)}, u32[]{:S(2)}) copy-start(f32[2,512,512]{2,1,0:T(8,128)} %refs_0_.1) | copy-start | bytes 6291460
  454.6 1.9 copy-start.4
  456.5 1.6 copy-start.11
  458.1 1.9 copy-start.24
  460.0 1.4 copy-start.26
Sparse Core Ops, SparseCore 0:
  10.3 33.8 all-gather.2
  46.4 61.2 all-gather.4
  239.5 31.0 reduce-scatter.3
  273.4 36.3 reduce-scatter.5
  311.9 63.9 reduce-scatter.7
  380.1 65.2 all-reduce.3

commit v3 on v2

--- a/solution.py
+++ b/solution.py
@@ -744,6 +744,288 @@
     )
 
 
+def pair_place(batches):
+    me = lax.axis_index("batch")
+    place = lax.div(me, 2)
+    return place, me - 2 * place, batches // 2
+
+
+def greet_pairs(tasks, batches):
+    place, core, chips = pair_place(batches)
+    task = lax.axis_index("task")
+    barrier = pltpu.get_barrier_semaphore()
+
+    def signal(device):
+        pl.semaphore_signal(barrier, inc=1, device_id=device, device_id_type=MESH)
+
+    for step in range(1, tasks):
+        signal({"task": lax.rem(task + step, tasks)})
+    signal({"batch": 2 * place + 1 - core})
+    for step in range(1, chips):
+        signal({"batch": 2 * lax.rem(place + step, chips) + core})
+    pl.semaphore_wait(barrier, tasks - 1 + chips)
+
+
+def block_rows(ref, index, count):
+    return ref.at[pl.ds(pl.multiple_of(index * count, 8), count), :]
+
+
+def far_first(chips):
+    return sorted(range(chips), key=lambda step: -min(step, chips - step))
+
+
+def pair_sum(batches, source, near, paired, far, sems):
+    place, core, chips = pair_place(batches)
+    count = near.shape[1]
+    near_send, near_receive, far_send, far_receive = sems
+    other = 2 * place + 1 - core
+
+    def near_copy(step):
+        chip = lax.rem(place + step, chips)
+        return remote(block_rows(source, 2 * chip + 1 - core, count), near.at[step],
+                      near_send.at[step], near_receive.at[step], other, "batch")
+
+    def far_copy(step, incoming=False):
+        chip = lax.rem(place + (chips - step if incoming else step), chips)
+        return remote(paired.at[step], far.at[step], far_send.at[step], far_receive.at[step],
+                      2 * chip + core, "batch")
+
+    for step in far_first(chips):
+        near_copy(step).start()
+
+    def middle():
+        for step in far_first(chips):
+            chip = lax.rem(place + step, chips)
+            near_copy(step).wait_recv()
+            if step:
+                total = block_rows(source, 2 * chip + core, count)[...].astype(F32)
+                paired[step] = (total + near[step].astype(F32)).astype(paired.dtype)
+                far_copy(step).start()
+
+    def end():
+        total = block_rows(source, 2 * place + core, count)[...].astype(F32)
+        total = total + near[0].astype(F32)
+        for step in range(1, chips):
+            far_copy(step, True).wait_recv()
+            total = total + far[step].astype(F32)
+        for step in range(chips):
+            near_copy(step).wait_send()
+            if step:
+                far_copy(step).wait_send()
+        return total
+
+    return middle, end
+
+
+def pair_scratch(batches, rows, width, kind):
+    chips = batches // 2
+    return [pltpu.VMEM((chips, rows // batches, width), kind)] * 3 + [
+        pltpu.SemaphoreType.DMA((chips,))
+    ] * 4
+
+
+def collect_body(
+    tasks, batches,
+    slots, flow, sums,
+    input_grad, owned, part, norm_sums,
+    near, paired, far, near_send, near_receive, far_send, far_receive,
+    flow_in, flow_send, flow_receive, send, receive, sum_send, sum_receive,
+):
+    task = lax.axis_index("task")
+    width = part.shape[1]
+    pixels = input_grad.shape[0]
+
+    def peer_of(step, incoming):
+        return lax.rem(task + (tasks - step if incoming else step), tasks)
+
+    def flow_copy(step, incoming=False):
+        peer = peer_of(step, incoming)
+        return remote(block_rows(flow, peer, pixels), flow_in.at[step - 1], flow_send.at[step],
+                      flow_receive.at[step], peer, "task")
+
+    def sum_copy(step, incoming=False):
+        peer = peer_of(step, incoming)
+        home = peer if incoming else task
+        return remote(sums, norm_sums.at[:, columns_of(home, width)], sum_send.at[step],
+                      sum_receive.at[step], peer, "task")
+
+    def part_copy(step, incoming=False):
+        peer = peer_of(step, incoming)
+        home = peer if incoming else task
+        return remote(part, owned.at[:, columns_of(home, width)], send.at[step], receive.at[step],
+                      peer, "task")
+
+    greet_pairs(tasks, batches)
+    middle, end = pair_sum(
+        batches, slots, near, paired, far, (near_send, near_receive, far_send, far_receive)
+    )
+    for step in range(1, tasks):
+        sum_copy(step).start()
+        flow_copy(step).start()
+    norm_sums[:, columns_of(task, width)] = sums[...]
+    middle()
+    total = end().astype(BF)
+    part[...] = total
+    for step in range(1, tasks):
+        part_copy(step).start()
+    owned[:, columns_of(task, width)] = total
+    total = block_rows(flow, task, pixels)[...].astype(F32)
+    for step in range(1, tasks):
+        flow_copy(step, True).wait_recv()
+        total = total + flow_in[step - 1].astype(F32)
+    input_grad[...] = total
+    for step in range(1, tasks):
+        sum_copy(step, True).wait_recv()
+        part_copy(step, True).wait_recv()
+        sum_copy(step).wait_send()
+        part_copy(step).wait_send()
+        flow_copy(step).wait_send()
+
+
+def collect(tasks, batches, slots, flow, sums):
+    count, width = slots.shape
+    rows = count // batches
+    pixels, channels = flow.shape[0] // tasks, flow.shape[1]
+    return exchange_kernel(
+        functools.partial(collect_body, tasks, batches),
+        [
+            shape((pixels, channels), F32),
+            shape((rows, channels), BF),
+            shape((rows, width), BF),
+            shape((8, channels), F32),
+        ],
+        "vvv",
+        (slots, flow, sums),
+        pair_scratch(batches, count, width, BF)
+        + [pltpu.VMEM((tasks - 1, pixels, channels), BF)]
+        + [pltpu.SemaphoreType.DMA((tasks,))] * 6,
+        5,
+        24,
+        flops=20000 * MIB,
+    )
+
+
+def grams_body(
+    tasks, batches,
+    grad, part, owners, head_grad, head_owners,
+    grams, head_grams,
+    mine, head_mine,
+    near, paired, far, near_send, near_receive, far_send, far_receive,
+    head_near, head_paired, head_far, *rest,
+):
+    head_sems = rest[:4]
+    chip_send, chip_receive, task_send, task_receive, pair_send, pair_receive = rest[4:]
+    task = lax.axis_index("task")
+    place, core, chips = pair_place(batches)
+    width = part.shape[1]
+    channels = grad.shape[1]
+    count, head_count = near.shape[1], head_near.shape[1]
+    for m in range(head_owners.shape[1]):
+        held = (head_grad[...].astype(F32) * head_owners[:, m : m + 1]).astype(BF)
+        head_mine[m * channels : (m + 1) * channels, :] = dot_tn(held, head_grad[...]).astype(
+            head_mine.dtype
+        )
+    greet_pairs(tasks, batches)
+    head_middle, head_end = pair_sum(
+        batches, head_mine, head_near, head_paired, head_far, head_sems
+    )
+    for m in range(owners.shape[1]):
+        held = (grad[...].astype(F32) * owners[:, m : m + 1]).astype(BF)
+        mine[m * channels : (m + 1) * channels, :] = dot_tn(held, part[...]).astype(mine.dtype)
+    middle, end = pair_sum(
+        batches, mine, near, paired, far, (near_send, near_receive, far_send, far_receive)
+    )
+    head_middle()
+    middle()
+
+    def trunk_block(chip, home, which):
+        rows = pl.ds(pl.multiple_of((2 * chip + which) * count, 8), count)
+        return grams.at[rows, columns_of(home, width)]
+
+    def head_block(chip, which):
+        return block_rows(head_grams, 2 * chip + which, head_count)
+
+    def chip_copy(kind, step, incoming=False):
+        peer = lax.rem(place + (chips - step if incoming else step), chips)
+        home = peer if incoming else place
+        block = head_block(home, core) if kind else trunk_block(home, task, core)
+        return remote(block, block, chip_send.at[kind, step], chip_receive.at[kind, step],
+                      2 * peer + core, "batch")
+
+    def task_copy(step, hop, incoming=False):
+        peer = lax.rem(task + (tasks - step if incoming else step), tasks)
+        chip = lax.rem(place + chips - hop, chips)
+        block = trunk_block(chip, peer if incoming else task, core)
+        return remote(block, block, task_send.at[step, hop], task_receive.at[step, hop], peer, "task")
+
+    def pair_copy(kind, hop, incoming=False):
+        chip = lax.rem(place + chips - hop, chips)
+        which = 1 - core if incoming else core
+        home = lax.rem(task + tasks - kind, tasks)
+        block = head_block(chip, which) if kind == tasks else trunk_block(chip, home, which)
+        return remote(block, block, pair_send.at[kind, hop], pair_receive.at[kind, hop],
+                      2 * place + 1 - core, "batch")
+
+    total = end().astype(grams.dtype)
+    trunk_block(place, task, core)[...] = total
+    for step in range(1, chips):
+        chip_copy(0, step).start()
+    for step in range(1, tasks):
+        task_copy(step, 0).start()
+    pair_copy(0, 0).start()
+    total = head_end().astype(head_grams.dtype)
+    head_block(place, core)[...] = total
+    for step in range(1, chips):
+        chip_copy(1, step).start()
+    pair_copy(tasks, 0).start()
+    for hop in range(1, chips):
+        chip_copy(0, hop, True).wait_recv()
+        for step in range(1, tasks):
+            task_copy(step, hop).start()
+        pair_copy(0, hop).start()
+    for hop in range(chips):
+        for step in range(1, tasks):
+            task_copy(step, hop, True).wait_recv()
+            pair_copy(step, hop).start()
+    for hop in range(1, chips):
+        chip_copy(1, hop, True).wait_recv()
+        pair_copy(tasks, hop).start()
+    for hop in range(chips):
+        for kind in range(tasks + 1):
+            pair_copy(kind, hop, True).wait_recv()
+    for hop in range(chips):
+        for kind in range(tasks + 1):
+            pair_copy(kind, hop).wait_send()
+        for step in range(1, tasks):
+            task_copy(step, hop).wait_send()
+        if hop:
+            chip_copy(0, hop).wait_send()
+            chip_copy(1, hop).wait_send()
+
+
+def all_grams(tasks, batches, grad, part, owners, head_grad, head_owners):
+    channels, width = grad.shape[1], part.shape[1]
+    rows, head_rows = owners.shape[1] * channels, head_owners.shape[1] * channels
+    chips = batches // 2
+    kind = BF if rows % (16 * batches) == 0 else F32
+    head_kind = BF if head_rows % (16 * batches) == 0 else F32
+    return exchange_kernel(
+        functools.partial(grams_body, tasks, batches),
+        [shape((rows, channels), kind), shape((head_rows, channels), head_kind)],
+        "vvvvv",
+        (grad, part, owners, head_grad, head_owners),
+        [pltpu.VMEM((rows, width), kind), pltpu.VMEM((head_rows, channels), head_kind)]
+        + pair_scratch(batches, rows, width, kind)
+        + pair_scratch(batches, head_rows, channels, head_kind)
+        + [pltpu.SemaphoreType.DMA((2, chips))] * 2
+        + [pltpu.SemaphoreType.DMA((tasks, chips))] * 2
+        + [pltpu.SemaphoreType.DMA((tasks + 1, chips))] * 2,
+        6,
+        32,
+        flops=20000 * MIB,
+    )
+
+
 def exchange(body, outs, args, scratch, identity, vmem=32):
     size = sum(o.size * o.dtype.itemsize for o in outs) + sum(a.size * a.dtype.itemsize for a in args)
     return pl.pallas_call(
@@ -942,23 +1224,6 @@
         [pltpu.VMEM(basis.shape, BF)],
         flops=4 * weight.size * weight.shape[1] * basis.shape[0],
     )
-
-
-def grams_body(grad, part, owners, grams):
-    for m in range(grams.shape[0]):
-        held = (grad[...].astype(F32) * owners[:, m : m + 1]).astype(BF)
-        grams[m] = dot_tn(held, part[...])
-
-
-def owner_grams(grad, part, owners):
-    dims = (owners.shape[1], grad.shape[1], part.shape[1])
-    return run(
-        grams_body,
-        [shape(dims, F32)],
-        "vvv",
-        (grad, part, owners),
-        flops=2 * grad.size * part.shape[1] * owners.shape[1],
-    )[0]
 
 
 def factor_rows(values, identity, turn):
@@ -1120,38 +1385,34 @@
         geometry, tasks, batches, small, upstream, enc_pre, enc_totals, dec_pre, dec_totals,
         scales, choose, choose_row, x, spread, enc_taps, dec_taps,
     )
-    trunk_part = lax.psum_scatter(
-        to_slots(row_slot, enc_grad, dec_grad), "batch", scatter_dimension=0, tiled=True
-    )
-    input_grad = lax.psum_scatter(flow, "task", scatter_dimension=0, tiled=True)
-    input_grad = input_grad.astype(F32).reshape(images.shape)
+    input_grad, trunk_owned, trunk_part, norm_sums = collect(
+        tasks, batches, to_slots(row_slot, enc_grad, dec_grad), flow, trunk_sums
+    )
+    input_grad = input_grad.reshape(images.shape)
 
     head_local = head_weight.shape[1]
     head_ids = batch * head_local + jnp.arange(head_local, dtype=jnp.int32)
     head_owner = jnp.minimum(head_ids // channels, 2)
     head_onehot = (head_owner[:, None] == jnp.arange(3, dtype=jnp.int32)).astype(F32)
-    head_grams = lax.psum(owner_grams(head_owned, head_owned, head_onehot).astype(BF), "batch")
     head_weight_new, head_one_new, head_two_new = soap(
         head_owned, head_onehot, head_weight[0], head_mean_grad[0], head_mean_square[0],
         head_basis[0],
     )
 
-    trunk_owned, norm_sums = gather_over("task", tasks, (trunk_part, trunk_sums), (1, 1), 5)
     local_rows = trunk_weight.shape[0]
     slot_ids = batch * local_rows + jnp.arange(local_rows, dtype=jnp.int32)
     trunk_owner = jnp.take(jnp.argsort(row_slot), slot_ids) // tap_rows
     trunk_onehot = (trunk_owner[:, None] == jnp.arange(2, dtype=jnp.int32)).astype(F32)
-    trunk_grams = lax.psum(owner_grams(trunk_owned, trunk_part, trunk_onehot), "batch").astype(BF)
-    trunk_grams = gather_over(
-        "task", tasks, (trunk_grams.reshape(2 * channels, width),), (1,), 6
-    )[0].reshape(2, channels, channels)
+    trunk_grams, head_grams = all_grams(
+        tasks, batches, trunk_owned, trunk_part, trunk_onehot, head_owned, head_onehot
+    )
     trunk_weight_new, trunk_one_new, trunk_two_new = soap(
         trunk_owned, trunk_onehot, trunk_weight, trunk_mean_grad, trunk_mean_square, trunk_basis
     )
     trunk_stat_new, head_stat_new, trunk_basis_new, head_basis_new = renew_bases(
         (trunk_statistic, head_statistic[0]),
         (trunk_basis, head_basis[0]),
-        (trunk_grams, head_grams),
+        (trunk_grams.reshape(trunk_basis.shape), head_grams.reshape(head_basis.shape[1:])),
     )
 
     trunk_norm = jnp.stack([trunk_gain, trunk_offset], axis=1)

time: 552 us -> 482 us (0.87)
  the two profiles are of different devices: /device:TPU:0 before, /device:TPU:25 now
where the time goes in v3:
time: 482 us; the launch traced here: 473 us
  Pallas kernels  389 us (81%)
  local copies, waits for them, and re-layouts  49.3 us (10%)
  between operations  15.9 us (3%)
  other arithmetic  13.2 us (3%)
  blocking collectives  5.35 us (1%)
    pallas_call x5, Pallas kernels, exchange_kernel(): pl.pallas_call(body, out_shape=tuple(outs), in_specs=[SMEM_SPEC if s == '...  259 us
    pallas_call x5, Pallas kernels, run(): pl.pallas_call(body, out_shape=tuple(outs), in_specs=[SMEM_SPEC if s == '...  107 us
    unnamed x114, local copies, waits for them, and re-layouts  34.8 us
    pallas_call x1, Pallas kernels, exchange(): pl.pallas_call(body, out_shape=tuple(outs), in_specs=[VMEM_SPEC] * len(ar...  22.6 us
  transfers between devices with their start and end apart: 3, of which 0 were waited for; matrix products, arithmetic and copies ran while one was open for 6% of the time, Pallas kernels for 35%

profile of v3, /device:TPU:25, one launch (start us, length us, event | category | flops | bytes accessed | tf_op | source)
XLA Modules:
  0.0 472.6 jit_solution(11678685439445346096)
XLA Ops:
  7.3 1.9 dynamic-slice_convert_fusion
  9.2 2.3 convert_element_type.42
  12.4 0.6 dynamic-slice
  13.6 0.2 add_dynamic-update-slice_fusion
  13.8 5.4 %all-reduce = s32[436]{0:T(512)S(1)} all-reduce(s32[436]{0:T(512)S(1)} %add_dynamic-update-slice_fusion), channel_id=1, replica_groups=mesh['task'=4,'batch'=8] {'task'}, use_global_device_ids=true, to_apply=%add | all-reduce | flops 436 | bytes 3488
  19.3 0.1 broadcast_multiply_fusion
  19.5 22.6 %shard_map.358.x = bf16[1728,512]{1,0:T(8,128)(2,1)S(1)} custom-call(bf16[432,512]{1,0:T(8,128)(2,1)S(1)} %bitcast.32), custom_call_target="tpu_custom_call" | custom-call | bytes 2211840 | tf_op jit(solution)/shard_map/pallas_call | solution.py:1031
  42.3 0.1 eq.75.clone
  42.5 0.2 eq.76
  43.0 0.4 copy.79
  43.5 0.1 slice_reduce_fusion.small
  43.8 0.4 and.119
  44.2 1.9 copy.81.cotangent
  46.1 0.6 reshape.401.scales
  46.7 0.1 and_convert_fusion.choose
  46.9 1.9 copy-done.4
  48.8 10.3 %shard_map.359 = (bf16[512,1152]{1,0:T(8,128)(2,1)S(1)}, bf16[512,1152]{1,0:T(8,128)(2,1)S(1)}) custom-call(s32[9216]{0:T(1024)S(1)} %copy-done.20, bf16[9216,128]{1,0:T(8,128)(2,1)S(1)} %copy-done.4), custom_call_target="tpu_custom_call" | custom-call | bytes 4755456 | tf_op jit(solution)/shard_map/pallas_call | solution.py:32
  59.2 48.2 %shard_map.360 = (f32[1728,128]{1,0:T(8,128)S(1)}, f32[8,128]{1,0:T(8,128)S(1)}, bf16[1728,512]{1,0:T(8,128)(2,1)S(1)}, f32[1728,128]{1,0:T(8,128)S(1)}, f32[8,1...) custom-call(s32[4]{0:T(128)S(1)} %slice_reduce_fusion.small, bf16[1728,512]{1,0:T(8,128)(2,1)S(1)} %shard_map.358.x, ...), custom_call_target="tpu_custom_call" | custom-call | flops 4076863488 | bytes 9454352 | tf_op jit(solution)/shard_map/pallas_call | solution.py:222
  107.4 1.0 copy-done.25
  108.4 1.0 copy-done.27
  109.4 1.2 copy-done.29
  110.6 1.2 copy-done.31
  111.8 0.9 copy-done.32
  112.8 0.9 copy-done.34
  113.7 0.6 copy-done.39
  114.3 85.5 %shard_map.361 = (bf16[4,108,512]{2,1,0:T(8,128)(2,1)}, bf16[5632,512]{1,0:T(8,128)(2,1)}, f32[1728,128]{1,0:T(8,128)}, f32[8,512]{1,0:T(8,128)}) custom-call(s32[4]{0:T(128)} %copy-done.21, bf16[1728,512]{1,0:T(8,128)(2,1)} %copy-done.31, bf16[5632,512]{1,0:T(8,128)(2,1)} %bitcast.53, bf16[4,108,512]{2,1,0:T(8,128)(2,1)} %copy.81.cotangent, ...), custom_call_target="tpu_custom_call" | custom-call | flops 29896998912 | bytes 15106064 | tf_op jit(solution)/shard_map/pallas_call | solution.py:222
  199.9 0.1 copy.77
  200.0 0.1 eq.83
  200.3 8.8 %sort.17 = (s32[9216]{0:T(1024)}, s32[9216]{0:T(1024)S(1)}) sort(s32[9216]{0:T(1024)S(1)} %copy-done.20, s32[9216]{0:T(1024)S(1)} %iota.68), dimensions={0}, to_apply=%region_0.1 | sort | flops 129024 | bytes 147456 | tf_op jit(solution)/shard_map/jit(argsort)/sort | solution.py:1404
  209.2 6.5 %gather_fusion = s32[1152]{0:T(1024)S(1)} fusion(s32[9216]{0:T(1024)S(1)} %get-tuple-element.67, s32[2048]{0:T(1024)S(1)} %pad_clamp_fusion), kind=kCustom, calls=%fused_computation | custom fusion | bytes 13824 | tf_op jit(solution)/shard_map/jit(_take)/gather | solution.py:1404
  215.8 0.2 fusion.1.head_owners.owners
  215.9 0.2 fusion.owners
  216.2 1.1 copy.82
  217.3 1.2 copy-done.17
  218.4 1.3 copy-done.26
  219.7 1.3 copy-done.28
  221.0 1.5 copy-done.30
  222.5 1.2 copy-done.33
  223.7 1.2 copy-done.35
  224.9 1.2 copy-done.36
  226.0 28.1 %shard_map.362 = (f32[512,1152]{1,0:T(8,128)S(1)}, f32[512,1152]{1,0:T(8,128)}, bf16[1728,512]{1,0:T(8,128)(2,1)S(1)}, f32[8,128]{1,0:T(8,128)S(1)}) custom-call(s32[4]{0:T(128)S(1)} %copy-done.22, f32[1728,128]{1,0:T(8,128)S(1)} %copy-done.36, f32[1728,128]{1,0:T(8,128)S(1)} %copy-done.33, f32[8,128]{1,0:T(8,128)S(1)} %copy-done.40, ...), custom_call_target="tpu_custom_call" | custom-call | flops 8153726976 | bytes 15068688 | tf_op jit(solution)/shard_map/pallas_call | solution.py:222
  254.2 1.7 copy-done.3
  255.8 9.9 %shard_map.363.slots = bf16[9216,128]{1,0:T(8,128)(2,1)S(1)} custom-call(s32[9216]{0:T(1024)S(1)} %copy-done.20, f32[512,1152]{1,0:T(8,128)S(1)} %get-tuple-element.61.enc, f32[512,1152]{1,0:T(8,128)S(1)} %copy-done.3), custom_call_target="tpu_custom_call" | custom-call | bytes 7114752 | tf_op jit(solution)/shard_map/pallas_call | solution.py:32
  265.8 40.5 %shard_map.364 = (f32[432,512]{1,0:T(8,128)S(1)}, bf16[1152,512]{1,0:T(8,128)(2,1)S(1)}, bf16[1152,128]{1,0:T(8,128)(2,1)S(1)}, f32[8,512]{1,0:T(8,128)S(1)}) custom-call(bf16[9216,128]{1,0:T(8,128)(2,1)S(1)} %shard_map.363.slots, bf16[1728,512]{1,0:T(8,128)(2,1)S(1)} %get-tuple-element.63.flow, f32[8,128]{1,0:T(8,128)S(1)} %get-tuple-element.64.sums), custom_call_target="tpu_custom_call" | custom-call | flops 20971520000 | bytes 6508544 | tf_op jit(solution)/shard_map/pallas_call | solution.py:222
  306.3 1.0 copy-done.11
  307.3 0.9 copy-done.14
  308.2 0.7 copy-done.37
  309.0 0.6 copy.89
  309.6 0.6 copy.90
  310.2 0.6 copy.91
  310.9 0.2 rev.7
  311.0 0.7 maximum_subtract_fusion
  311.7 1.7 copy-done.5
  313.4 1.7 copy-done.6
  315.0 1.6 copy-done.7
  316.6 1.3 copy-done.12
  317.9 8.0 %shard_map.365 = (f32[1152,512]{1,0:T(8,128)}, f32[1152,512]{1,0:T(8,128)}, f32[1152,512]{1,0:T(8,128)}) custom-call(bf16[1152,512]{1,0:T(8,128)(2,1)S(1)} %copy-done.12, f32[1152,2]{1,0:T(8,128)S(1)} %fusion.owners, f32[1152,512]{1,0:T(8,128)S(1)} %copy-done.2, f32[1152,512]{1,0:T(8,128)S(1)} %copy-done.5, f32[1152,512]{1,0:T(8,128)S(1)} %copy-done.6, ...), custom_call_target="tpu_custom_call" | custom-call | flops 2415919104 | bytes 17441792 | tf_op jit(solution)/shard_map/pallas_call | solution.py:32
  325.9 1.3 copy-done.13
  327.2 1.1 copy-done.18
  328.3 1.0 copy-done.38
  329.2 56.4 %shard_map.366 = (bf16[1024,512]{1,0:T(8,128)(2,1)S(1)}, bf16[1536,512]{1,0:T(8,128)(2,1)S(1)}) custom-call(bf16[1152,512]{1,0:T(8,128)(2,1)S(1)} %copy-done.13, bf16[1152,128]{1,0:T(8,128)(2,1)S(1)} %copy-done.38, f32[1152,2]{1,0:T(8,128)S(1)} %fusion.owners, bf16[704,512]{1,0:T(8,128)(2,1)S(1)} %copy-done.18, f32[704,3]{1,0:T(8,128)S(1)} %fusion.1.head_owners.owners), custom_call_target="tpu_custom_call" | custom-call | flops 20971520000 | bytes 4834560 | tf_op jit(solution)/shard_map/pallas_call | solution.py:222
  385.7 72.4 %shard_map.367 = (f32[2,512,512]{2,1,0:T(8,128)}, f32[3,512,512]{2,1,0:T(8,128)}, f32[2,512,512]{2,1,0:T(8,128)}, f32[3,512,512]{2,1,0:T(8,128)}) custom-call(f32[2,512,512]{2,1,0:T(8,128)S(1)} %copy-done.24, f32[3,512,512]{2,1,0:T(8,128)S(1)} %bitcast.38, f32[2,512,512]{2,1,0:T(8,128)S(1)} %copy-done.8, f32[3,512,512]{2,1,0:T(8,128)S(1)} %bitcast.30, ...), custom_call_target="tpu_custom_call" | custom-call | flops 64424509440 | bytes 23592960 | tf_op jit(solution)/shard_map/pallas_call | solution.py:32
  458.2 6.8 %shard_map.368 = (f32[704,512]{1,0:T(8,128)}, f32[704,512]{1,0:T(8,128)}, f32[704,512]{1,0:T(8,128)}) custom-call(bf16[704,512]{1,0:T(8,128)(2,1)S(1)} %copy-done.19, f32[704,3]{1,0:T(8,128)S(1)} %fusion.1.head_owners.owners, f32[704,512]{1,0:T(8,128)S(1)} %bitcast.29, f32[704,512]{1,0:T(8,128)S(1)} %bitcast.33, f32[704,512]{1,0:T(8,128)S(1)} %bitcast.34, ...), custom_call_target="tpu_custom_call" | custom-call | flops 2214592512 | bytes 12525824 | tf_op jit(solution)/shard_map/pallas_call | solution.py:32
  464.9 0.9 copy.104
  (128 shorter events, 1.8 us)
Async XLA Ops:
  7.2 5.2 %copy-start.53 = (u32[32]{0:T(128)S(1)}, u32[32]{0:T(128)}, u32[]{:S(2)}) copy-start(u32[32]{0:T(128)} %constant.110) | copy-start | bytes 388
  7.2 4.4 copy-start.52
  7.2 12.1 %copy-start.42 = (bf16[1,18,24,512]{3,2,1,0:T(8,128)(2,1)S(1)}, bf16[1,18,24,512]{3,2,1,0:T(8,128)(2,1)}, u32[]{:S(2)}) copy-start(bf16[1,18,24,512]{3,2,1,0:T(8,128)(2,1)} %param.23) | copy-start | bytes 1327108
  7.2 39.6 %all-gather.3.cloned.1.call-start = ((), (), s32[]{:S(2)}) async-start(), calls=%async_computation.1 | async-start | bytes 2654208 | tf_op jit(solution)/shard_map/all_gather | solution.py:1358
  9.2 105.1 %all-gather.5.cloned.1.call-start = ((), (), s32[]{:S(2)}) async-start(), calls=%async_computation.2 | async-start | bytes 6488064 | tf_op jit(solution)/shard_map/all_gather | solution.py:1359
  11.5 30.6 %copy-start.45 = (f32[2,512]{1,0:T(2,128)S(1)}, f32[2,512]{1,0:T(2,128)}, u32[]{:S(2)}) copy-start(f32[2,512]{1,0:T(2,128)} %param.37) | copy-start | bytes 12292
  11.5 30.6 %copy-start.46 = (f32[2,512]{1,0:T(2,128)S(1)}, f32[2,512]{1,0:T(2,128)}, u32[]{:S(2)}) copy-start(f32[2,512]{1,0:T(2,128)} %param.38) | copy-start | bytes 12292
  11.5 314.3 %reduce-scatter.2.cloned.1.call-start = ((), (), s32[]{:S(2)}) async-start(), calls=%async_computation.3 | async-start | bytes 6488064 | tf_op jit(solution)/shard_map/reduce_scatter | solution.py:1383
  42.1 4.0 copy-start.43
  42.1 4.0 copy-start.44
  42.3 4.5 copy-start.20
  43.6 15.6 %copy-start.21 = (s32[4]{0:T(128)}, s32[4]{0:T(128)S(1)}, u32[]{:S(2)}) copy-start(s32[4]{0:T(128)S(1)} %slice_reduce_fusion.small) | copy-start | bytes 52
  46.8 60.6 %copy-start.16 = (f32[1728,1]{1,0:T(8,128)}, f32[1728,1]{1,0:T(8,128)S(1)}, u32[]{:S(2)}) copy-start(f32[1728,1]{1,0:T(8,128)S(1)} %and_convert_fusion.choose) | copy-start | bytes 20740
  46.9 2.0 copy-start.4
  107.4 1.0 copy-start.25
  108.4 1.0 copy-start.27
  109.4 1.2 copy-start.29
  110.6 1.2 copy-start.31
  111.8 0.9 copy-start.32
  112.8 0.9 copy-start.34
  113.7 0.6 copy-start.39
  209.2 7.0 %copy-start.41 = (bf16[4,108,512]{2,1,0:T(8,128)(2,1)S(1)}, bf16[4,108,512]{2,1,0:T(8,128)(2,1)}, u32[]{:S(2)}) copy-start(bf16[4,108,512]{2,1,0:T(8,128)(2,1)} %get-tuple-element.55) | copy-start | bytes 1327108
  209.2 8.1 %copy-start.22 = (s32[4]{0:T(128)S(1)}, s32[4]{0:T(128)}, u32[]{:S(2)}) copy-start(s32[4]{0:T(128)} %copy-done.21) | copy-start | bytes 52
  209.2 8.1 %copy-start.40 = (f32[8,128]{1,0:T(8,128)S(1)}, f32[8,128]{1,0:T(8,128)}, u32[]{:S(2)}) copy-start(f32[8,128]{1,0:T(8,128)} %copy-done.39) | copy-start | bytes 12292
  217.3 1.2 copy-start.17
  218.4 1.3 copy-start.26
  219.7 1.3 copy-start.28
  221.0 1.5 copy-start.30
  222.5 1.2 copy-start.33
  223.7 1.2 copy-start.35
  224.9 1.2 copy-start.36
  254.2 1.7 copy-start.3
  265.8 43.2 %copy-start.50 = (f32[2,2,512]{2,1,0:T(2,128)S(1)}, f32[2,2,512]{2,1,0:T(2,128)}, u32[]{:S(2)}) copy-start(f32[2,2,512]{2,1,0:T(2,128)} %param.39) | copy-start | bytes 24580
  265.8 43.2 %copy-start.51 = (f32[2,2,512]{2,1,0:T(2,128)S(1)}, f32[2,2,512]{2,1,0:T(2,128)}, u32[]{:S(2)}) copy-start(f32[2,2,512]{2,1,0:T(2,128)} %param.40) | copy-start | bytes 24580
  265.8 45.1 %copy-start.47 = (f32[8,512]{1,0:T(8,128)S(1)}, f32[8,512]{1,0:T(8,128)}, u32[]{:S(2)}) copy-start(f32[8,512]{1,0:T(8,128)} %get-tuple-element.83) | copy-start | bytes 49156
  265.8 45.2 %copy-start.48 = (f32[1,3,2,512]{3,2,1,0:T(2,128)S(1)}, f32[1,3,2,512]{3,2,1,0:T(2,128)}, u32[]{:S(2)}) copy-start(f32[1,3,2,512]{3,2,1,0:T(2,128)} %param.43) | copy-start | bytes 36868
  265.8 45.2 %copy-start.49 = (f32[1,3,2,512]{3,2,1,0:T(2,128)S(1)}, f32[1,3,2,512]{3,2,1,0:T(2,128)}, u32[]{:S(2)}) copy-start(f32[1,3,2,512]{3,2,1,0:T(2,128)} %param.44) | copy-start | bytes 36868
  265.8 45.9 %copy-start.2 = (f32[1152,512]{1,0:T(8,128)S(1)}, f32[1152,512]{1,0:T(8,128)}, u32[]{:S(2)}) copy-start(f32[1152,512]{1,0:T(8,128)} %weight.1) | copy-start | bytes 7077892
  306.3 1.0 copy-start.11
  307.3 0.9 copy-start.14
  308.2 0.7 copy-start.37
  311.7 1.7 copy-start.5
  313.4 1.7 copy-start.6
  315.0 1.6 copy-start.7
  316.6 1.3 copy-start.12
  325.9 1.3 copy-start.13
  327.2 1.1 copy-start.18
  328.3 1.0 copy-start.38
  329.2 56.4 %copy-start.1 = (f32[1,3,512,512]{3,2,1,0:T(8,128)S(1)}, f32[1,3,512,512]{3,2,1,0:T(8,128)}, u32[]{:S(2)}) copy-start(f32[1,3,512,512]{3,2,1,0:T(8,128)} %param.36) | copy-start | bytes 9437188
  329.2 56.4 %copy-start.8 = (f32[2,512,512]{2,1,0:T(8,128)S(1)}, f32[2,512,512]{2,1,0:T(8,128)}, u32[]{:S(2)}) copy-start(f32[2,512,512]{2,1,0:T(8,128)} %refs_2_.1) | copy-start | bytes 6291460
  329.2 56.4 %copy-start.23 = (f32[1,3,512,512]{3,2,1,0:T(8,128)S(1)}, f32[1,3,512,512]{3,2,1,0:T(8,128)}, u32[]{:S(2)}) copy-start(f32[1,3,512,512]{3,2,1,0:T(8,128)} %param.35) | copy-start | bytes 9437188
  329.2 56.4 %copy-start.24 = (f32[2,512,512]{2,1,0:T(8,128)S(1)}, f32[2,512,512]{2,1,0:T(8,128)}, u32[]{:S(2)}) copy-start(f32[2,512,512]{2,1,0:T(8,128)} %refs_0_.1) | copy-start | bytes 6291460
  385.7 72.5 %copy-start = (f32[1,704,512]{2,1,0:T(8,128)S(1)}, f32[1,704,512]{2,1,0:T(8,128)}, u32[]{:S(2)}) copy-start(f32[1,704,512]{2,1,0:T(8,128)} %param.32) | copy-start | bytes 4325380
  385.7 72.5 %copy-start.9 = (f32[1,704,512]{2,1,0:T(8,128)S(1)}, f32[1,704,512]{2,1,0:T(8,128)}, u32[]{:S(2)}) copy-start(f32[1,704,512]{2,1,0:T(8,128)} %param.33) | copy-start | bytes 4325380
  385.7 72.4 %copy-start.10 = (f32[1,704,512]{2,1,0:T(8,128)S(1)}, f32[1,704,512]{2,1,0:T(8,128)}, u32[]{:S(2)}) copy-start(f32[1,704,512]{2,1,0:T(8,128)} %param.34) | copy-start | bytes 4325380
  385.7 72.4 %copy-start.19 = (bf16[704,512]{1,0:T(8,128)(2,1)S(1)}, bf16[704,512]{1,0:T(8,128)(2,1)}, u32[]{:S(2)}) copy-start(bf16[704,512]{1,0:T(8,128)(2,1)} %reduce-scatter.2.cloned.1.call-done.head_grad.grad) | copy-start | bytes 2162692
  458.1 6.8 %copy-start.15 = (f32[432,512]{1,0:T(8,128)S(1)}, f32[432,512]{1,0:T(8,128)}, u32[]{:S(2)}) copy-start(f32[432,512]{1,0:T(8,128)} %copy-done.14) | copy-start | bytes 2654212
Sparse Core Ops, SparseCore 0:
  10.3 31.2 all-gather.2
  43.8 60.0 all-gather.4
  199.9 63.0 reduce-scatter.1
